TPU v7x, 32 devices: a whole 2x2x4 slice. The times are simulated.
32 devices in a mesh: dp: 4 (over y, core), expert: 8 (over z, x).
Axes of the slice: x: 2, y: 2, z: 4, core: 2. Of those that a mesh axis runs over, the one named last changes fastest.
Arguments:
- grad_out: bfloat16 [4096, 2048], P(('dp', 'expert')), may hold values from -6 to 6
- route_prob: bfloat16 [4096, 1], P(('dp', 'expert')), may hold values from 0.099609375 to 1
- expert_ids: int32 [4096, 1], P(('dp', 'expert')), may hold values from 0 to 7; in each aligned block of 128 rows (0 to 127, 128 to 255, ...) at most 24 rows name the same one
- saved_act: bfloat16 [4, 8, 192, 768], P('dp', 'expert'), may hold values from -0.21875 to 0.21875
- down_weight: bfloat16 [8, 768, 2048], P('expert'), may hold values from -0.21875 to 0.21875
Outputs:
- grad_act: bfloat16 [4, 8, 192, 768], P('dp', 'expert')
- grad_weight: float32 [8, 2048, 768], P('expert', 'dp')
- grad_prob: float32 [4096, 1], P(('dp', 'expert'))
Inputs may be any that keep to these rules, and one draw needn't show every extreme that they name: `expert_ids`: among the 128 tokens of one device no expert is named more than 24 times, a bound that some block reaches on every device.
All inputs are finite; a program needn't handle non-finite values.
Results may differ from a plain program's by a relative error of at most 0.0029.
Values may be sent and summed in bfloat16 or wider, within the bound.
No kernel may reach another device: no remote copies, remote signals or barrier semaphores. Data moves between devices by JAX's collectives and lax.ppermute only.
A program may use at most 64 MiB of HBM per device.

v0:
```python
import jax
import jax.numpy as jnp
from jax import lax
from jax.sharding import PartitionSpec as P


def shards(grad_out, route_prob, expert_ids, saved_act, down_weight):
    expert_count = lax.axis_size("expert")
    slots = saved_act.shape[2]
    capacity = slots // expert_count
    width = grad_out.shape[1]
    routed = expert_ids[:, 0]
    member = (routed[:, None] == jnp.arange(expert_count, dtype=jnp.int32)[None, :]).astype(
        jnp.int32
    )
    before = jnp.cumsum(member, axis=0) - member
    placed = routed * capacity + jnp.sum(before * member, axis=1)
    send_rows = jnp.zeros((slots, width), jnp.bfloat16).at[placed].set(grad_out)
    send_prob = jnp.zeros((slots, 1), jnp.bfloat16).at[placed].set(route_prob)
    arrived, arrived_prob = (
        lax.all_to_all(send_rows, "expert", split_axis=0, concat_axis=0, tiled=True),
        lax.all_to_all(send_prob, "expert", split_axis=0, concat_axis=0, tiled=True),
    )
    stored = saved_act[0, 0]
    weight = down_weight[0]
    factor = arrived_prob.astype(jnp.float32)
    backed = lax.dot_general(
        arrived, weight, (((1,), (1,)), ((), ())), preferred_element_type=jnp.float32
    )
    grad_act = (factor * backed).astype(jnp.bfloat16)[None, None]
    slot_grad = jnp.sum(backed * stored.astype(jnp.float32), axis=1, keepdims=True)
    weighted = (factor * arrived.astype(jnp.float32)).astype(jnp.bfloat16)
    returned = lax.all_to_all(slot_grad, "expert", split_axis=0, concat_axis=0, tiled=True)
    grad_prob = returned[placed]
    grad_weight = lax.psum_scatter(
        lax.dot_general(
            weighted, stored, (((0,), (0,)), ((), ())), preferred_element_type=jnp.float32
        ),
        "dp",
        scatter_dimension=0,
        tiled=True,
    )
    return (grad_act, grad_weight[None], grad_prob)


def solution(mesh):
    return jax.shard_map(
        shards,
        mesh=mesh,
        in_specs=(
            P(("dp", "expert"), None),
            P(("dp", "expert"), None),
            P(("dp", "expert"), None),
            P("dp", "expert", None, None),
            P("expert", None, None),
        ),
        out_specs=(
            P("dp", "expert", None, None),
            P("expert", "dp", None),
            P(("dp", "expert"), None),
        ),
        check_vma=False,
    )
```

profile of v0, /device:TPU:0, one launch (start us, length us, event | category | flops | bytes accessed | tf_op | source)
XLA Modules:
  0.0 119.8 jit_solution(16575679590564046106)
XLA Ops:
  7.2 0.0 copy-start
  7.2 0.0 copy-start.1
  7.2 1.5 %fusion.7 = s32[128,8]{1,0:T(8,128)} fusion(s32[128]{0:T(128)} %bitcast.36), kind=kLoop, calls=%fused_computation.15 | loop fusion | flops 2048 | bytes 4608 | tf_op jit(solution)/shard_map/convert_element_type | solution.py:13
  8.7 1.0 reduce_window_sum.11
  9.7 0.8 select_reduce_fusion
  10.6 0.7 fusion.8
  11.2 1.5 %scatter_custom_fusion = bf16[192]{0:T(256)(128)(2,1)S(1)} fusion(s32[128]{0:T(128)S(1)} %fusion.8, bf16[128]{0:T(256)(128)(2,1)} %bitcast.40, bf16[]{:T(256)} %constant.5.clone.1), kind=kCustom, calls=%fused_computation.21 | custom fusion | bytes 896 | tf_op jit(solution)/shard_map/scatter | solution.py:19
  12.7 0.7 all_to_all.30
  13.4 7.3 %all-to-all-start = ((bf16[8,24,1]{1,2,0:T(2,128)(2,1)}), bf16[8,24,1]{1,2,0:T(2,128)(2,1)S(1)}, u32[]{:S(2)}, u32[]{:S(2)}) async-start(bf16[8,24,1]{1,2,0:T(2,128)(2,1)} %all_to_all.30), calls=%async_computation | async-start | bytes 8192 | tf_op jit(solution)/shard_map/all_to_all | solution.py:22
  20.6 2.8 %scatter_custom_fusion.1 = bf16[192,2048]{1,0:T(8,128)(2,1)} fusion(s32[128]{0:T(128)S(1)} %fusion.8, bf16[128,2048]{1,0:T(8,128)(2,1)} %param.5, bf16[]{:T(256)} %constant.5.clone.1), kind=kCustom, calls=%fused_computation.8 | custom fusion | bytes 786944 | tf_op jit(solution)/shard_map/scatter | solution.py:18
  23.4 3.6 %all-to-all-done = bf16[8,24,1]{1,2,0:T(2,128)(2,1)S(1)} async-done(((bf16[8,24,1]{1,2,0:T(2,128)(2,1)}), bf16[8,24,1]{1,2,0:T(2,128)(2,1)S(1)}, u32[]{:S(2)}, u32[]{:S(2)}) %all-to-all-start) | async-done | bytes 416 | tf_op jit(solution)/shard_map/all_to_all | solution.py:22
  27.0 4.2 %all-to-all-start.1 = ((bf16[8,24,2048]{2,1,0:T(8,128)(2,1)}), bf16[8,24,2048]{2,1,0:T(8,128)(2,1)}, u32[]{:S(2)}, u32[]{:S(2)}) async-start(bf16[8,24,2048]{2,1,0:T(8,128)(2,1)} %bitcast.35), calls=%async_computation.1 | async-start | bytes 1572864 | tf_op jit(solution)/shard_map/all_to_all | solution.py:21
  31.2 0.0 reduce-scatter.2.cloned.1.call-start
  31.3 19.0 %all-to-all-done.1 = bf16[8,24,2048]{2,1,0:T(8,128)(2,1)} async-done(((bf16[8,24,2048]{2,1,0:T(8,128)(2,1)}), bf16[8,24,2048]{2,1,0:T(8,128)(2,1)}, u32[]{:S(2)}, u32[]{:S(2)}) %all-to-all-start.1) | async-done | bytes 786464 | tf_op jit(solution)/shard_map/all_to_all | solution.py:21
  50.3 1.3 %multiply_convert_fusion = bf16[8,24,2048]{2,1,0:T(8,128)(2,1)S(1)} fusion(bf16[8,24,2048]{2,1,0:T(8,128)(2,1)} %all-to-all-done.1, f32[8,24]{1,0:T(8,128)S(1)} %get-tuple-element.5), kind=kLoop, calls=%fused_computation.5 | loop fusion | flops 1179648 | bytes 1573632 | tf_op jit(solution)/shard_map/convert_element_type | solution.py:32
  51.7 0.0 copy-done.1
  51.7 3.7 %fusion.5 = f32[2048,768]{1,0:T(8,128)} fusion(bf16[192,2048]{1,0:T(8,128)(2,1)S(1)} %bitcast.34, bf16[1,1,192,768]{3,2,1,0:T(8,128)(2,1)S(1)} %copy-done.1), kind=kOutput, calls=%fused_computation.11 | convolution fusion | flops 603979776 | bytes 7372800 | tf_op jit(solution)/shard_map/dot_general | solution.py:36
  55.4 0.0 reduce-scatter.2.cloned.1.call-update
  55.4 0.1 reshape.32
  55.5 0.0 copy-done
  55.5 3.2 %multiply_reduce_fusion = (f32[192]{0:T(256)S(1)}, bf16[1,1,192,768]{3,2,1,0:T(8,128)(2,1)}) fusion(bf16[1,1,192,768]{3,2,1,0:T(8,128)(2,1)S(1)} %copy-done.1, f32[192]{0:T(256)S(1)} %reshape.32, bf16[192,2048]{1,0:T(8,128)(2,1)} %bitcast.5, bf16[1,768,2048]{2,1,0:T(8,128)(2,1)S(1)} %copy-done), kind=kOutput, calls=%fused_computation.6 | convolution fusion | flops 604716864 | bytes 4523520 | tf_op jit(solution)/shard_map/dot_general | solution.py:27
  58.7 0.7 all_to_all.27
  59.3 3.5 %all-to-all-start.2 = ((f32[8,24,1]{1,2,0:T(1,128)}), f32[8,24,1]{1,2,0:T(1,128)S(1)}, u32[]{:S(2)}, u32[]{:S(2)}) async-start(f32[8,24,1]{1,2,0:T(1,128)} %bitcast.12), calls=%async_computation.3 | async-start | bytes 8192 | tf_op jit(solution)/shard_map/all_to_all | solution.py:33
  62.9 6.5 %all-to-all-done.2 = f32[8,24,1]{1,2,0:T(1,128)S(1)} async-done(((f32[8,24,1]{1,2,0:T(1,128)}), f32[8,24,1]{1,2,0:T(1,128)S(1)}, u32[]{:S(2)}, u32[]{:S(2)}) %all-to-all-start.2) | async-done | bytes 800 | tf_op jit(solution)/shard_map/all_to_all | solution.py:33
  69.3 0.5 broadcast.31
  69.8 0.7 reduce.3
  70.5 0.1 reshape.34
  70.6 1.8 %gather_fusion = f32[128]{0:T(128)} fusion(f32[192]{0:T(256)S(1)} %reshape.34, s32[1024]{0:T(1024)S(1)} %pad_clamp_fusion), kind=kCustom, calls=%fused_computation | custom fusion | bytes 1536 | tf_op jit(solution)/shard_map/gather | solution.py:34
  72.3 40.6 %reduce-scatter.2.cloned.1.call-done = f32[512,768]{1,0:T(8,128)} async-done(((f32[2048,768]{1,0:T(8,128)}), f32[512,768]{1,0:T(8,128)}) %reduce-scatter.2.cloned.1.call-update) | async-done | bytes 1572880 | tf_op jit(solution)/shard_map/reduce_scatter | solution.py:35
  (2 shorter events, 0.0 us)
Async XLA Ops:
  7.2 48.3 %copy-start = (bf16[1,768,2048]{2,1,0:T(8,128)(2,1)S(1)}, bf16[1,768,2048]{2,1,0:T(8,128)(2,1)}, u32[]{:S(2)}) copy-start(bf16[1,768,2048]{2,1,0:T(8,128)(2,1)} %param.9) | copy-start | bytes 9437188
  7.2 44.5 %copy-start.1 = (bf16[1,1,192,768]{3,2,1,0:T(8,128)(2,1)S(1)}, bf16[1,1,192,768]{3,2,1,0:T(8,128)(2,1)}, u32[]{:S(2)}) copy-start(bf16[1,1,192,768]{3,2,1,0:T(8,128)(2,1)} %param.8) | copy-start | bytes 884740
  13.4 13.6 %all-to-all-start = ((bf16[8,24,1]{1,2,0:T(2,128)(2,1)}), bf16[8,24,1]{1,2,0:T(2,128)(2,1)S(1)}, u32[]{:S(2)}, u32[]{:S(2)}) async-start(bf16[8,24,1]{1,2,0:T(2,128)(2,1)} %all_to_all.30), calls=%async_computation | async-start | bytes 8192 | tf_op jit(solution)/shard_map/all_to_all | solution.py:22
  27.0 23.3 %all-to-all-start.1 = ((bf16[8,24,2048]{2,1,0:T(8,128)(2,1)}), bf16[8,24,2048]{2,1,0:T(8,128)(2,1)}, u32[]{:S(2)}, u32[]{:S(2)}) async-start(bf16[8,24,2048]{2,1,0:T(8,128)(2,1)} %bitcast.35), calls=%async_computation.1 | async-start | bytes 1572864 | tf_op jit(solution)/shard_map/all_to_all | solution.py:21
  31.2 81.7 %reduce-scatter.2.cloned.1.call-start = ((), (), s32[]{:S(2)}) async-start(), calls=%async_computation.4 | async-start | bytes 7864320 | tf_op jit(solution)/shard_map/reduce_scatter | solution.py:35
  59.3 10.0 %all-to-all-start.2 = ((f32[8,24,1]{1,2,0:T(1,128)}), f32[8,24,1]{1,2,0:T(1,128)S(1)}, u32[]{:S(2)}, u32[]{:S(2)}) async-start(f32[8,24,1]{1,2,0:T(1,128)} %bitcast.12), calls=%async_computation.3 | async-start | bytes 8192 | tf_op jit(solution)/shard_map/all_to_all | solution.py:33
Sparse Core Ops, SparseCore 0:
  55.5 57.3 reduce-scatter.1
where the time goes:
time: 120 us
  waiting for transfers between devices  69.7 us (58%)
  starting transfers between devices  15 us (12%)
  between operations  14.1 us (12%)
  local copies, waits for them, and re-layouts  8.08 us (7%)
  matrix products  6.86 us (6%)
  other arithmetic  6.03 us (5%)
    reduce_scatter x1, waiting for transfers between devices, shards(): lax.psum_scatter(lax.dot_general(weighted, stored, (((0,), (0,)), ((), ()...  40.6 us
    all_to_all x1, waiting for transfers between devices, shards(): lax.all_to_all(send_rows, 'expert', split_axis=0, concat_axis=0, tiled=True)  19 us
    all_to_all x1, starting transfers between devices, shards(): lax.all_to_all(send_prob, 'expert', split_axis=0, concat_axis=0, tiled=True)  7.25 us
    all_to_all x1, waiting for transfers between devices, shards(): lax.all_to_all(slot_grad, 'expert', split_axis=0, concat_axis=0, tiled=True)  6.46 us
    all_to_all x1, starting transfers between devices, shards(): lax.all_to_all(send_rows, 'expert', split_axis=0, concat_axis=0, tiled=True)  4.2 us
    dot_general x1, matrix products, shards(): lax.dot_general(weighted, stored, (((0,), (0,)), ((), ())), preferred_ele...  3.7 us
    all_to_all x1, waiting for transfers between devices, shards(): lax.all_to_all(send_prob, 'expert', split_axis=0, concat_axis=0, tiled=True)  3.59 us
    all_to_all x1, starting transfers between devices, shards(): lax.all_to_all(slot_grad, 'expert', split_axis=0, concat_axis=0, tiled=True)  3.52 us
  transfers between devices with their start and end apart: 4, of which 4 were waited for; matrix products, arithmetic and copies ran while one was open for 8% of the time, Pallas kernels for 0%

commit v1 on v0

v1 whole, which is shorter than its diff:
```python
import functools

import jax
import jax.numpy as jnp
from jax import lax
from jax.experimental import pallas as pl
from jax.experimental.pallas import tpu as pltpu
from jax.sharding import PartitionSpec as P

LANES = 128
F32 = jnp.float32
BF16 = jnp.bfloat16
ORDER = (4, 1, 5, 2, 6, 7, 3, 0)
LATE = 6


def kernel_call(body, outs, operands, name, flops=0, scratch=(), stay=()):
    nbytes = sum(a.size * a.dtype.itemsize for a in (*outs, *operands))
    vmem, hbm = pl.BlockSpec(memory_space=pltpu.VMEM), pl.BlockSpec(memory_space=pltpu.HBM)
    operands = [
        pltpu.with_memory_space_constraint(a, pltpu.HBM) if i in stay else a
        for i, a in enumerate(operands)
    ]
    return pl.pallas_call(
        body,
        out_shape=outs,
        in_specs=[hbm if i in stay else vmem for i in range(len(operands))],
        out_specs=[vmem] * len(outs),
        scratch_shapes=scratch,
        compiler_params=pltpu.CompilerParams(vmem_limit_bytes=16 * 2**20),
        cost_estimate=pl.CostEstimate(flops=flops, bytes_accessed=nbytes, transcendentals=0),
        name=name,
    )(*operands)


def shape(dims, kind):
    return jax.ShapeDtypeStruct(dims, kind)


def dot(a, b, dims=((1,), (0,)), precision=None):
    return lax.dot_general(
        a, b, (dims, ((), ())), preferred_element_type=F32, precision=precision
    )


def iota(dims, axis):
    return lax.broadcasted_iota(jnp.int32, dims, axis)


def place_body(experts, order, cap, *refs):
    (ids_hbm, prob_hbm, rows_hbm), refs = refs[:3], refs[3:]
    *chunk_refs, within_ref, ids_ref, prob_ref, rows_ref, sems = refs
    copies = [
        pltpu.make_async_copy(source, target, sems.at[i])
        for i, (source, target) in enumerate(
            ((ids_hbm, ids_ref), (prob_hbm, prob_ref), (rows_hbm, rows_ref))
        )
    ]
    for copy in copies:
        copy.start()
    tokens, width = rows_ref.shape
    copies[0].wait()
    ids = ids_ref[...]
    slots, rows = experts * cap, chunk_refs[0].shape[0]
    member = (iota((experts, tokens), 0) == ids).astype(F32)
    earlier = (iota((tokens, tokens), 0) < iota((tokens, tokens), 1)).astype(BF16)
    before = dot(member.astype(BF16), earlier)
    within = jnp.sum(before * member, axis=0, keepdims=True).astype(jnp.int32)
    within_ref[...] = within
    partner = ids ^ lax.axis_index("expert")
    place = 0
    for i, k in enumerate(order):
        place = jnp.where(partner == k, i, place)
    if not order:
        place = ids
    chosen = iota((slots, tokens), 0) == place * cap + within
    copies[1].wait()
    prob = jnp.sum(jnp.where(chosen, prob_ref[...].astype(F32), 0.0), axis=1, keepdims=True)
    chosen = chosen.astype(BF16)
    copies[2].wait()

    def put(columns, values):
        for i, ref in enumerate(chunk_refs):
            ref[:, columns] = values[i * rows : (i + 1) * rows].astype(BF16)

    step = 2 * LANES
    for c in range(0, width, step):
        put(slice(c, c + step), dot(chosen, rows_ref[:, c : c + step]))
    put(slice(width, width + LANES), jnp.broadcast_to(prob, (slots, LANES)))


def weigh_body(replicas, order, *refs):
    n_dp = len(replicas)
    *chunk_refs, rows_ref, prob_ref = refs[: -n_dp - 1]
    weighted_refs, all_ref = refs[-n_dp - 1 : -1], refs[-1]
    width = rows_ref.shape[1]
    chunk = width // n_dp
    size = chunk_refs[0].shape[0]
    for c in range(0, width + LANES, LANES):
        columns = slice(c, c + LANES)
        for k, ref in zip(order or (0,), chunk_refs):
            at = (lax.axis_index("expert") ^ k) * size if order else 0
            all_ref[pl.ds(at, size), columns] = ref[:, columns].astype(F32)
    prob = all_ref[:, width:]
    prob_ref[...] = prob
    replica = lax.axis_index("dp")
    for k, ref in zip(replicas, weighted_refs):
        for c in range(0, chunk, LANES):
            columns = pl.ds(pl.multiple_of((replica ^ k) * chunk + c, LANES), LANES)
            piece = all_ref[:, columns]
            rows_ref[:, columns] = piece.astype(BF16)
            ref[:, c : c + LANES] = (piece * prob).astype(BF16)


def fetch_body(weight_hbm, out_ref, sem):
    copy = pltpu.make_async_copy(weight_hbm, out_ref, sem)
    copy.start()
    copy.wait()


def by_source(column, experts, cap):
    slots = experts * cap
    spread = jnp.where(iota((slots, LANES), 1) == iota((slots, LANES), 0) % cap, column, 0.0)
    if cap % 8 == 0:
        return jnp.sum(spread.reshape(experts, cap, LANES), axis=1)
    owner = (iota((experts, slots), 0) == iota((experts, slots), 1) // cap).astype(F32)
    return dot(owner, spread, precision=lax.Precision.HIGHEST)


def act_body(experts, cap, rows_ref, prob_ref, weight_ref, stored_ref, act_ref, table_ref):
    backed = dot(rows_ref[...], weight_ref[...], ((1,), (1,)))
    act_ref[...] = (prob_ref[:, 0:1] * backed).astype(BF16)
    column = jnp.sum(backed * stored_ref[...].astype(F32), axis=1, keepdims=True)
    table = by_source(column, experts, cap)
    table_ref[...] = jnp.broadcast_to(table[:, None], table_ref.shape)


def gradient_body(n_dp, *refs):
    lhs = jnp.concatenate([ref[...] for ref in refs[:n_dp]], axis=0)
    rhs = jnp.concatenate([ref[...] for ref in refs[n_dp:-1]], axis=0)
    refs[-1][...] = dot(lhs, rhs, ((0,), (0,)))


def pick_body(experts, ids_ref, within_ref, table_ref, out_ref):
    ids = ids_ref[...]
    tokens = ids.shape[1]
    at = jnp.broadcast_to(within_ref[...], (experts, tokens))
    values = jnp.take_along_axis(table_ref[:, 0, :], at, axis=1, mode="promise_in_bounds")
    member = iota((experts, tokens), 0) == ids
    out_ref[...] = jnp.sum(jnp.where(member, values, 0.0), axis=0, keepdims=True)


def shards(n_dp, experts, grad_out, route_prob, expert_ids, saved_act, down_weight):
    slots, ffw = saved_act.shape[2:]
    cap = slots // experts
    tokens, width = grad_out.shape
    chunk = width // n_dp
    stored = saved_act[0, 0]
    order = ORDER if experts == len(ORDER) else ()
    chunks = max(len(order), 1)
    ids = expert_ids.reshape(1, tokens)
    prob_row = route_prob.reshape(1, tokens)

    def swap(array, axis, k):
        size = lax.axis_size(axis)
        return lax.ppermute(array, axis, [(r, r ^ k) for r in range(size)])

    def exchange(array):
        return lax.all_to_all(array, "expert", split_axis=0, concat_axis=0, tiled=True)

    *packed, within = kernel_call(
        functools.partial(place_body, experts, order, cap),
        (shape((slots // chunks, width + LANES), BF16),) * chunks + (shape((1, tokens), jnp.int32),),
        (ids, prob_row, grad_out),
        flops=2 * slots * tokens * width,
        name="place",
        stay=(0, 1, 2),
        scratch=(
            pltpu.VMEM((1, tokens), jnp.int32),
            pltpu.VMEM((1, tokens), BF16),
            pltpu.VMEM((tokens, width), BF16),
            pltpu.SemaphoreType.DMA((3,)),
        ),
    )
    (weight,) = kernel_call(
        fetch_body,
        (shape((ffw, width), BF16),),
        (lax.optimization_barrier((down_weight[0], within))[0],),
        flops=2 * slots * width * ffw,
        name="fetch",
        stay=(0,),
        scratch=(pltpu.SemaphoreType.DMA(()),),
    )
    if order:
        packed[LATE], weight = lax.optimization_barrier((packed[LATE], weight))
        arrived = [swap(rows, "expert", k) if k else rows for k, rows in zip(order, packed)]
    else:
        arrived = [exchange(packed[0])]
    replicas = [*range(2, n_dp), 1, 0]
    all_stored = [swap(stored, "dp", k) if k else stored for k in replicas]

    rows, prob, *weighted = kernel_call(
        functools.partial(weigh_body, replicas, order),
        (shape((slots, width), BF16), shape((slots, LANES), F32))
        + (shape((slots, chunk), BF16),) * n_dp,
        arrived,
        flops=2 * slots * width,
        name="weigh",
        scratch=(pltpu.VMEM((slots, width + LANES), F32),),
    )
    weighted = [swap(rows, "dp", k) if k else rows for k, rows in zip(replicas, weighted)]
    grad_act, table = kernel_call(
        functools.partial(act_body, experts, cap),
        (shape((slots, ffw), BF16), shape((experts, 8, LANES), F32)),
        (rows, prob, weight, stored),
        flops=2 * slots * width * ffw,
        name="act",
    )
    reweight = exchange(table)
    (grad_weight,) = kernel_call(
        functools.partial(gradient_body, n_dp),
        (shape((chunk, ffw), F32),),
        (*weighted, *all_stored),
        flops=2 * n_dp * slots * chunk * ffw,
        name="gradient",
    )
    reweight, grad_weight = lax.optimization_barrier((reweight, grad_weight))
    (grad_prob,) = kernel_call(
        functools.partial(pick_body, experts),
        (shape((1, tokens), F32),),
        (ids, within, reweight),
        name="pick",
    )
    return (grad_act[None, None], grad_weight[None], grad_prob.reshape(tokens, 1))


def solution(mesh):
    return jax.shard_map(
        functools.partial(shards, mesh.shape["dp"], mesh.shape["expert"]),
        mesh=mesh,
        in_specs=(
            P(("dp", "expert"), None),
            P(("dp", "expert"), None),
            P(("dp", "expert"), None),
            P("dp", "expert", None, None),
            P("expert", None, None),
        ),
        out_specs=(
            P("dp", "expert", None, None),
            P("expert", "dp", None),
            P(("dp", "expert"), None),
        ),
        check_vma=False,
    )
```

time: 120 us -> 43.6 us (0.36)
  waiting for transfers between devices: 69.7 us -> 10.9 us
  between operations: 14.1 us -> 0.71 us
  Pallas kernels: 0 us -> 8.42 us
  starting transfers between devices: 15 us -> 23.4 us
  local copies, waits for them, and re-layouts: 8.08 us -> 0.01 us
  matrix products: 6.86 us -> 0 us
  other arithmetic: 6.03 us -> 0 us
    reduce_scatter x1 -> x0, waiting for transfers between devices: 40.6 us -> none  [shards(): lax.psum_scatter(lax.dot_general(weighted, stored, (((0,), (0,)), ((), ()...]
    all_to_all x3 -> x1, waiting for transfers between devices: 29.1 us -> 3.62 us  [exchange(): lax.all_to_all(array, 'expert', split_axis=0, concat_axis=0, tiled=True)]
    ppermute x0 -> x13, starting transfers between devices: none -> 19.8 us  [swap(): return lax.ppermute(array, axis, [(r, r ^ k) for r in range(size)])]
    all_to_all x3 -> x1, starting transfers between devices: 15 us -> 3.62 us  [exchange(): lax.all_to_all(array, 'expert', split_axis=0, concat_axis=0, tiled=True)]
    pallas_call x0 -> x6, Pallas kernels: none -> 8.42 us  [kernel_call(): pl.pallas_call(body, out_shape=outs, in_specs=[hbm if i in stay else vmem...]
    ppermute x0 -> x13, waiting for transfers between devices: none -> 7.25 us  [swap(): return lax.ppermute(array, axis, [(r, r ^ k) for r in range(size)])]
    dot_general x2 -> x0, matrix products: 6.86 us -> none  [the longest x1 3.7 us: shards(): lax.dot_general(weighted, stored, (((0,), (0,)), ((), ())), preferred_ele...]
    scatter x2 -> x0, local copies, waits for them, and re-layouts: 4.27 us -> none  [the longest x1 2.8 us: shards(): send_rows = jnp.zeros((slots, width), jnp.bfloat16).at[placed].set(grad_out)]
  transfers between devices with their start and end apart: 4 -> 14, of which waited for: 4 -> 5; matrix products, arithmetic and copies ran while one was open for 8% -> 0% of each run, Pallas kernels for 0% -> 15%
where the time goes in v1:
time: 43.6 us; the launch traced here: 43.4 us
  starting transfers between devices  23.4 us (54%)
  waiting for transfers between devices  10.9 us (25%)
  Pallas kernels  8.42 us (19%)
  between operations  0.71 us (2%)
    ppermute x13, starting transfers between devices, swap(): return lax.ppermute(array, axis, [(r, r ^ k) for r in range(size)])  19.8 us
    pallas_call x6, Pallas kernels, kernel_call(): pl.pallas_call(body, out_shape=outs, in_specs=[hbm if i in stay else vmem...  8.42 us
    ppermute x13, waiting for transfers between devices, swap(): return lax.ppermute(array, axis, [(r, r ^ k) for r in range(size)])  7.25 us
    all_to_all x1, starting transfers between devices, exchange(): lax.all_to_all(array, 'expert', split_axis=0, concat_axis=0, tiled=True)  3.62 us
    all_to_all x1, waiting for transfers between devices, exchange(): lax.all_to_all(array, 'expert', split_axis=0, concat_axis=0, tiled=True)  3.62 us
  transfers between devices with their start and end apart: 14, of which 5 were waited for; matrix products, arithmetic and copies ran while one was open for 0% of the time, Pallas kernels for 15%

profile of v1, /device:TPU:0, one launch (start us, length us, event | category | flops | bytes accessed | tf_op | source)
XLA Modules:
  0.0 43.4 jit_solution(3404491589410458515)
XLA Ops:
  0.6 1.5 %place.1 = (bf16[24,2176]{1,0:T(8,128)(2,1)S(1)}, bf16[24,2176]{1,0:T(8,128)(2,1)S(1)}, bf16[24,2176]{1,0:T(8,128)(2,1)S(1)}, bf16[24,2176]{1,0:T(8,128)(2,1)S(1...) custom-call(s32[1,128]{1,0:T(1,128)} %bitcast.12, ...), custom_call_target="tpu_custom_call" | custom-call | flops 100663296 | bytes 1361152 | tf_op jit(solution)/shard_map/place/pallas_call | solution.py:24
  2.1 4.1 %collective-permute-start = (bf16[24,2176]{1,0:T(8,128)(2,1)S(1)}, bf16[24,2176]{1,0:T(8,128)(2,1)S(1)}, u32[]{:S(2)}, u32[]{:S(2)}) collective-permute-start(bf16[24,2176]{1,0:T(8,128)(2,1)S(1)} %get-tuple-element.25), channel_id=1, source_target_pairs={{0,4},{1,5},{2,6},{3,7},{4,0},{5,1},{6,2},{7,3},{8,12},{9,13},{10,... | collective-permute-start | bytes 313352 | tf_op jit(solution)/shard_map/ppermute | solution.py:166
  6.2 1.5 %collective-permute-start.10 = (bf16[192,768]{1,0:T(8,128)(2,1)}, bf16[192,768]{1,0:T(8,128)(2,1)S(1)}, u32[]{:S(2)}, u32[]{:S(2)}) collective-permute-start(bf16[192,768]{1,0:T(8,128)(2,1)} %bitcast.7), channel_id=1, source_target_pairs={{0,16},{8,24},{16,0},{24,8},{1,17},{9,25},{17,1},{25,9},{2,18},{10... | collective-permute-start | bytes 884744 | tf_op jit(solution)/shard_map/ppermute | solution.py:166
  7.7 1.5 %collective-permute-start.1 = (bf16[24,2176]{1,0:T(8,128)(2,1)S(1)}, bf16[24,2176]{1,0:T(8,128)(2,1)S(1)}, u32[]{:S(2)}, u32[]{:S(2)}) collective-permute-start(bf16[24,2176]{1,0:T(8,128)(2,1)S(1)} %get-tuple-element.26), channel_id=1, source_target_pairs={{0,1},{1,0},{2,3},{3,2},{4,5},{5,4},{6,7},{7,6},{8,9},{9,8},{10,11... | collective-permute-start | bytes 313352 | tf_op jit(solution)/shard_map/ppermute | solution.py:166
  9.2 0.3 collective-permute-start.2
  9.5 1.6 %collective-permute-start.3 = (bf16[24,2176]{1,0:T(8,128)(2,1)S(1)}, bf16[24,2176]{1,0:T(8,128)(2,1)S(1)}, u32[]{:S(2)}, u32[]{:S(2)}) collective-permute-start(bf16[24,2176]{1,0:T(8,128)(2,1)S(1)} %get-tuple-element.28), channel_id=1, source_target_pairs={{0,2},{1,3},{2,0},{3,1},{4,6},{5,7},{6,4},{7,5},{8,10},{9,11},{10,... | collective-permute-start | bytes 313352 | tf_op jit(solution)/shard_map/ppermute | solution.py:166
  11.1 0.3 collective-permute-done.refs_0_
  11.4 5.9 %collective-permute-start.4 = (bf16[24,2176]{1,0:T(8,128)(2,1)S(1)}, bf16[24,2176]{1,0:T(8,128)(2,1)S(1)}, u32[]{:S(2)}, u32[]{:S(2)}) collective-permute-start(bf16[24,2176]{1,0:T(8,128)(2,1)S(1)} %get-tuple-element.29), channel_id=1, source_target_pairs={{0,6},{1,7},{2,4},{3,5},{4,2},{5,3},{6,0},{7,1},{8,14},{9,15},{10,... | collective-permute-start | bytes 313352 | tf_op jit(solution)/shard_map/ppermute | solution.py:166
  17.3 1.9 %fetch.1.weight_ref = bf16[768,2048]{1,0:T(8,128)(2,1)S(1)} custom-call(bf16[768,2048]{1,0:T(8,128)(2,1)} %bitcast.14), custom_call_target="tpu_custom_call" | custom-call | flops 603979776 | bytes 6291456 | tf_op jit(solution)/shard_map/fetch/pallas_call | solution.py:24
  19.3 0.0 collective-permute-done.1.refs_1_
  19.3 1.0 %collective-permute-start.5 = (bf16[24,2176]{1,0:T(8,128)(2,1)S(1)}, bf16[24,2176]{1,0:T(8,128)(2,1)S(1)}, u32[]{:S(2)}, u32[]{:S(2)}) collective-permute-start(bf16[24,2176]{1,0:T(8,128)(2,1)S(1)} %get-tuple-element.30), channel_id=1, source_target_pairs={{0,7},{1,6},{2,5},{3,4},{4,3},{5,2},{6,1},{7,0},{8,15},{9,14},{10,... | collective-permute-start | bytes 313352 | tf_op jit(solution)/shard_map/ppermute | solution.py:166
  20.3 0.0 collective-permute-done.2.refs_2_
  20.3 0.0 collective-permute-start.6
  20.3 0.0 collective-permute-done.3.refs_3_
  20.3 0.8 %collective-permute-start.11 = (bf16[192,768]{1,0:T(8,128)(2,1)S(1)}, bf16[192,768]{1,0:T(8,128)(2,1)S(1)}, u32[]{:S(2)}, u32[]{:S(2)}) collective-permute-start(bf16[192,768]{1,0:T(8,128)(2,1)S(1)} %bitcast.8), channel_id=1, source_target_pairs={{0,24},{8,16},{16,8},{24,0},{1,25},{9,17},{17,9},{25,1},{2,26},{10... | collective-permute-start | bytes 884744 | tf_op jit(solution)/shard_map/ppermute | solution.py:166
  21.1 0.0 collective-permute-done.4.refs_4_
  21.1 0.9 %collective-permute-start.12 = (bf16[192,768]{1,0:T(8,128)(2,1)S(1)}, bf16[192,768]{1,0:T(8,128)(2,1)S(1)}, u32[]{:S(2)}, u32[]{:S(2)}) collective-permute-start(bf16[192,768]{1,0:T(8,128)(2,1)S(1)} %bitcast.9), channel_id=1, source_target_pairs={{0,8},{8,0},{16,24},{24,16},{1,9},{9,1},{17,25},{25,17},{2,10},{10... | collective-permute-start | bytes 884744 | tf_op jit(solution)/shard_map/ppermute | solution.py:166
  22.0 5.6 %collective-permute-done.5.refs_5_ = bf16[24,2176]{1,0:T(8,128)(2,1)S(1)} collective-permute-done((bf16[24,2176]{1,0:T(8,128)(2,1)S(1)}, bf16[24,2176]{1,0:T(8,128)(2,1)S(1)}, u32[]{:S(2)}, u32[]{:S(2)}) %collective-permute-start.5) | collective-permute-done | bytes 104480 | tf_op jit(solution)/shard_map/ppermute | solution.py:166
  27.6 0.3 collective-permute-done.6.refs_6_
  27.8 0.5 %weigh.1 = (bf16[192,2048]{1,0:T(8,128)(2,1)S(1)}, f32[192,128]{1,0:T(8,128)S(1)}, bf16[192,512]{1,0:T(8,128)(2,1)S(1)}, bf16[192,512]{1,0:T(8,128)(2,1)S(1)}, b...) custom-call(bf16[24,2176]{1,0:T(8,128)(2,1)S(1)} %collective-permute-done.refs_0_, ...), custom_call_target="tpu_custom_call" | custom-call | flops 786432 | bytes 2506752 | tf_op jit(solution)/shard_map/weigh/pallas_call | solution.py:24
  28.3 1.6 %collective-permute-start.7 = (bf16[192,512]{1,0:T(8,128)(2,1)S(1)}, bf16[192,512]{1,0:T(8,128)(2,1)S(1)}, u32[]{:S(2)}, u32[]{:S(2)}) collective-permute-start(bf16[192,512]{1,0:T(8,128)(2,1)S(1)} %get-tuple-element.41), channel_id=1, source_target_pairs={{0,16},{8,24},{16,0},{24,8},{1,17},{9,25},{17,1},{25,9},{2,18},{10... | collective-permute-start | bytes 589832 | tf_op jit(solution)/shard_map/ppermute | solution.py:166
  29.9 0.0 collective-permute-start.8
  29.9 0.0 collective-permute-done.10.refs_4_
  29.9 0.6 %collective-permute-start.9 = (bf16[192,512]{1,0:T(8,128)(2,1)S(1)}, bf16[192,512]{1,0:T(8,128)(2,1)S(1)}, u32[]{:S(2)}, u32[]{:S(2)}) collective-permute-start(bf16[192,512]{1,0:T(8,128)(2,1)S(1)} %get-tuple-element.43), channel_id=1, source_target_pairs={{0,8},{8,0},{16,24},{24,16},{1,9},{9,1},{17,25},{25,17},{2,10},{10... | collective-permute-start | bytes 589832 | tf_op jit(solution)/shard_map/ppermute | solution.py:166
  30.5 2.0 %act.1 = (bf16[192,768]{1,0:T(8,128)(2,1)}, f32[8,8,128]{2,1,0:T(8,128)}) custom-call(bf16[192,2048]{1,0:T(8,128)(2,1)S(1)} %get-tuple-element.36.rows_ref, f32[192,128]{1,0:T(8,128)S(1)} %get-tuple-element.37.prob_ref, bf16[768,2048]{1,0:T(8,128)(2,1)S(1)} %fetch.1.weight_ref, bf16[192,768]{1,0:T(8,128)(2,1)S(1)} %bitcast.10), custom_call_target="tpu_custom_call" | custom-call | flops 603979776 | bytes 4653056 | tf_op jit(solution)/shard_map/act/pallas_call | solution.py:24
  32.5 3.6 %all-to-all-start = ((f32[8,8,128]{2,1,0:T(8,128)}), f32[8,8,128]{2,1,0:T(8,128)S(1)}, u32[]{:S(2)}, u32[]{:S(2)}) async-start(f32[8,8,128]{2,1,0:T(8,128)} %get-tuple-element.40), calls=%async_computation | async-start | bytes 65536 | tf_op jit(solution)/shard_map/all_to_all | solution.py:169
  36.1 0.0 collective-permute-done.11.refs_5_
  36.1 0.0 collective-permute-done.7.refs_0_
  36.1 1.1 %collective-permute-done.8.refs_1_ = bf16[192,512]{1,0:T(8,128)(2,1)S(1)} collective-permute-done((bf16[192,512]{1,0:T(8,128)(2,1)S(1)}, bf16[192,512]{1,0:T(8,128)(2,1)S(1)}, u32[]{:S(2)}, u32[]{:S(2)}) %collective-permute-start.8) | collective-permute-done | bytes 196640 | tf_op jit(solution)/shard_map/ppermute | solution.py:166
  37.2 2.0 %gradient.1 = f32[512,768]{1,0:T(8,128)} custom-call(bf16[192,512]{1,0:T(8,128)(2,1)S(1)} %collective-permute-done.7.refs_0_, bf16[192,512]{1,0:T(8,128)(2,1)S(1)} %collective-permute-done.8.refs_1_, bf16[192,512]{1,0:T(8,128)(2,1)S(1)} %collective-permute-done.9.refs_2_, bf16[192,512]{1,0:T(8,128)(2,1)S(1)} %get-tuple-element.44.refs_3_, ...), custom_call_target="tpu_custom_call" | custom-call | flops 603979776 | bytes 3538944 | tf_op jit(solution)/shard_map/gradient/pallas_call | solution.py:24
  39.2 3.6 %all-to-all-done.table_ref = f32[8,8,128]{2,1,0:T(8,128)S(1)} async-done(((f32[8,8,128]{2,1,0:T(8,128)}), f32[8,8,128]{2,1,0:T(8,128)S(1)}, u32[]{:S(2)}, u32[]{:S(2)}) %all-to-all-start) | async-done | bytes 32800 | tf_op jit(solution)/shard_map/all_to_all | solution.py:169
  42.8 0.6 %pick.1 = f32[1,128]{1,0:T(1,128)} custom-call(s32[1,128]{1,0:T(1,128)S(1)} %bitcast.13, s32[1,128]{1,0:T(1,128)S(1)} %get-tuple-element.32.within_ref, f32[8,8,128]{2,1,0:T(8,128)S(1)} %all-to-all-done.table_ref), custom_call_target="tpu_custom_call" | custom-call | bytes 34304 | tf_op jit(solution)/shard_map/pick/pallas_call | solution.py:24
  (6 shorter events, 0.0 us)
Async XLA Ops:
  2.1 9.3 %collective-permute-start = (bf16[24,2176]{1,0:T(8,128)(2,1)S(1)}, bf16[24,2176]{1,0:T(8,128)(2,1)S(1)}, u32[]{:S(2)}, u32[]{:S(2)}) collective-permute-start(bf16[24,2176]{1,0:T(8,128)(2,1)S(1)} %get-tuple-element.25), channel_id=1, source_target_pairs={{0,4},{1,5},{2,6},{3,7},{4,0},{5,1},{6,2},{7,3},{8,12},{9,13},{10,... | collective-permute-start | bytes 313352 | tf_op jit(solution)/shard_map/ppermute | solution.py:166
  6.2 23.7 %collective-permute-start.10 = (bf16[192,768]{1,0:T(8,128)(2,1)}, bf16[192,768]{1,0:T(8,128)(2,1)S(1)}, u32[]{:S(2)}, u32[]{:S(2)}) collective-permute-start(bf16[192,768]{1,0:T(8,128)(2,1)} %bitcast.7), channel_id=1, source_target_pairs={{0,16},{8,24},{16,0},{24,8},{1,17},{9,25},{17,1},{25,9},{2,18},{10... | collective-permute-start | bytes 884744 | tf_op jit(solution)/shard_map/ppermute | solution.py:166
  7.7 11.5 %collective-permute-start.1 = (bf16[24,2176]{1,0:T(8,128)(2,1)S(1)}, bf16[24,2176]{1,0:T(8,128)(2,1)S(1)}, u32[]{:S(2)}, u32[]{:S(2)}) collective-permute-start(bf16[24,2176]{1,0:T(8,128)(2,1)S(1)} %get-tuple-element.26), channel_id=1, source_target_pairs={{0,1},{1,0},{2,3},{3,2},{4,5},{5,4},{6,7},{7,6},{8,9},{9,8},{10,11... | collective-permute-start | bytes 313352 | tf_op jit(solution)/shard_map/ppermute | solution.py:166
  9.2 11.0 %collective-permute-start.2 = (bf16[24,2176]{1,0:T(8,128)(2,1)S(1)}, bf16[24,2176]{1,0:T(8,128)(2,1)S(1)}, u32[]{:S(2)}, u32[]{:S(2)}) collective-permute-start(bf16[24,2176]{1,0:T(8,128)(2,1)S(1)} %get-tuple-element.27), channel_id=1, source_target_pairs={{0,5},{1,4},{2,7},{3,6},{4,1},{5,0},{6,3},{7,2},{8,13},{9,12},{10,... | collective-permute-start | bytes 313352 | tf_op jit(solution)/shard_map/ppermute | solution.py:166
  9.5 10.7 %collective-permute-start.3 = (bf16[24,2176]{1,0:T(8,128)(2,1)S(1)}, bf16[24,2176]{1,0:T(8,128)(2,1)S(1)}, u32[]{:S(2)}, u32[]{:S(2)}) collective-permute-start(bf16[24,2176]{1,0:T(8,128)(2,1)S(1)} %get-tuple-element.28), channel_id=1, source_target_pairs={{0,2},{1,3},{2,0},{3,1},{4,6},{5,7},{6,4},{7,5},{8,10},{9,11},{10,... | collective-permute-start | bytes 313352 | tf_op jit(solution)/shard_map/ppermute | solution.py:166
  11.4 9.6 %collective-permute-start.4 = (bf16[24,2176]{1,0:T(8,128)(2,1)S(1)}, bf16[24,2176]{1,0:T(8,128)(2,1)S(1)}, u32[]{:S(2)}, u32[]{:S(2)}) collective-permute-start(bf16[24,2176]{1,0:T(8,128)(2,1)S(1)} %get-tuple-element.29), channel_id=1, source_target_pairs={{0,6},{1,7},{2,4},{3,5},{4,2},{5,3},{6,0},{7,1},{8,14},{9,15},{10,... | collective-permute-start | bytes 313352 | tf_op jit(solution)/shard_map/ppermute | solution.py:166
  17.3 3.0 %copy-start = (bf16[1,1,192,768]{3,2,1,0:T(8,128)(2,1)S(1)}, bf16[1,1,192,768]{3,2,1,0:T(8,128)(2,1)}, u32[]{:S(2)}) copy-start(bf16[1,1,192,768]{3,2,1,0:T(8,128)(2,1)} %param.8) | copy-start | bytes 884740
  19.3 8.3 %collective-permute-start.5 = (bf16[24,2176]{1,0:T(8,128)(2,1)S(1)}, bf16[24,2176]{1,0:T(8,128)(2,1)S(1)}, u32[]{:S(2)}, u32[]{:S(2)}) collective-permute-start(bf16[24,2176]{1,0:T(8,128)(2,1)S(1)} %get-tuple-element.30), channel_id=1, source_target_pairs={{0,7},{1,6},{2,5},{3,4},{4,3},{5,2},{6,1},{7,0},{8,15},{9,14},{10,... | collective-permute-start | bytes 313352 | tf_op jit(solution)/shard_map/ppermute | solution.py:166
  20.3 7.6 %collective-permute-start.6 = (bf16[24,2176]{1,0:T(8,128)(2,1)S(1)}, bf16[24,2176]{1,0:T(8,128)(2,1)S(1)}, u32[]{:S(2)}, u32[]{:S(2)}) collective-permute-start(bf16[24,2176]{1,0:T(8,128)(2,1)S(1)} %get-tuple-element.34), channel_id=1, source_target_pairs={{0,3},{1,2},{2,1},{3,0},{4,7},{5,6},{6,5},{7,4},{8,11},{9,10},{10,... | collective-permute-start | bytes 313352 | tf_op jit(solution)/shard_map/ppermute | solution.py:166
  20.3 15.8 %collective-permute-start.11 = (bf16[192,768]{1,0:T(8,128)(2,1)S(1)}, bf16[192,768]{1,0:T(8,128)(2,1)S(1)}, u32[]{:S(2)}, u32[]{:S(2)}) collective-permute-start(bf16[192,768]{1,0:T(8,128)(2,1)S(1)} %bitcast.8), channel_id=1, source_target_pairs={{0,24},{8,16},{16,8},{24,0},{1,25},{9,17},{17,9},{25,1},{2,26},{10... | collective-permute-start | bytes 884744 | tf_op jit(solution)/shard_map/ppermute | solution.py:166
  21.1 15.1 %collective-permute-start.12 = (bf16[192,768]{1,0:T(8,128)(2,1)S(1)}, bf16[192,768]{1,0:T(8,128)(2,1)S(1)}, u32[]{:S(2)}, u32[]{:S(2)}) collective-permute-start(bf16[192,768]{1,0:T(8,128)(2,1)S(1)} %bitcast.9), channel_id=1, source_target_pairs={{0,8},{8,0},{16,24},{24,16},{1,9},{9,1},{17,25},{25,17},{2,10},{10... | collective-permute-start | bytes 884744 | tf_op jit(solution)/shard_map/ppermute | solution.py:166
  28.3 7.8 %collective-permute-start.7 = (bf16[192,512]{1,0:T(8,128)(2,1)S(1)}, bf16[192,512]{1,0:T(8,128)(2,1)S(1)}, u32[]{:S(2)}, u32[]{:S(2)}) collective-permute-start(bf16[192,512]{1,0:T(8,128)(2,1)S(1)} %get-tuple-element.41), channel_id=1, source_target_pairs={{0,16},{8,24},{16,0},{24,8},{1,17},{9,25},{17,1},{25,9},{2,18},{10... | collective-permute-start | bytes 589832 | tf_op jit(solution)/shard_map/ppermute | solution.py:166
  29.9 7.3 %collective-permute-start.8 = (bf16[192,512]{1,0:T(8,128)(2,1)S(1)}, bf16[192,512]{1,0:T(8,128)(2,1)S(1)}, u32[]{:S(2)}, u32[]{:S(2)}) collective-permute-start(bf16[192,512]{1,0:T(8,128)(2,1)S(1)} %get-tuple-element.42), channel_id=1, source_target_pairs={{0,24},{8,16},{16,8},{24,0},{1,25},{9,17},{17,9},{25,1},{2,26},{10... | collective-permute-start | bytes 589832 | tf_op jit(solution)/shard_map/ppermute | solution.py:166
  29.9 7.3 %collective-permute-start.9 = (bf16[192,512]{1,0:T(8,128)(2,1)S(1)}, bf16[192,512]{1,0:T(8,128)(2,1)S(1)}, u32[]{:S(2)}, u32[]{:S(2)}) collective-permute-start(bf16[192,512]{1,0:T(8,128)(2,1)S(1)} %get-tuple-element.43), channel_id=1, source_target_pairs={{0,8},{8,0},{16,24},{24,16},{1,9},{9,1},{17,25},{25,17},{2,10},{10... | collective-permute-start | bytes 589832 | tf_op jit(solution)/shard_map/ppermute | solution.py:166
  30.5 12.3 %copy-start.1 = (s32[128,1]{0,1:T(1,128)S(1)}, s32[128,1]{0,1:T(1,128)}, u32[]{:S(2)}) copy-start(s32[128,1]{0,1:T(1,128)} %param.7) | copy-start | bytes 1540
  32.5 10.3 %all-to-all-start = ((f32[8,8,128]{2,1,0:T(8,128)}), f32[8,8,128]{2,1,0:T(8,128)S(1)}, u32[]{:S(2)}, u32[]{:S(2)}) async-start(f32[8,8,128]{2,1,0:T(8,128)} %get-tuple-element.40), calls=%async_computation | async-start | bytes 65536 | tf_op jit(solution)/shard_map/all_to_all | solution.py:169

commit v2 on v1

--- a/solution.py
+++ b/solution.py
@@ -10,7 +10,7 @@
 LANES = 128
 F32 = jnp.float32
 BF16 = jnp.bfloat16
-ORDER = (4, 1, 5, 2, 6, 7, 3, 0)
+ORDER = (6, 1, 7, 2, 4, 5, 3, 0)
 LATE = 6
 
 
@@ -197,7 +197,11 @@
     else:
         arrived = [exchange(packed[0])]
     replicas = [*range(2, n_dp), 1, 0]
-    all_stored = [swap(stored, "dp", k) if k else stored for k in replicas]
+    held, step = {0: stored}, n_dp // 2
+    while step:
+        held |= {k | step: swap(array, "dp", step) for k, array in held.items()}
+        step //= 2
+    all_stored = [held[k] for k in replicas]
 
     rows, prob, *weighted = kernel_call(
         functools.partial(weigh_body, replicas, order),
@@ -216,7 +220,7 @@
         flops=2 * slots * width * ffw,
         name="act",
     )
-    reweight = exchange(table)
+    returned = exchange(table)
     (grad_weight,) = kernel_call(
         functools.partial(gradient_body, n_dp),
         (shape((chunk, ffw), F32),),
@@ -224,11 +228,11 @@
         flops=2 * n_dp * slots * chunk * ffw,
         name="gradient",
     )
-    reweight, grad_weight = lax.optimization_barrier((reweight, grad_weight))
+    returned, grad_weight = lax.optimization_barrier((returned, grad_weight))
     (grad_prob,) = kernel_call(
         functools.partial(pick_body, experts),
         (shape((1, tokens), F32),),
-        (ids, within, reweight),
+        (ids, within, returned),
         name="pick",
     )
     return (grad_act[None, None], grad_weight[None], grad_prob.reshape(tokens, 1))

time: 43.6 us -> 44.4 us (1.018)
  starting transfers between devices: 23.4 us -> 25.2 us
  waiting for transfers between devices: 10.9 us -> 9.86 us
    ppermute x13, waiting for transfers between devices: 7.25 us -> 5.19 us  [swap(): return lax.ppermute(array, axis, [(r, r ^ k) for r in range(size)])]
    all_to_all x1, starting transfers between devices: 3.62 us -> 5.03 us  [exchange(): lax.all_to_all(array, 'expert', split_axis=0, concat_axis=0, tiled=True)]
    all_to_all x1, waiting for transfers between devices: 3.62 us -> 4.67 us  [exchange(): lax.all_to_all(array, 'expert', split_axis=0, concat_axis=0, tiled=True)]
  transfers between devices with their start and end apart: 14 -> 14, of which waited for: 5 -> 3; matrix products, arithmetic and copies ran while one was open for 0% -> 0% of each run, Pallas kernels for 15% -> 18%
where the time goes in v2:
time: 44.4 us; the launch traced here: 44.2 us
  starting transfers between devices  25.2 us (57%)
  waiting for transfers between devices  9.86 us (22%)
  Pallas kernels  8.42 us (19%)
  between operations  0.72 us (2%)
    ppermute x13, starting transfers between devices, swap(): return lax.ppermute(array, axis, [(r, r ^ k) for r in range(size)])  20.2 us
    pallas_call x6, Pallas kernels, kernel_call(): pl.pallas_call(body, out_shape=outs, in_specs=[hbm if i in stay else vmem...  8.42 us
    ppermute x13, waiting for transfers between devices, swap(): return lax.ppermute(array, axis, [(r, r ^ k) for r in range(size)])  5.19 us
    all_to_all x1, starting transfers between devices, exchange(): lax.all_to_all(array, 'expert', split_axis=0, concat_axis=0, tiled=True)  5.03 us
    all_to_all x1, waiting for transfers between devices, exchange(): lax.all_to_all(array, 'expert', split_axis=0, concat_axis=0, tiled=True)  4.67 us
  transfers between devices with their start and end apart: 14, of which 3 were waited for; matrix products, arithmetic and copies ran while one was open for 0% of the time, Pallas kernels for 18%

profile of v2, /device:TPU:0, one launch (start us, length us, event | category | flops | bytes accessed | tf_op | source)
XLA Modules:
  0.0 44.2 jit_solution(2060068144392354484)
XLA Ops:
  0.6 3.0 %collective-permute-start.10 = (bf16[192,768]{1,0:T(8,128)(2,1)}, bf16[192,768]{1,0:T(8,128)(2,1)S(1)}, u32[]{:S(2)}, u32[]{:S(2)}) collective-permute-start(bf16[192,768]{1,0:T(8,128)(2,1)} %bitcast.7), channel_id=1, source_target_pairs={{0,16},{8,24},{16,0},{24,8},{1,17},{9,25},{17,1},{25,9},{2,18},{10... | collective-permute-start | bytes 884744 | tf_op jit(solution)/shard_map/ppermute | solution.py:166
  3.7 1.5 %place.1 = (bf16[24,2176]{1,0:T(8,128)(2,1)S(1)}, bf16[24,2176]{1,0:T(8,128)(2,1)S(1)}, bf16[24,2176]{1,0:T(8,128)(2,1)S(1)}, bf16[24,2176]{1,0:T(8,128)(2,1)S(1...) custom-call(s32[1,128]{1,0:T(1,128)} %bitcast.11, ...), custom_call_target="tpu_custom_call" | custom-call | flops 100663296 | bytes 1361152 | tf_op jit(solution)/shard_map/place/pallas_call | solution.py:24
  5.1 3.7 %collective-permute-start = (bf16[24,2176]{1,0:T(8,128)(2,1)S(1)}, bf16[24,2176]{1,0:T(8,128)(2,1)S(1)}, u32[]{:S(2)}, u32[]{:S(2)}) collective-permute-start(bf16[24,2176]{1,0:T(8,128)(2,1)S(1)} %get-tuple-element.25), channel_id=1, source_target_pairs={{0,6},{1,7},{2,4},{3,5},{4,2},{5,3},{6,0},{7,1},{8,14},{9,15},{10,... | collective-permute-start | bytes 313352 | tf_op jit(solution)/shard_map/ppermute | solution.py:166
  8.8 1.5 %collective-permute-start.1 = (bf16[24,2176]{1,0:T(8,128)(2,1)S(1)}, bf16[24,2176]{1,0:T(8,128)(2,1)S(1)}, u32[]{:S(2)}, u32[]{:S(2)}) collective-permute-start(bf16[24,2176]{1,0:T(8,128)(2,1)S(1)} %get-tuple-element.26), channel_id=1, source_target_pairs={{0,1},{1,0},{2,3},{3,2},{4,5},{5,4},{6,7},{7,6},{8,9},{9,8},{10,11... | collective-permute-start | bytes 313352 | tf_op jit(solution)/shard_map/ppermute | solution.py:166
  10.3 0.2 collective-permute-start.2
  10.5 0.0 collective-permute-start.3
  10.5 1.9 %fetch.1.weight_ref = bf16[768,2048]{1,0:T(8,128)(2,1)S(1)} custom-call(bf16[768,2048]{1,0:T(8,128)(2,1)} %bitcast.13), custom_call_target="tpu_custom_call" | custom-call | flops 603979776 | bytes 6291456 | tf_op jit(solution)/shard_map/fetch/pallas_call | solution.py:24
  12.4 0.0 collective-permute-done.refs_0_
  12.5 5.6 %collective-permute-start.4 = (bf16[24,2176]{1,0:T(8,128)(2,1)S(1)}, bf16[24,2176]{1,0:T(8,128)(2,1)S(1)}, u32[]{:S(2)}, u32[]{:S(2)}) collective-permute-start(bf16[24,2176]{1,0:T(8,128)(2,1)S(1)} %get-tuple-element.29), channel_id=1, source_target_pairs={{0,4},{1,5},{2,6},{3,7},{4,0},{5,1},{6,2},{7,3},{8,12},{9,13},{10,... | collective-permute-start | bytes 313352 | tf_op jit(solution)/shard_map/ppermute | solution.py:166
  18.1 0.0 collective-permute-done.1.refs_1_
  18.1 0.9 %collective-permute-start.5 = (bf16[24,2176]{1,0:T(8,128)(2,1)S(1)}, bf16[24,2176]{1,0:T(8,128)(2,1)S(1)}, u32[]{:S(2)}, u32[]{:S(2)}) collective-permute-start(bf16[24,2176]{1,0:T(8,128)(2,1)S(1)} %get-tuple-element.30), channel_id=1, source_target_pairs={{0,5},{1,4},{2,7},{3,6},{4,1},{5,0},{6,3},{7,2},{8,13},{9,12},{10,... | collective-permute-start | bytes 313352 | tf_op jit(solution)/shard_map/ppermute | solution.py:166
  19.0 0.0 collective-permute-done.2.refs_2_
  19.0 2.5 %collective-permute-start.6 = (bf16[24,2176]{1,0:T(8,128)(2,1)S(1)}, bf16[24,2176]{1,0:T(8,128)(2,1)S(1)}, u32[]{:S(2)}, u32[]{:S(2)}) collective-permute-start(bf16[24,2176]{1,0:T(8,128)(2,1)S(1)} %get-tuple-element.34), channel_id=1, source_target_pairs={{0,3},{1,2},{2,1},{3,0},{4,7},{5,6},{6,5},{7,4},{8,11},{9,10},{10,... | collective-permute-start | bytes 313352 | tf_op jit(solution)/shard_map/ppermute | solution.py:166
  21.6 0.0 collective-permute-done.3.refs_3_
  21.6 0.0 collective-permute-start.12
  21.6 0.0 collective-permute-done.10.refs_4_
  21.6 0.5 %collective-permute-start.11 = (bf16[192,768]{1,0:T(8,128)(2,1)S(1)}, bf16[192,768]{1,0:T(8,128)(2,1)S(1)}, u32[]{:S(2)}, u32[]{:S(2)}) collective-permute-start(bf16[192,768]{1,0:T(8,128)(2,1)S(1)} %collective-permute-done.10.refs_4_), channel_id=1, source_target_pairs={{0,8},{8,0},{16,24},{24,16},{1,9},{9,1},{17,25},{25,17},{2,10},{10... | collective-permute-start | bytes 884744 | tf_op jit(solution)/shard_map/ppermute | solution.py:166
  22.1 3.0 %collective-permute-done.4.refs_4_ = bf16[24,2176]{1,0:T(8,128)(2,1)S(1)} collective-permute-done((bf16[24,2176]{1,0:T(8,128)(2,1)S(1)}, bf16[24,2176]{1,0:T(8,128)(2,1)S(1)}, u32[]{:S(2)}, u32[]{:S(2)}) %collective-permute-start.4) | collective-permute-done | bytes 104480 | tf_op jit(solution)/shard_map/ppermute | solution.py:166
  25.1 2.1 %collective-permute-done.5.refs_5_ = bf16[24,2176]{1,0:T(8,128)(2,1)S(1)} collective-permute-done((bf16[24,2176]{1,0:T(8,128)(2,1)S(1)}, bf16[24,2176]{1,0:T(8,128)(2,1)S(1)}, u32[]{:S(2)}, u32[]{:S(2)}) %collective-permute-start.5) | collective-permute-done | bytes 104480 | tf_op jit(solution)/shard_map/ppermute | solution.py:166
  27.2 0.0 collective-permute-done.6.refs_6_
  27.2 0.5 %weigh.1 = (bf16[192,2048]{1,0:T(8,128)(2,1)S(1)}, f32[192,128]{1,0:T(8,128)S(1)}, bf16[192,512]{1,0:T(8,128)(2,1)S(1)}, bf16[192,512]{1,0:T(8,128)(2,1)S(1)}, b...) custom-call(bf16[24,2176]{1,0:T(8,128)(2,1)S(1)} %collective-permute-done.refs_0_, ...), custom_call_target="tpu_custom_call" | custom-call | flops 786432 | bytes 2506752 | tf_op jit(solution)/shard_map/weigh/pallas_call | solution.py:24
  27.7 0.6 %collective-permute-start.7 = (bf16[192,512]{1,0:T(8,128)(2,1)S(1)}, bf16[192,512]{1,0:T(8,128)(2,1)S(1)}, u32[]{:S(2)}, u32[]{:S(2)}) collective-permute-start(bf16[192,512]{1,0:T(8,128)(2,1)S(1)} %get-tuple-element.41), channel_id=1, source_target_pairs={{0,16},{8,24},{16,0},{24,8},{1,17},{9,25},{17,1},{25,9},{2,18},{10... | collective-permute-start | bytes 589832 | tf_op jit(solution)/shard_map/ppermute | solution.py:166
  28.3 0.2 collective-permute-start.8
  28.5 1.4 %collective-permute-start.9 = (bf16[192,512]{1,0:T(8,128)(2,1)S(1)}, bf16[192,512]{1,0:T(8,128)(2,1)S(1)}, u32[]{:S(2)}, u32[]{:S(2)}) collective-permute-start(bf16[192,512]{1,0:T(8,128)(2,1)S(1)} %get-tuple-element.43), channel_id=1, source_target_pairs={{0,8},{8,0},{16,24},{24,16},{1,9},{9,1},{17,25},{25,17},{2,10},{10... | collective-permute-start | bytes 589832 | tf_op jit(solution)/shard_map/ppermute | solution.py:166
  29.9 2.0 %act.1 = (bf16[192,768]{1,0:T(8,128)(2,1)}, f32[8,8,128]{2,1,0:T(8,128)}) custom-call(bf16[192,2048]{1,0:T(8,128)(2,1)S(1)} %get-tuple-element.36.rows_ref, f32[192,128]{1,0:T(8,128)S(1)} %get-tuple-element.37.prob_ref, bf16[768,2048]{1,0:T(8,128)(2,1)S(1)} %fetch.1.weight_ref, bf16[192,768]{1,0:T(8,128)(2,1)S(1)} %bitcast.9), custom_call_target="tpu_custom_call" | custom-call | flops 603979776 | bytes 4653056 | tf_op jit(solution)/shard_map/act/pallas_call | solution.py:24
  31.9 5.0 %all-to-all-start = ((f32[8,8,128]{2,1,0:T(8,128)}), f32[8,8,128]{2,1,0:T(8,128)S(1)}, u32[]{:S(2)}, u32[]{:S(2)}) async-start(f32[8,8,128]{2,1,0:T(8,128)} %get-tuple-element.40), calls=%async_computation | async-start | bytes 65536 | tf_op jit(solution)/shard_map/all_to_all | solution.py:169
  36.9 0.0 collective-permute-done.12.refs_6_
  37.0 0.0 collective-permute-done.9.refs_2_
  37.0 0.0 collective-permute-done.11.refs_5_
  37.0 2.0 %gradient.1 = f32[512,768]{1,0:T(8,128)} custom-call(bf16[192,512]{1,0:T(8,128)(2,1)S(1)} %collective-permute-done.7.refs_0_, bf16[192,512]{1,0:T(8,128)(2,1)S(1)} %collective-permute-done.8.refs_1_, bf16[192,512]{1,0:T(8,128)(2,1)S(1)} %collective-permute-done.9.refs_2_, bf16[192,512]{1,0:T(8,128)(2,1)S(1)} %get-tuple-element.44.refs_3_, ...), custom_call_target="tpu_custom_call" | custom-call | flops 603979776 | bytes 3538944 | tf_op jit(solution)/shard_map/gradient/pallas_call | solution.py:24
  39.0 4.7 %all-to-all-done.table_ref = f32[8,8,128]{2,1,0:T(8,128)S(1)} async-done(((f32[8,8,128]{2,1,0:T(8,128)}), f32[8,8,128]{2,1,0:T(8,128)S(1)}, u32[]{:S(2)}, u32[]{:S(2)}) %all-to-all-start) | async-done | bytes 32800 | tf_op jit(solution)/shard_map/all_to_all | solution.py:169
  43.6 0.6 %pick.1 = f32[1,128]{1,0:T(1,128)} custom-call(s32[1,128]{1,0:T(1,128)S(1)} %bitcast.12, s32[1,128]{1,0:T(1,128)S(1)} %get-tuple-element.32.within_ref, f32[8,8,128]{2,1,0:T(8,128)S(1)} %all-to-all-done.table_ref), custom_call_target="tpu_custom_call" | custom-call | bytes 34304 | tf_op jit(solution)/shard_map/pick/pallas_call | solution.py:24
  (6 shorter events, 0.0 us)
Async XLA Ops:
  0.6 20.9 %collective-permute-start.10 = (bf16[192,768]{1,0:T(8,128)(2,1)}, bf16[192,768]{1,0:T(8,128)(2,1)S(1)}, u32[]{:S(2)}, u32[]{:S(2)}) collective-permute-start(bf16[192,768]{1,0:T(8,128)(2,1)} %bitcast.7), channel_id=1, source_target_pairs={{0,16},{8,24},{16,0},{24,8},{1,17},{9,25},{17,1},{25,9},{2,18},{10... | collective-permute-start | bytes 884744 | tf_op jit(solution)/shard_map/ppermute | solution.py:166
  5.1 7.3 %collective-permute-start = (bf16[24,2176]{1,0:T(8,128)(2,1)S(1)}, bf16[24,2176]{1,0:T(8,128)(2,1)S(1)}, u32[]{:S(2)}, u32[]{:S(2)}) collective-permute-start(bf16[24,2176]{1,0:T(8,128)(2,1)S(1)} %get-tuple-element.25), channel_id=1, source_target_pairs={{0,6},{1,7},{2,4},{3,5},{4,2},{5,3},{6,0},{7,1},{8,14},{9,15},{10,... | collective-permute-start | bytes 313352 | tf_op jit(solution)/shard_map/ppermute | solution.py:166
  8.8 9.3 %collective-permute-start.1 = (bf16[24,2176]{1,0:T(8,128)(2,1)S(1)}, bf16[24,2176]{1,0:T(8,128)(2,1)S(1)}, u32[]{:S(2)}, u32[]{:S(2)}) collective-permute-start(bf16[24,2176]{1,0:T(8,128)(2,1)S(1)} %get-tuple-element.26), channel_id=1, source_target_pairs={{0,1},{1,0},{2,3},{3,2},{4,5},{5,4},{6,7},{7,6},{8,9},{9,8},{10,11... | collective-permute-start | bytes 313352 | tf_op jit(solution)/shard_map/ppermute | solution.py:166
  10.3 8.7 %collective-permute-start.2 = (bf16[24,2176]{1,0:T(8,128)(2,1)S(1)}, bf16[24,2176]{1,0:T(8,128)(2,1)S(1)}, u32[]{:S(2)}, u32[]{:S(2)}) collective-permute-start(bf16[24,2176]{1,0:T(8,128)(2,1)S(1)} %get-tuple-element.27), channel_id=1, source_target_pairs={{0,7},{1,6},{2,5},{3,4},{4,3},{5,2},{6,1},{7,0},{8,15},{9,14},{10,... | collective-permute-start | bytes 313352 | tf_op jit(solution)/shard_map/ppermute | solution.py:166
  10.5 11.1 %collective-permute-start.3 = (bf16[24,2176]{1,0:T(8,128)(2,1)S(1)}, bf16[24,2176]{1,0:T(8,128)(2,1)S(1)}, u32[]{:S(2)}, u32[]{:S(2)}) collective-permute-start(bf16[24,2176]{1,0:T(8,128)(2,1)S(1)} %get-tuple-element.28), channel_id=1, source_target_pairs={{0,2},{1,3},{2,0},{3,1},{4,6},{5,7},{6,4},{7,5},{8,10},{9,11},{10,... | collective-permute-start | bytes 313352 | tf_op jit(solution)/shard_map/ppermute | solution.py:166
  10.5 11.1 %copy-start = (bf16[1,1,192,768]{3,2,1,0:T(8,128)(2,1)S(1)}, bf16[1,1,192,768]{3,2,1,0:T(8,128)(2,1)}, u32[]{:S(2)}) copy-start(bf16[1,1,192,768]{3,2,1,0:T(8,128)(2,1)} %param.8) | copy-start | bytes 884740
  12.5 12.6 %collective-permute-start.4 = (bf16[24,2176]{1,0:T(8,128)(2,1)S(1)}, bf16[24,2176]{1,0:T(8,128)(2,1)S(1)}, u32[]{:S(2)}, u32[]{:S(2)}) collective-permute-start(bf16[24,2176]{1,0:T(8,128)(2,1)S(1)} %get-tuple-element.29), channel_id=1, source_target_pairs={{0,4},{1,5},{2,6},{3,7},{4,0},{5,1},{6,2},{7,3},{8,12},{9,13},{10,... | collective-permute-start | bytes 313352 | tf_op jit(solution)/shard_map/ppermute | solution.py:166
  18.1 9.2 %collective-permute-start.5 = (bf16[24,2176]{1,0:T(8,128)(2,1)S(1)}, bf16[24,2176]{1,0:T(8,128)(2,1)S(1)}, u32[]{:S(2)}, u32[]{:S(2)}) collective-permute-start(bf16[24,2176]{1,0:T(8,128)(2,1)S(1)} %get-tuple-element.30), channel_id=1, source_target_pairs={{0,5},{1,4},{2,7},{3,6},{4,1},{5,0},{6,3},{7,2},{8,13},{9,12},{10,... | collective-permute-start | bytes 313352 | tf_op jit(solution)/shard_map/ppermute | solution.py:166
  19.0 8.2 %collective-permute-start.6 = (bf16[24,2176]{1,0:T(8,128)(2,1)S(1)}, bf16[24,2176]{1,0:T(8,128)(2,1)S(1)}, u32[]{:S(2)}, u32[]{:S(2)}) collective-permute-start(bf16[24,2176]{1,0:T(8,128)(2,1)S(1)} %get-tuple-element.34), channel_id=1, source_target_pairs={{0,3},{1,2},{2,1},{3,0},{4,7},{5,6},{6,5},{7,4},{8,11},{9,10},{10,... | collective-permute-start | bytes 313352 | tf_op jit(solution)/shard_map/ppermute | solution.py:166
  21.6 15.4 %collective-permute-start.12 = (bf16[192,768]{1,0:T(8,128)(2,1)S(1)}, bf16[192,768]{1,0:T(8,128)(2,1)S(1)}, u32[]{:S(2)}, u32[]{:S(2)}) collective-permute-start(bf16[192,768]{1,0:T(8,128)(2,1)S(1)} %bitcast.8), channel_id=1, source_target_pairs={{0,8},{8,0},{16,24},{24,16},{1,9},{9,1},{17,25},{25,17},{2,10},{10... | collective-permute-start | bytes 884744 | tf_op jit(solution)/shard_map/ppermute | solution.py:166
  21.6 15.4 %collective-permute-start.11 = (bf16[192,768]{1,0:T(8,128)(2,1)S(1)}, bf16[192,768]{1,0:T(8,128)(2,1)S(1)}, u32[]{:S(2)}, u32[]{:S(2)}) collective-permute-start(bf16[192,768]{1,0:T(8,128)(2,1)S(1)} %collective-permute-done.10.refs_4_), channel_id=1, source_target_pairs={{0,8},{8,0},{16,24},{24,16},{1,9},{9,1},{17,25},{25,17},{2,10},{10... | collective-permute-start | bytes 884744 | tf_op jit(solution)/shard_map/ppermute | solution.py:166
  27.7 9.2 %collective-permute-start.7 = (bf16[192,512]{1,0:T(8,128)(2,1)S(1)}, bf16[192,512]{1,0:T(8,128)(2,1)S(1)}, u32[]{:S(2)}, u32[]{:S(2)}) collective-permute-start(bf16[192,512]{1,0:T(8,128)(2,1)S(1)} %get-tuple-element.41), channel_id=1, source_target_pairs={{0,16},{8,24},{16,0},{24,8},{1,17},{9,25},{17,1},{25,9},{2,18},{10... | collective-permute-start | bytes 589832 | tf_op jit(solution)/shard_map/ppermute | solution.py:166
  28.3 8.7 %collective-permute-start.8 = (bf16[192,512]{1,0:T(8,128)(2,1)S(1)}, bf16[192,512]{1,0:T(8,128)(2,1)S(1)}, u32[]{:S(2)}, u32[]{:S(2)}) collective-permute-start(bf16[192,512]{1,0:T(8,128)(2,1)S(1)} %get-tuple-element.42), channel_id=1, source_target_pairs={{0,24},{8,16},{16,8},{24,0},{1,25},{9,17},{17,9},{25,1},{2,26},{10... | collective-permute-start | bytes 589832 | tf_op jit(solution)/shard_map/ppermute | solution.py:166
  28.5 8.4 %collective-permute-start.9 = (bf16[192,512]{1,0:T(8,128)(2,1)S(1)}, bf16[192,512]{1,0:T(8,128)(2,1)S(1)}, u32[]{:S(2)}, u32[]{:S(2)}) collective-permute-start(bf16[192,512]{1,0:T(8,128)(2,1)S(1)} %get-tuple-element.43), channel_id=1, source_target_pairs={{0,8},{8,0},{16,24},{24,16},{1,9},{9,1},{17,25},{25,17},{2,10},{10... | collective-permute-start | bytes 589832 | tf_op jit(solution)/shard_map/ppermute | solution.py:166
  29.9 13.7 %copy-start.1 = (s32[128,1]{0,1:T(1,128)S(1)}, s32[128,1]{0,1:T(1,128)}, u32[]{:S(2)}) copy-start(s32[128,1]{0,1:T(1,128)} %param.7) | copy-start | bytes 1540
  31.9 11.7 %all-to-all-start = ((f32[8,8,128]{2,1,0:T(8,128)}), f32[8,8,128]{2,1,0:T(8,128)S(1)}, u32[]{:S(2)}, u32[]{:S(2)}) async-start(f32[8,8,128]{2,1,0:T(8,128)} %get-tuple-element.40), calls=%async_computation | async-start | bytes 65536 | tf_op jit(solution)/shard_map/all_to_all | solution.py:169

commit v3 on v1

--- a/solution.py
+++ b/solution.py
@@ -91,10 +91,9 @@
 
 def weigh_body(replicas, order, *refs):
     n_dp = len(replicas)
-    *chunk_refs, rows_ref, prob_ref = refs[: -n_dp - 1]
-    weighted_refs, all_ref = refs[-n_dp - 1 : -1], refs[-1]
-    width = rows_ref.shape[1]
-    chunk = width // n_dp
+    chunk_refs, weighted_refs, all_ref = refs[: -n_dp - 1], refs[-n_dp - 1 : -1], refs[-1]
+    chunk = weighted_refs[0].shape[1]
+    width = chunk * n_dp
     size = chunk_refs[0].shape[0]
     for c in range(0, width + LANES, LANES):
         columns = slice(c, c + LANES)
@@ -102,13 +101,11 @@
             at = (lax.axis_index("expert") ^ k) * size if order else 0
             all_ref[pl.ds(at, size), columns] = ref[:, columns].astype(F32)
     prob = all_ref[:, width:]
-    prob_ref[...] = prob
     replica = lax.axis_index("dp")
     for k, ref in zip(replicas, weighted_refs):
         for c in range(0, chunk, LANES):
             columns = pl.ds(pl.multiple_of((replica ^ k) * chunk + c, LANES), LANES)
             piece = all_ref[:, columns]
-            rows_ref[:, columns] = piece.astype(BF16)
             ref[:, c : c + LANES] = (piece * prob).astype(BF16)
 
 
@@ -127,12 +124,39 @@
     return dot(owner, spread, precision=lax.Precision.HIGHEST)
 
 
-def act_body(experts, cap, rows_ref, prob_ref, weight_ref, stored_ref, act_ref, table_ref):
-    backed = dot(rows_ref[...], weight_ref[...], ((1,), (1,)))
-    act_ref[...] = (prob_ref[:, 0:1] * backed).astype(BF16)
-    column = jnp.sum(backed * stored_ref[...].astype(F32), axis=1, keepdims=True)
-    table = by_source(column, experts, cap)
-    table_ref[...] = jnp.broadcast_to(table[:, None], table_ref.shape)
+def act_body(order, cap, experts, count, *refs):
+    chunk_refs, (weight_ref, stored_ref), refs = refs[:count], refs[count : count + 2], refs[count + 2 :]
+    *earlier_refs, act_ref, table_ref, stored_all_ref, act_all_ref = refs
+    width, ffw = weight_ref.shape[1], weight_ref.shape[0]
+    rows = jnp.concatenate([ref[:, :width].astype(F32) for ref in chunk_refs], axis=0)
+    prob = jnp.concatenate([ref[:, width:].astype(F32) for ref in chunk_refs], axis=0)
+    backed = dot(rows.astype(BF16), weight_ref[...], ((1,), (1,)))
+    acts = prob[:, 0:1] * backed
+    stored_all_ref[...] = stored_ref[...].astype(F32)
+    table = jnp.zeros((experts, LANES), F32)
+    last = len(earlier_refs) > 0 or not order
+    if order:
+        act_all_ref[...] = earlier_refs[0][...] if last else jnp.zeros_like(act_all_ref)
+        table = earlier_refs[1][...] if last else table
+    size = chunk_refs[0].shape[0]
+    for i, k in enumerate(order or (0,)):
+        source = lax.axis_index("expert") ^ k if order else 0
+        mine = slice(i * size, (i + 1) * size)
+        column = jnp.sum(
+            backed[mine] * stored_all_ref[pl.ds(source * size, size), :], axis=1, keepdims=True
+        )
+        if order:
+            row = by_source(column, 1, cap)
+            table += jnp.where(iota((experts, LANES), 0) == source, row, 0.0)
+        else:
+            table = by_source(column, experts, cap)
+        act_all_ref[pl.ds(source * size, size), :] = acts[mine]
+    if last:
+        act_ref[...] = act_all_ref[...].astype(BF16)
+        table_ref[...] = jnp.broadcast_to(table[:, None], table_ref.shape)
+    else:
+        act_ref[...] = act_all_ref[...]
+        table_ref[...] = table
 
 
 def gradient_body(n_dp, *refs):
@@ -199,24 +223,35 @@
     replicas = [*range(2, n_dp), 1, 0]
     all_stored = [swap(stored, "dp", k) if k else stored for k in replicas]
 
-    rows, prob, *weighted = kernel_call(
+
+    def multiply(part, earlier, last):
+        return kernel_call(
+            functools.partial(act_body, order[part], cap, experts, len(arrived[part])),
+            (shape((slots, ffw), BF16), shape((experts, 8, LANES), F32))
+            if last
+            else (shape((slots, ffw), F32), shape((experts, LANES), F32)),
+            (*arrived[part], weight, saved_act[0, 0], *earlier),
+            flops=2 * slots * width * ffw // 2,
+            name="act",
+            scratch=(pltpu.VMEM((slots, ffw), F32),) * 2,
+        )
+
+    early, late = slice(0, len(order) // 2), slice(len(order) // 2, None)
+    earlier = ()
+    if order:
+        bound = lax.optimization_barrier((*multiply(early, (), False), *arrived[late]))
+        earlier, arrived[late] = bound[:2], bound[2:]
+    weighted = kernel_call(
         functools.partial(weigh_body, replicas, order),
-        (shape((slots, width), BF16), shape((slots, LANES), F32))
-        + (shape((slots, chunk), BF16),) * n_dp,
+        (shape((slots, chunk), BF16),) * n_dp,
         arrived,
         flops=2 * slots * width,
         name="weigh",
         scratch=(pltpu.VMEM((slots, width + LANES), F32),),
     )
     weighted = [swap(rows, "dp", k) if k else rows for k, rows in zip(replicas, weighted)]
-    grad_act, table = kernel_call(
-        functools.partial(act_body, experts, cap),
-        (shape((slots, ffw), BF16), shape((experts, 8, LANES), F32)),
-        (rows, prob, weight, stored),
-        flops=2 * slots * width * ffw,
-        name="act",
-    )
-    reweight = exchange(table)
+    grad_act, table = multiply(late, earlier, True)
+    returned = exchange(table)
     (grad_weight,) = kernel_call(
         functools.partial(gradient_body, n_dp),
         (shape((chunk, ffw), F32),),
@@ -224,11 +259,11 @@
         flops=2 * n_dp * slots * chunk * ffw,
         name="gradient",
     )
-    reweight, grad_weight = lax.optimization_barrier((reweight, grad_weight))
+    returned, grad_weight = lax.optimization_barrier((returned, grad_weight))
     (grad_prob,) = kernel_call(
         functools.partial(pick_body, experts),
         (shape((1, tokens), F32),),
-        (ids, within, reweight),
+        (ids, within, returned),
         name="pick",
     )
     return (grad_act[None, None], grad_weight[None], grad_prob.reshape(tokens, 1))

time: 43.6 us -> 43.5 us (level)
  waiting for transfers between devices: 10.9 us -> 9.61 us
  Pallas kernels: 8.42 us -> 9.51 us
    ppermute x13, waiting for transfers between devices: 7.25 us -> 5.99 us  [swap(): return lax.ppermute(array, axis, [(r, r ^ k) for r in range(size)])]
    pallas_call x6 -> x7, Pallas kernels: 8.42 us -> 9.51 us  [kernel_call(): pl.pallas_call(body, out_shape=outs, in_specs=[hbm if i in stay else vmem...]
  transfers between devices with their start and end apart: 14 -> 14, of which waited for: 5 -> 5; matrix products, arithmetic and copies ran while one was open for 0% -> 0% of each run, Pallas kernels for 15% -> 17%
where the time goes in v3:
time: 43.5 us; the launch traced here: 43.2 us
  starting transfers between devices  23.4 us (54%)
  waiting for transfers between devices  9.61 us (22%)
  Pallas kernels  9.51 us (22%)
  between operations  0.71 us (2%)
    ppermute x13, starting transfers between devices, swap(): return lax.ppermute(array, axis, [(r, r ^ k) for r in range(size)])  19.8 us
    pallas_call x7, Pallas kernels, kernel_call(): pl.pallas_call(body, out_shape=outs, in_specs=[hbm if i in stay else vmem...  9.51 us
    ppermute x13, waiting for transfers between devices, swap(): return lax.ppermute(array, axis, [(r, r ^ k) for r in range(size)])  5.99 us
    all_to_all x1, starting transfers between devices, exchange(): lax.all_to_all(array, 'expert', split_axis=0, concat_axis=0, tiled=True)  3.62 us
    all_to_all x1, waiting for transfers between devices, exchange(): lax.all_to_all(array, 'expert', split_axis=0, concat_axis=0, tiled=True)  3.62 us
  transfers between devices with their start and end apart: 14, of which 5 were waited for; matrix products, arithmetic and copies ran while one was open for 0% of the time, Pallas kernels for 17%

profile of v3, /device:TPU:0, one launch (start us, length us, event | category | flops | bytes accessed | tf_op | source)
XLA Modules:
  0.0 43.2 jit_solution(12585536524134833830)
XLA Ops:
  0.6 1.5 %place.1 = (bf16[24,2176]{1,0:T(8,128)(2,1)S(1)}, bf16[24,2176]{1,0:T(8,128)(2,1)S(1)}, bf16[24,2176]{1,0:T(8,128)(2,1)S(1)}, bf16[24,2176]{1,0:T(8,128)(2,1)S(1...) custom-call(s32[1,128]{1,0:T(1,128)} %bitcast.13, ...), custom_call_target="tpu_custom_call" | custom-call | flops 100663296 | bytes 1361152 | tf_op jit(solution)/shard_map/place/pallas_call | solution.py:24
  2.1 4.1 %collective-permute-start = (bf16[24,2176]{1,0:T(8,128)(2,1)S(1)}, bf16[24,2176]{1,0:T(8,128)(2,1)S(1)}, u32[]{:S(2)}, u32[]{:S(2)}) collective-permute-start(bf16[24,2176]{1,0:T(8,128)(2,1)S(1)} %get-tuple-element.31), channel_id=1, source_target_pairs={{0,4},{1,5},{2,6},{3,7},{4,0},{5,1},{6,2},{7,3},{8,12},{9,13},{10,... | collective-permute-start | bytes 313352 | tf_op jit(solution)/shard_map/ppermute | solution.py:190
  6.2 1.5 %collective-permute-start.10 = (bf16[192,768]{1,0:T(8,128)(2,1)}, bf16[192,768]{1,0:T(8,128)(2,1)S(1)}, u32[]{:S(2)}, u32[]{:S(2)}) collective-permute-start(bf16[192,768]{1,0:T(8,128)(2,1)} %bitcast.7), channel_id=1, source_target_pairs={{0,16},{8,24},{16,0},{24,8},{1,17},{9,25},{17,1},{25,9},{2,18},{10... | collective-permute-start | bytes 884744 | tf_op jit(solution)/shard_map/ppermute | solution.py:190
  7.7 1.5 %collective-permute-start.1 = (bf16[24,2176]{1,0:T(8,128)(2,1)S(1)}, bf16[24,2176]{1,0:T(8,128)(2,1)S(1)}, u32[]{:S(2)}, u32[]{:S(2)}) collective-permute-start(bf16[24,2176]{1,0:T(8,128)(2,1)S(1)} %get-tuple-element.32), channel_id=1, source_target_pairs={{0,1},{1,0},{2,3},{3,2},{4,5},{5,4},{6,7},{7,6},{8,9},{9,8},{10,11... | collective-permute-start | bytes 313352 | tf_op jit(solution)/shard_map/ppermute | solution.py:190
  9.2 0.3 collective-permute-start.2
  9.5 1.6 %collective-permute-start.3 = (bf16[24,2176]{1,0:T(8,128)(2,1)S(1)}, bf16[24,2176]{1,0:T(8,128)(2,1)S(1)}, u32[]{:S(2)}, u32[]{:S(2)}) collective-permute-start(bf16[24,2176]{1,0:T(8,128)(2,1)S(1)} %get-tuple-element.34), channel_id=1, source_target_pairs={{0,2},{1,3},{2,0},{3,1},{4,6},{5,7},{6,4},{7,5},{8,10},{9,11},{10,... | collective-permute-start | bytes 313352 | tf_op jit(solution)/shard_map/ppermute | solution.py:190
  11.1 0.3 collective-permute-done.refs_0_
  11.4 5.9 %collective-permute-start.4 = (bf16[24,2176]{1,0:T(8,128)(2,1)S(1)}, bf16[24,2176]{1,0:T(8,128)(2,1)S(1)}, u32[]{:S(2)}, u32[]{:S(2)}) collective-permute-start(bf16[24,2176]{1,0:T(8,128)(2,1)S(1)} %get-tuple-element.41), channel_id=1, source_target_pairs={{0,6},{1,7},{2,4},{3,5},{4,2},{5,3},{6,0},{7,1},{8,14},{9,15},{10,... | collective-permute-start | bytes 313352 | tf_op jit(solution)/shard_map/ppermute | solution.py:190
  17.3 1.9 %fetch.1.refs_4_ = bf16[768,2048]{1,0:T(8,128)(2,1)S(1)} custom-call(bf16[768,2048]{1,0:T(8,128)(2,1)} %bitcast.15), custom_call_target="tpu_custom_call" | custom-call | flops 603979776 | bytes 6291456 | tf_op jit(solution)/shard_map/fetch/pallas_call | solution.py:24
  19.3 1.0 %collective-permute-start.5 = (bf16[24,2176]{1,0:T(8,128)(2,1)S(1)}, bf16[24,2176]{1,0:T(8,128)(2,1)S(1)}, u32[]{:S(2)}, u32[]{:S(2)}) collective-permute-start(bf16[24,2176]{1,0:T(8,128)(2,1)S(1)} %get-tuple-element.42), channel_id=1, source_target_pairs={{0,7},{1,6},{2,5},{3,4},{4,3},{5,2},{6,1},{7,0},{8,15},{9,14},{10,... | collective-permute-start | bytes 313352 | tf_op jit(solution)/shard_map/ppermute | solution.py:190
  20.3 0.0 collective-permute-done.2.refs_2_
  20.3 0.0 collective-permute-start.6
  20.3 0.0 collective-permute-done.3.refs_3_
  20.3 0.8 %collective-permute-start.11 = (bf16[192,768]{1,0:T(8,128)(2,1)S(1)}, bf16[192,768]{1,0:T(8,128)(2,1)S(1)}, u32[]{:S(2)}, u32[]{:S(2)}) collective-permute-start(bf16[192,768]{1,0:T(8,128)(2,1)S(1)} %bitcast.8), channel_id=1, source_target_pairs={{0,24},{8,16},{16,8},{24,0},{1,25},{9,17},{17,9},{25,1},{2,26},{10... | collective-permute-start | bytes 884744 | tf_op jit(solution)/shard_map/ppermute | solution.py:190
  21.1 0.0 collective-permute-done.4.refs_0_.refs_4_
  21.1 0.9 %collective-permute-start.12 = (bf16[192,768]{1,0:T(8,128)(2,1)S(1)}, bf16[192,768]{1,0:T(8,128)(2,1)S(1)}, u32[]{:S(2)}, u32[]{:S(2)}) collective-permute-start(bf16[192,768]{1,0:T(8,128)(2,1)S(1)} %bitcast.9), channel_id=1, source_target_pairs={{0,8},{8,0},{16,24},{24,16},{1,9},{9,1},{17,25},{25,17},{2,10},{10... | collective-permute-start | bytes 884744 | tf_op jit(solution)/shard_map/ppermute | solution.py:190
  22.0 1.3 %act.2 = (f32[192,768]{1,0:T(8,128)S(1)}, f32[8,128]{1,0:T(8,128)S(1)}) custom-call(bf16[24,2176]{1,0:T(8,128)(2,1)S(1)} %collective-permute-done.refs_0_, bf16[24,2176]{1,0:T(8,128)(2,1)S(1)} %collective-permute-done.1.refs_1_, bf16[24,2176]{1,0:T(8,128)(2,1)S(1)} %collective-permute-done.2.refs_2_, bf16[24,2176]{1,0:T(8,128)(2,1)S(1)} %collective-permute-done.3.refs_3_, ...), custom_call_target="tpu_custom_call" | custom-call | flops 301989888 | bytes 4452352 | tf_op jit(solution)/shard_map/act/pallas_call | solution.py:24
  23.3 4.3 %collective-permute-done.5.refs_1_.refs_5_ = bf16[24,2176]{1,0:T(8,128)(2,1)S(1)} collective-permute-done((bf16[24,2176]{1,0:T(8,128)(2,1)S(1)}, bf16[24,2176]{1,0:T(8,128)(2,1)S(1)}, u32[]{:S(2)}, u32[]{:S(2)}) %collective-permute-start.5) | collective-permute-done | bytes 104480 | tf_op jit(solution)/shard_map/ppermute | solution.py:190
  27.6 0.3 collective-permute-done.6.refs_2_.refs_6_
  27.8 0.3 weigh.1
  28.1 1.6 %collective-permute-start.7 = (bf16[192,512]{1,0:T(8,128)(2,1)S(1)}, bf16[192,512]{1,0:T(8,128)(2,1)S(1)}, u32[]{:S(2)}, u32[]{:S(2)}) collective-permute-start(bf16[192,512]{1,0:T(8,128)(2,1)S(1)} %get-tuple-element.53), channel_id=1, source_target_pairs={{0,16},{8,24},{16,0},{24,8},{1,17},{9,25},{17,1},{25,9},{2,18},{10... | collective-permute-start | bytes 589832 | tf_op jit(solution)/shard_map/ppermute | solution.py:190
  29.7 0.0 collective-permute-start.8
  29.7 0.0 collective-permute-done.10.refs_4_
  29.7 0.6 %collective-permute-start.9 = (bf16[192,512]{1,0:T(8,128)(2,1)S(1)}, bf16[192,512]{1,0:T(8,128)(2,1)S(1)}, u32[]{:S(2)}, u32[]{:S(2)}) collective-permute-start(bf16[192,512]{1,0:T(8,128)(2,1)S(1)} %get-tuple-element.55), channel_id=1, source_target_pairs={{0,8},{8,0},{16,24},{24,16},{1,9},{9,1},{17,25},{25,17},{2,10},{10... | collective-permute-start | bytes 589832 | tf_op jit(solution)/shard_map/ppermute | solution.py:190
  30.3 2.0 %act.3 = (bf16[192,768]{1,0:T(8,128)(2,1)}, f32[8,8,128]{2,1,0:T(8,128)}) custom-call(bf16[24,2176]{1,0:T(8,128)(2,1)S(1)} %collective-permute-done.4.refs_0_.refs_4_, bf16[24,2176]{1,0:T(8,128)(2,1)S(1)} %collective-permute-done.5.refs_1_.refs_5_, bf16[24,2176]{1,0:T(8,128)(2,1)S(1)} %collective-permute-done.6.refs_2_.refs_6_, ...), custom_call_target="tpu_custom_call" | custom-call | flops 301989888 | bytes 4780032 | tf_op jit(solution)/shard_map/act/pallas_call | solution.py:24
  32.3 3.6 %all-to-all-start = ((f32[8,8,128]{2,1,0:T(8,128)}), f32[8,8,128]{2,1,0:T(8,128)S(1)}, u32[]{:S(2)}, u32[]{:S(2)}) async-start(f32[8,8,128]{2,1,0:T(8,128)} %get-tuple-element.52), calls=%async_computation | async-start | bytes 65536 | tf_op jit(solution)/shard_map/all_to_all | solution.py:193
  35.9 0.0 collective-permute-done.12.refs_6_
  36.0 1.1 %collective-permute-done.8.refs_1_ = bf16[192,512]{1,0:T(8,128)(2,1)S(1)} collective-permute-done((bf16[192,512]{1,0:T(8,128)(2,1)S(1)}, bf16[192,512]{1,0:T(8,128)(2,1)S(1)}, u32[]{:S(2)}, u32[]{:S(2)}) %collective-permute-start.8) | collective-permute-done | bytes 196640 | tf_op jit(solution)/shard_map/ppermute | solution.py:190
  37.0 0.0 collective-permute-done.9.refs_2_
  37.0 2.0 %gradient.1 = f32[512,768]{1,0:T(8,128)} custom-call(bf16[192,512]{1,0:T(8,128)(2,1)S(1)} %collective-permute-done.7.refs_0_, bf16[192,512]{1,0:T(8,128)(2,1)S(1)} %collective-permute-done.8.refs_1_, bf16[192,512]{1,0:T(8,128)(2,1)S(1)} %collective-permute-done.9.refs_2_, bf16[192,512]{1,0:T(8,128)(2,1)S(1)} %get-tuple-element.56.refs_3_, ...), custom_call_target="tpu_custom_call" | custom-call | flops 603979776 | bytes 3538944 | tf_op jit(solution)/shard_map/gradient/pallas_call | solution.py:24
  39.0 3.6 %all-to-all-done.table_ref = f32[8,8,128]{2,1,0:T(8,128)S(1)} async-done(((f32[8,8,128]{2,1,0:T(8,128)}), f32[8,8,128]{2,1,0:T(8,128)S(1)}, u32[]{:S(2)}, u32[]{:S(2)}) %all-to-all-start) | async-done | bytes 32800 | tf_op jit(solution)/shard_map/all_to_all | solution.py:193
  42.6 0.6 %pick.1 = f32[1,128]{1,0:T(1,128)} custom-call(s32[1,128]{1,0:T(1,128)S(1)} %bitcast.14, s32[1,128]{1,0:T(1,128)S(1)} %get-tuple-element.36.within_ref, f32[8,8,128]{2,1,0:T(8,128)S(1)} %all-to-all-done.table_ref), custom_call_target="tpu_custom_call" | custom-call | bytes 34304 | tf_op jit(solution)/shard_map/pick/pallas_call | solution.py:24
  (7 shorter events, 0.0 us)
Async XLA Ops:
  2.1 9.3 %collective-permute-start = (bf16[24,2176]{1,0:T(8,128)(2,1)S(1)}, bf16[24,2176]{1,0:T(8,128)(2,1)S(1)}, u32[]{:S(2)}, u32[]{:S(2)}) collective-permute-start(bf16[24,2176]{1,0:T(8,128)(2,1)S(1)} %get-tuple-element.31), channel_id=1, source_target_pairs={{0,4},{1,5},{2,6},{3,7},{4,0},{5,1},{6,2},{7,3},{8,12},{9,13},{10,... | collective-permute-start | bytes 313352 | tf_op jit(solution)/shard_map/ppermute | solution.py:190
  6.2 23.5 %collective-permute-start.10 = (bf16[192,768]{1,0:T(8,128)(2,1)}, bf16[192,768]{1,0:T(8,128)(2,1)S(1)}, u32[]{:S(2)}, u32[]{:S(2)}) collective-permute-start(bf16[192,768]{1,0:T(8,128)(2,1)} %bitcast.7), channel_id=1, source_target_pairs={{0,16},{8,24},{16,0},{24,8},{1,17},{9,25},{17,1},{25,9},{2,18},{10... | collective-permute-start | bytes 884744 | tf_op jit(solution)/shard_map/ppermute | solution.py:190
  7.7 11.5 %collective-permute-start.1 = (bf16[24,2176]{1,0:T(8,128)(2,1)S(1)}, bf16[24,2176]{1,0:T(8,128)(2,1)S(1)}, u32[]{:S(2)}, u32[]{:S(2)}) collective-permute-start(bf16[24,2176]{1,0:T(8,128)(2,1)S(1)} %get-tuple-element.32), channel_id=1, source_target_pairs={{0,1},{1,0},{2,3},{3,2},{4,5},{5,4},{6,7},{7,6},{8,9},{9,8},{10,11... | collective-permute-start | bytes 313352 | tf_op jit(solution)/shard_map/ppermute | solution.py:190
  9.2 11.0 %collective-permute-start.2 = (bf16[24,2176]{1,0:T(8,128)(2,1)S(1)}, bf16[24,2176]{1,0:T(8,128)(2,1)S(1)}, u32[]{:S(2)}, u32[]{:S(2)}) collective-permute-start(bf16[24,2176]{1,0:T(8,128)(2,1)S(1)} %get-tuple-element.33), channel_id=1, source_target_pairs={{0,5},{1,4},{2,7},{3,6},{4,1},{5,0},{6,3},{7,2},{8,13},{9,12},{10,... | collective-permute-start | bytes 313352 | tf_op jit(solution)/shard_map/ppermute | solution.py:190
  9.5 10.7 %collective-permute-start.3 = (bf16[24,2176]{1,0:T(8,128)(2,1)S(1)}, bf16[24,2176]{1,0:T(8,128)(2,1)S(1)}, u32[]{:S(2)}, u32[]{:S(2)}) collective-permute-start(bf16[24,2176]{1,0:T(8,128)(2,1)S(1)} %get-tuple-element.34), channel_id=1, source_target_pairs={{0,2},{1,3},{2,0},{3,1},{4,6},{5,7},{6,4},{7,5},{8,10},{9,11},{10,... | collective-permute-start | bytes 313352 | tf_op jit(solution)/shard_map/ppermute | solution.py:190
  11.4 9.6 %collective-permute-start.4 = (bf16[24,2176]{1,0:T(8,128)(2,1)S(1)}, bf16[24,2176]{1,0:T(8,128)(2,1)S(1)}, u32[]{:S(2)}, u32[]{:S(2)}) collective-permute-start(bf16[24,2176]{1,0:T(8,128)(2,1)S(1)} %get-tuple-element.41), channel_id=1, source_target_pairs={{0,6},{1,7},{2,4},{3,5},{4,2},{5,3},{6,0},{7,1},{8,14},{9,15},{10,... | collective-permute-start | bytes 313352 | tf_op jit(solution)/shard_map/ppermute | solution.py:190
  17.3 3.0 %copy-start = (bf16[1,1,192,768]{3,2,1,0:T(8,128)(2,1)S(1)}, bf16[1,1,192,768]{3,2,1,0:T(8,128)(2,1)}, u32[]{:S(2)}) copy-start(bf16[1,1,192,768]{3,2,1,0:T(8,128)(2,1)} %param.8) | copy-start | bytes 884740
  19.3 8.3 %collective-permute-start.5 = (bf16[24,2176]{1,0:T(8,128)(2,1)S(1)}, bf16[24,2176]{1,0:T(8,128)(2,1)S(1)}, u32[]{:S(2)}, u32[]{:S(2)}) collective-permute-start(bf16[24,2176]{1,0:T(8,128)(2,1)S(1)} %get-tuple-element.42), channel_id=1, source_target_pairs={{0,7},{1,6},{2,5},{3,4},{4,3},{5,2},{6,1},{7,0},{8,15},{9,14},{10,... | collective-permute-start | bytes 313352 | tf_op jit(solution)/shard_map/ppermute | solution.py:190
  20.3 7.6 %collective-permute-start.6 = (bf16[24,2176]{1,0:T(8,128)(2,1)S(1)}, bf16[24,2176]{1,0:T(8,128)(2,1)S(1)}, u32[]{:S(2)}, u32[]{:S(2)}) collective-permute-start(bf16[24,2176]{1,0:T(8,128)(2,1)S(1)} %get-tuple-element.43), channel_id=1, source_target_pairs={{0,3},{1,2},{2,1},{3,0},{4,7},{5,6},{6,5},{7,4},{8,11},{9,10},{10,... | collective-permute-start | bytes 313352 | tf_op jit(solution)/shard_map/ppermute | solution.py:190
  20.3 15.7 %collective-permute-start.11 = (bf16[192,768]{1,0:T(8,128)(2,1)S(1)}, bf16[192,768]{1,0:T(8,128)(2,1)S(1)}, u32[]{:S(2)}, u32[]{:S(2)}) collective-permute-start(bf16[192,768]{1,0:T(8,128)(2,1)S(1)} %bitcast.8), channel_id=1, source_target_pairs={{0,24},{8,16},{16,8},{24,0},{1,25},{9,17},{17,9},{25,1},{2,26},{10... | collective-permute-start | bytes 884744 | tf_op jit(solution)/shard_map/ppermute | solution.py:190
  21.1 14.9 %collective-permute-start.12 = (bf16[192,768]{1,0:T(8,128)(2,1)S(1)}, bf16[192,768]{1,0:T(8,128)(2,1)S(1)}, u32[]{:S(2)}, u32[]{:S(2)}) collective-permute-start(bf16[192,768]{1,0:T(8,128)(2,1)S(1)} %bitcast.9), channel_id=1, source_target_pairs={{0,8},{8,0},{16,24},{24,16},{1,9},{9,1},{17,25},{25,17},{2,10},{10... | collective-permute-start | bytes 884744 | tf_op jit(solution)/shard_map/ppermute | solution.py:190
  28.1 7.8 %collective-permute-start.7 = (bf16[192,512]{1,0:T(8,128)(2,1)S(1)}, bf16[192,512]{1,0:T(8,128)(2,1)S(1)}, u32[]{:S(2)}, u32[]{:S(2)}) collective-permute-start(bf16[192,512]{1,0:T(8,128)(2,1)S(1)} %get-tuple-element.53), channel_id=1, source_target_pairs={{0,16},{8,24},{16,0},{24,8},{1,17},{9,25},{17,1},{25,9},{2,18},{10... | collective-permute-start | bytes 589832 | tf_op jit(solution)/shard_map/ppermute | solution.py:190
  29.7 7.3 %collective-permute-start.8 = (bf16[192,512]{1,0:T(8,128)(2,1)S(1)}, bf16[192,512]{1,0:T(8,128)(2,1)S(1)}, u32[]{:S(2)}, u32[]{:S(2)}) collective-permute-start(bf16[192,512]{1,0:T(8,128)(2,1)S(1)} %get-tuple-element.54), channel_id=1, source_target_pairs={{0,24},{8,16},{16,8},{24,0},{1,25},{9,17},{17,9},{25,1},{2,26},{10... | collective-permute-start | bytes 589832 | tf_op jit(solution)/shard_map/ppermute | solution.py:190
  29.7 12.9 %copy-start.1 = (s32[128,1]{0,1:T(1,128)S(1)}, s32[128,1]{0,1:T(1,128)}, u32[]{:S(2)}) copy-start(s32[128,1]{0,1:T(1,128)} %param.7) | copy-start | bytes 1540
  29.7 7.3 %collective-permute-start.9 = (bf16[192,512]{1,0:T(8,128)(2,1)S(1)}, bf16[192,512]{1,0:T(8,128)(2,1)S(1)}, u32[]{:S(2)}, u32[]{:S(2)}) collective-permute-start(bf16[192,512]{1,0:T(8,128)(2,1)S(1)} %get-tuple-element.55), channel_id=1, source_target_pairs={{0,8},{8,0},{16,24},{24,16},{1,9},{9,1},{17,25},{25,17},{2,10},{10... | collective-permute-start | bytes 589832 | tf_op jit(solution)/shard_map/ppermute | solution.py:190
  32.3 10.3 %all-to-all-start = ((f32[8,8,128]{2,1,0:T(8,128)}), f32[8,8,128]{2,1,0:T(8,128)S(1)}, u32[]{:S(2)}, u32[]{:S(2)}) async-start(f32[8,8,128]{2,1,0:T(8,128)} %get-tuple-element.52), calls=%async_computation | async-start | bytes 65536 | tf_op jit(solution)/shard_map/all_to_all | solution.py:193

commit v4 on v3

--- a/solution.py
+++ b/solution.py
@@ -10,8 +10,7 @@
 LANES = 128
 F32 = jnp.float32
 BF16 = jnp.bfloat16
-ORDER = (4, 1, 5, 2, 6, 7, 3, 0)
-LATE = 6
+ORDER = (6, 1, 7, 2, 4, 5, 3, 0)
 
 
 def kernel_call(body, outs, operands, name, flops=0, scratch=(), stay=()):
@@ -206,6 +205,10 @@
             pltpu.SemaphoreType.DMA((3,)),
         ),
     )
+    if order:
+        arrived = [swap(rows, "expert", k) if k else rows for k, rows in zip(order, packed)]
+    else:
+        arrived = [exchange(packed[0])]
     (weight,) = kernel_call(
         fetch_body,
         (shape((ffw, width), BF16),),
@@ -215,11 +218,6 @@
         stay=(0,),
         scratch=(pltpu.SemaphoreType.DMA(()),),
     )
-    if order:
-        packed[LATE], weight = lax.optimization_barrier((packed[LATE], weight))
-        arrived = [swap(rows, "expert", k) if k else rows for k, rows in zip(order, packed)]
-    else:
-        arrived = [exchange(packed[0])]
     replicas = [*range(2, n_dp), 1, 0]
     all_stored = [swap(stored, "dp", k) if k else stored for k in replicas]
 

time: 43.5 us -> 43.3 us (level)
  starting transfers between devices: 23.4 us -> 19.8 us
  waiting for transfers between devices: 9.61 us -> 13 us
    ppermute x13, waiting for transfers between devices: 5.99 us -> 11.2 us  [swap(): return lax.ppermute(array, axis, [(r, r ^ k) for r in range(size)])]
    ppermute x13, starting transfers between devices: 19.8 us -> 15.7 us  [swap(): return lax.ppermute(array, axis, [(r, r ^ k) for r in range(size)])]
    all_to_all x1, waiting for transfers between devices: 3.62 us -> 1.79 us  [exchange(): lax.all_to_all(array, 'expert', split_axis=0, concat_axis=0, tiled=True)]
    all_to_all x1, starting transfers between devices: 3.62 us -> 4.11 us  [exchange(): lax.all_to_all(array, 'expert', split_axis=0, concat_axis=0, tiled=True)]
  transfers between devices with their start and end apart: 14 -> 14, of which waited for: 5 -> 4; matrix products, arithmetic and copies ran while one was open for 0% -> 0% of each run, Pallas kernels for 17% -> 17%
where the time goes in v4:
time: 43.3 us; the launch traced here: 43 us
  starting transfers between devices  19.8 us (46%)
  waiting for transfers between devices  13 us (30%)
  Pallas kernels  9.52 us (22%)
  between operations  0.72 us (2%)
    ppermute x13, starting transfers between devices, swap(): return lax.ppermute(array, axis, [(r, r ^ k) for r in range(size)])  15.7 us
    ppermute x13, waiting for transfers between devices, swap(): return lax.ppermute(array, axis, [(r, r ^ k) for r in range(size)])  11.2 us
    pallas_call x7, Pallas kernels, kernel_call(): pl.pallas_call(body, out_shape=outs, in_specs=[hbm if i in stay else vmem...  9.52 us
    all_to_all x1, starting transfers between devices, exchange(): lax.all_to_all(array, 'expert', split_axis=0, concat_axis=0, tiled=True)  4.11 us
    all_to_all x1, waiting for transfers between devices, exchange(): lax.all_to_all(array, 'expert', split_axis=0, concat_axis=0, tiled=True)  1.79 us
  transfers between devices with their start and end apart: 14, of which 4 were waited for; matrix products, arithmetic and copies ran while one was open for 0% of the time, Pallas kernels for 17%

profile of v4, /device:TPU:0, one launch (start us, length us, event | category | flops | bytes accessed | tf_op | source)
XLA Modules:
  0.0 43.0 jit_solution(16640352548040348024)
XLA Ops:
  0.6 1.5 %place.1 = (bf16[24,2176]{1,0:T(8,128)(2,1)S(1)}, bf16[24,2176]{1,0:T(8,128)(2,1)S(1)}, bf16[24,2176]{1,0:T(8,128)(2,1)S(1)}, bf16[24,2176]{1,0:T(8,128)(2,1)S(1...) custom-call(s32[1,128]{1,0:T(1,128)} %bitcast.13, ...), custom_call_target="tpu_custom_call" | custom-call | flops 100663296 | bytes 1361152 | tf_op jit(solution)/shard_map/place/pallas_call | solution.py:23
  2.1 5.1 %collective-permute-start = (bf16[24,2176]{1,0:T(8,128)(2,1)S(1)}, bf16[24,2176]{1,0:T(8,128)(2,1)S(1)}, u32[]{:S(2)}, u32[]{:S(2)}) collective-permute-start(bf16[24,2176]{1,0:T(8,128)(2,1)S(1)} %get-tuple-element.29), channel_id=1, source_target_pairs={{0,6},{1,7},{2,4},{3,5},{4,2},{5,3},{6,0},{7,1},{8,14},{9,15},{10,... | collective-permute-start | bytes 313352 | tf_op jit(solution)/shard_map/ppermute | solution.py:189
  7.2 1.5 %collective-permute-start.10 = (bf16[192,768]{1,0:T(8,128)(2,1)}, bf16[192,768]{1,0:T(8,128)(2,1)S(1)}, u32[]{:S(2)}, u32[]{:S(2)}) collective-permute-start(bf16[192,768]{1,0:T(8,128)(2,1)} %bitcast.7), channel_id=1, source_target_pairs={{0,16},{8,24},{16,0},{24,8},{1,17},{9,25},{17,1},{25,9},{2,18},{10... | collective-permute-start | bytes 884744 | tf_op jit(solution)/shard_map/ppermute | solution.py:189
  8.7 1.5 %collective-permute-start.1 = (bf16[24,2176]{1,0:T(8,128)(2,1)S(1)}, bf16[24,2176]{1,0:T(8,128)(2,1)S(1)}, u32[]{:S(2)}, u32[]{:S(2)}) collective-permute-start(bf16[24,2176]{1,0:T(8,128)(2,1)S(1)} %get-tuple-element.30), channel_id=1, source_target_pairs={{0,1},{1,0},{2,3},{3,2},{4,5},{5,4},{6,7},{7,6},{8,9},{9,8},{10,11... | collective-permute-start | bytes 313352 | tf_op jit(solution)/shard_map/ppermute | solution.py:189
  10.2 0.2 collective-permute-start.2
  10.4 0.0 collective-permute-start.3
  10.4 0.0 collective-permute-done.refs_0_
  10.4 4.2 %collective-permute-start.4 = (bf16[24,2176]{1,0:T(8,128)(2,1)S(1)}, bf16[24,2176]{1,0:T(8,128)(2,1)S(1)}, u32[]{:S(2)}, u32[]{:S(2)}) collective-permute-start(bf16[24,2176]{1,0:T(8,128)(2,1)S(1)} %get-tuple-element.37), channel_id=1, source_target_pairs={{0,4},{1,5},{2,6},{3,7},{4,0},{5,1},{6,2},{7,3},{8,12},{9,13},{10,... | collective-permute-start | bytes 313352 | tf_op jit(solution)/shard_map/ppermute | solution.py:189
  14.6 0.0 collective-permute-done.1.refs_1_
  14.6 1.0 %collective-permute-start.5 = (bf16[24,2176]{1,0:T(8,128)(2,1)S(1)}, bf16[24,2176]{1,0:T(8,128)(2,1)S(1)}, u32[]{:S(2)}, u32[]{:S(2)}) collective-permute-start(bf16[24,2176]{1,0:T(8,128)(2,1)S(1)} %get-tuple-element.38), channel_id=1, source_target_pairs={{0,5},{1,4},{2,7},{3,6},{4,1},{5,0},{6,3},{7,2},{8,13},{9,12},{10,... | collective-permute-start | bytes 313352 | tf_op jit(solution)/shard_map/ppermute | solution.py:189
  15.6 3.3 %collective-permute-done.2.refs_2_ = bf16[24,2176]{1,0:T(8,128)(2,1)S(1)} collective-permute-done((bf16[24,2176]{1,0:T(8,128)(2,1)S(1)}, bf16[24,2176]{1,0:T(8,128)(2,1)S(1)}, u32[]{:S(2)}, u32[]{:S(2)}) %collective-permute-start.2) | collective-permute-done | bytes 104480 | tf_op jit(solution)/shard_map/ppermute | solution.py:189
  18.9 0.0 collective-permute-start.6
  18.9 0.0 collective-permute-done.3.refs_3_
  18.9 0.0 collective-permute-start.11
  18.9 5.0 %collective-permute-done.4.refs_0_.refs_4_ = bf16[24,2176]{1,0:T(8,128)(2,1)S(1)} collective-permute-done((bf16[24,2176]{1,0:T(8,128)(2,1)S(1)}, bf16[24,2176]{1,0:T(8,128)(2,1)S(1)}, u32[]{:S(2)}, u32[]{:S(2)}) %collective-permute-start.4) | collective-permute-done | bytes 104480 | tf_op jit(solution)/shard_map/ppermute | solution.py:189
  23.9 0.0 collective-permute-start.12
  23.9 1.9 %fetch.1.refs_4_ = bf16[768,2048]{1,0:T(8,128)(2,1)S(1)} custom-call(bf16[768,2048]{1,0:T(8,128)(2,1)} %bitcast.15), custom_call_target="tpu_custom_call" | custom-call | flops 603979776 | bytes 6291456 | tf_op jit(solution)/shard_map/fetch/pallas_call | solution.py:23
  25.9 1.3 %act.2 = (f32[192,768]{1,0:T(8,128)S(1)}, f32[8,128]{1,0:T(8,128)S(1)}) custom-call(bf16[24,2176]{1,0:T(8,128)(2,1)S(1)} %collective-permute-done.refs_0_, bf16[24,2176]{1,0:T(8,128)(2,1)S(1)} %collective-permute-done.1.refs_1_, bf16[24,2176]{1,0:T(8,128)(2,1)S(1)} %collective-permute-done.2.refs_2_, bf16[24,2176]{1,0:T(8,128)(2,1)S(1)} %collective-permute-done.3.refs_3_, ...), custom_call_target="tpu_custom_call" | custom-call | flops 301989888 | bytes 4452352 | tf_op jit(solution)/shard_map/act/pallas_call | solution.py:23
  27.1 0.0 collective-permute-done.5.refs_1_.refs_5_
  27.1 0.0 collective-permute-done.6.refs_2_.refs_6_
  27.1 0.3 weigh.1
  27.4 1.5 %collective-permute-start.7 = (bf16[192,512]{1,0:T(8,128)(2,1)S(1)}, bf16[192,512]{1,0:T(8,128)(2,1)S(1)}, u32[]{:S(2)}, u32[]{:S(2)}) collective-permute-start(bf16[192,512]{1,0:T(8,128)(2,1)S(1)} %get-tuple-element.49), channel_id=1, source_target_pairs={{0,16},{8,24},{16,0},{24,8},{1,17},{9,25},{17,1},{25,9},{2,18},{10... | collective-permute-start | bytes 589832 | tf_op jit(solution)/shard_map/ppermute | solution.py:189
  28.9 0.4 %collective-permute-start.8 = (bf16[192,512]{1,0:T(8,128)(2,1)S(1)}, bf16[192,512]{1,0:T(8,128)(2,1)S(1)}, u32[]{:S(2)}, u32[]{:S(2)}) collective-permute-start(bf16[192,512]{1,0:T(8,128)(2,1)S(1)} %get-tuple-element.50), channel_id=1, source_target_pairs={{0,24},{8,16},{16,8},{24,0},{1,25},{9,17},{17,9},{25,1},{2,26},{10... | collective-permute-start | bytes 589832 | tf_op jit(solution)/shard_map/ppermute | solution.py:189
  29.4 0.3 collective-permute-start.9
  29.7 2.0 %act.3 = (bf16[192,768]{1,0:T(8,128)(2,1)}, f32[8,8,128]{2,1,0:T(8,128)}) custom-call(bf16[24,2176]{1,0:T(8,128)(2,1)S(1)} %collective-permute-done.4.refs_0_.refs_4_, bf16[24,2176]{1,0:T(8,128)(2,1)S(1)} %collective-permute-done.5.refs_1_.refs_5_, bf16[24,2176]{1,0:T(8,128)(2,1)S(1)} %collective-permute-done.6.refs_2_.refs_6_, ...), custom_call_target="tpu_custom_call" | custom-call | flops 301989888 | bytes 4780032 | tf_op jit(solution)/shard_map/act/pallas_call | solution.py:23
  31.6 4.1 %all-to-all-start = ((f32[8,8,128]{2,1,0:T(8,128)}), f32[8,8,128]{2,1,0:T(8,128)S(1)}, u32[]{:S(2)}, u32[]{:S(2)}) async-start(f32[8,8,128]{2,1,0:T(8,128)} %get-tuple-element.48), calls=%async_computation | async-start | bytes 65536 | tf_op jit(solution)/shard_map/all_to_all | solution.py:192
  35.8 0.0 collective-permute-done.12.refs_6_
  35.8 2.9 %collective-permute-done.8.refs_1_ = bf16[192,512]{1,0:T(8,128)(2,1)S(1)} collective-permute-done((bf16[192,512]{1,0:T(8,128)(2,1)S(1)}, bf16[192,512]{1,0:T(8,128)(2,1)S(1)}, u32[]{:S(2)}, u32[]{:S(2)}) %collective-permute-start.8) | collective-permute-done | bytes 196640 | tf_op jit(solution)/shard_map/ppermute | solution.py:189
  38.7 0.0 collective-permute-done.9.refs_2_
  38.7 2.0 %gradient.1 = f32[512,768]{1,0:T(8,128)} custom-call(bf16[192,512]{1,0:T(8,128)(2,1)S(1)} %collective-permute-done.7.refs_0_, bf16[192,512]{1,0:T(8,128)(2,1)S(1)} %collective-permute-done.8.refs_1_, bf16[192,512]{1,0:T(8,128)(2,1)S(1)} %collective-permute-done.9.refs_2_, bf16[192,512]{1,0:T(8,128)(2,1)S(1)} %get-tuple-element.52.refs_3_, ...), custom_call_target="tpu_custom_call" | custom-call | flops 603979776 | bytes 3538944 | tf_op jit(solution)/shard_map/gradient/pallas_call | solution.py:23
  40.6 1.8 %all-to-all-done.table_ref = f32[8,8,128]{2,1,0:T(8,128)S(1)} async-done(((f32[8,8,128]{2,1,0:T(8,128)}), f32[8,8,128]{2,1,0:T(8,128)S(1)}, u32[]{:S(2)}, u32[]{:S(2)}) %all-to-all-start) | async-done | bytes 32800 | tf_op jit(solution)/shard_map/all_to_all | solution.py:192
  42.4 0.6 %pick.1 = f32[1,128]{1,0:T(1,128)} custom-call(s32[1,128]{1,0:T(1,128)S(1)} %bitcast.14, s32[1,128]{1,0:T(1,128)S(1)} %get-tuple-element.33.within_ref, f32[8,8,128]{2,1,0:T(8,128)S(1)} %all-to-all-done.table_ref), custom_call_target="tpu_custom_call" | custom-call | bytes 34304 | tf_op jit(solution)/shard_map/pick/pallas_call | solution.py:23
  (7 shorter events, 0.0 us)
Async XLA Ops:
  2.1 8.3 %collective-permute-start = (bf16[24,2176]{1,0:T(8,128)(2,1)S(1)}, bf16[24,2176]{1,0:T(8,128)(2,1)S(1)}, u32[]{:S(2)}, u32[]{:S(2)}) collective-permute-start(bf16[24,2176]{1,0:T(8,128)(2,1)S(1)} %get-tuple-element.29), channel_id=1, source_target_pairs={{0,6},{1,7},{2,4},{3,5},{4,2},{5,3},{6,0},{7,1},{8,14},{9,15},{10,... | collective-permute-start | bytes 313352 | tf_op jit(solution)/shard_map/ppermute | solution.py:189
  7.2 22.2 %collective-permute-start.10 = (bf16[192,768]{1,0:T(8,128)(2,1)}, bf16[192,768]{1,0:T(8,128)(2,1)S(1)}, u32[]{:S(2)}, u32[]{:S(2)}) collective-permute-start(bf16[192,768]{1,0:T(8,128)(2,1)} %bitcast.7), channel_id=1, source_target_pairs={{0,16},{8,24},{16,0},{24,8},{1,17},{9,25},{17,1},{25,9},{2,18},{10... | collective-permute-start | bytes 884744 | tf_op jit(solution)/shard_map/ppermute | solution.py:189
  8.7 5.9 %collective-permute-start.1 = (bf16[24,2176]{1,0:T(8,128)(2,1)S(1)}, bf16[24,2176]{1,0:T(8,128)(2,1)S(1)}, u32[]{:S(2)}, u32[]{:S(2)}) collective-permute-start(bf16[24,2176]{1,0:T(8,128)(2,1)S(1)} %get-tuple-element.30), channel_id=1, source_target_pairs={{0,1},{1,0},{2,3},{3,2},{4,5},{5,4},{6,7},{7,6},{8,9},{9,8},{10,11... | collective-permute-start | bytes 313352 | tf_op jit(solution)/shard_map/ppermute | solution.py:189
  10.2 8.7 %collective-permute-start.2 = (bf16[24,2176]{1,0:T(8,128)(2,1)S(1)}, bf16[24,2176]{1,0:T(8,128)(2,1)S(1)}, u32[]{:S(2)}, u32[]{:S(2)}) collective-permute-start(bf16[24,2176]{1,0:T(8,128)(2,1)S(1)} %get-tuple-element.31), channel_id=1, source_target_pairs={{0,7},{1,6},{2,5},{3,4},{4,3},{5,2},{6,1},{7,0},{8,15},{9,14},{10,... | collective-permute-start | bytes 313352 | tf_op jit(solution)/shard_map/ppermute | solution.py:189
  10.4 8.5 %collective-permute-start.3 = (bf16[24,2176]{1,0:T(8,128)(2,1)S(1)}, bf16[24,2176]{1,0:T(8,128)(2,1)S(1)}, u32[]{:S(2)}, u32[]{:S(2)}) collective-permute-start(bf16[24,2176]{1,0:T(8,128)(2,1)S(1)} %get-tuple-element.32), channel_id=1, source_target_pairs={{0,2},{1,3},{2,0},{3,1},{4,6},{5,7},{6,4},{7,5},{8,10},{9,11},{10,... | collective-permute-start | bytes 313352 | tf_op jit(solution)/shard_map/ppermute | solution.py:189
  10.4 13.4 %collective-permute-start.4 = (bf16[24,2176]{1,0:T(8,128)(2,1)S(1)}, bf16[24,2176]{1,0:T(8,128)(2,1)S(1)}, u32[]{:S(2)}, u32[]{:S(2)}) collective-permute-start(bf16[24,2176]{1,0:T(8,128)(2,1)S(1)} %get-tuple-element.37), channel_id=1, source_target_pairs={{0,4},{1,5},{2,6},{3,7},{4,0},{5,1},{6,2},{7,3},{8,12},{9,13},{10,... | collective-permute-start | bytes 313352 | tf_op jit(solution)/shard_map/ppermute | solution.py:189
  14.6 12.5 %collective-permute-start.5 = (bf16[24,2176]{1,0:T(8,128)(2,1)S(1)}, bf16[24,2176]{1,0:T(8,128)(2,1)S(1)}, u32[]{:S(2)}, u32[]{:S(2)}) collective-permute-start(bf16[24,2176]{1,0:T(8,128)(2,1)S(1)} %get-tuple-element.38), channel_id=1, source_target_pairs={{0,5},{1,4},{2,7},{3,6},{4,1},{5,0},{6,3},{7,2},{8,13},{9,12},{10,... | collective-permute-start | bytes 313352 | tf_op jit(solution)/shard_map/ppermute | solution.py:189
  18.9 8.2 %collective-permute-start.6 = (bf16[24,2176]{1,0:T(8,128)(2,1)S(1)}, bf16[24,2176]{1,0:T(8,128)(2,1)S(1)}, u32[]{:S(2)}, u32[]{:S(2)}) collective-permute-start(bf16[24,2176]{1,0:T(8,128)(2,1)S(1)} %get-tuple-element.39), channel_id=1, source_target_pairs={{0,3},{1,2},{2,1},{3,0},{4,7},{5,6},{6,5},{7,4},{8,11},{9,10},{10,... | collective-permute-start | bytes 313352 | tf_op jit(solution)/shard_map/ppermute | solution.py:189
  18.9 16.8 %collective-permute-start.11 = (bf16[192,768]{1,0:T(8,128)(2,1)}, bf16[192,768]{1,0:T(8,128)(2,1)S(1)}, u32[]{:S(2)}, u32[]{:S(2)}) collective-permute-start(bf16[192,768]{1,0:T(8,128)(2,1)} %bitcast.8), channel_id=1, source_target_pairs={{0,24},{8,16},{16,8},{24,0},{1,25},{9,17},{17,9},{25,1},{2,26},{10... | collective-permute-start | bytes 884744 | tf_op jit(solution)/shard_map/ppermute | solution.py:189
  23.9 11.9 %collective-permute-start.12 = (bf16[192,768]{1,0:T(8,128)(2,1)}, bf16[192,768]{1,0:T(8,128)(2,1)S(1)}, u32[]{:S(2)}, u32[]{:S(2)}) collective-permute-start(bf16[192,768]{1,0:T(8,128)(2,1)} %bitcast.9), channel_id=1, source_target_pairs={{0,8},{8,0},{16,24},{24,16},{1,9},{9,1},{17,25},{25,17},{2,10},{10... | collective-permute-start | bytes 884744 | tf_op jit(solution)/shard_map/ppermute | solution.py:189
  23.9 2.0 %copy-start = (bf16[1,1,192,768]{3,2,1,0:T(8,128)(2,1)S(1)}, bf16[1,1,192,768]{3,2,1,0:T(8,128)(2,1)}, u32[]{:S(2)}) copy-start(bf16[1,1,192,768]{3,2,1,0:T(8,128)(2,1)} %param.8) | copy-start | bytes 884740
  27.4 8.3 %collective-permute-start.7 = (bf16[192,512]{1,0:T(8,128)(2,1)S(1)}, bf16[192,512]{1,0:T(8,128)(2,1)S(1)}, u32[]{:S(2)}, u32[]{:S(2)}) collective-permute-start(bf16[192,512]{1,0:T(8,128)(2,1)S(1)} %get-tuple-element.49), channel_id=1, source_target_pairs={{0,16},{8,24},{16,0},{24,8},{1,17},{9,25},{17,1},{25,9},{2,18},{10... | collective-permute-start | bytes 589832 | tf_op jit(solution)/shard_map/ppermute | solution.py:189
  28.9 9.7 %collective-permute-start.8 = (bf16[192,512]{1,0:T(8,128)(2,1)S(1)}, bf16[192,512]{1,0:T(8,128)(2,1)S(1)}, u32[]{:S(2)}, u32[]{:S(2)}) collective-permute-start(bf16[192,512]{1,0:T(8,128)(2,1)S(1)} %get-tuple-element.50), channel_id=1, source_target_pairs={{0,24},{8,16},{16,8},{24,0},{1,25},{9,17},{17,9},{25,1},{2,26},{10... | collective-permute-start | bytes 589832 | tf_op jit(solution)/shard_map/ppermute | solution.py:189
  29.4 13.1 %copy-start.1 = (s32[128,1]{0,1:T(1,128)S(1)}, s32[128,1]{0,1:T(1,128)}, u32[]{:S(2)}) copy-start(s32[128,1]{0,1:T(1,128)} %param.7) | copy-start | bytes 1540
  29.4 9.3 %collective-permute-start.9 = (bf16[192,512]{1,0:T(8,128)(2,1)S(1)}, bf16[192,512]{1,0:T(8,128)(2,1)S(1)}, u32[]{:S(2)}, u32[]{:S(2)}) collective-permute-start(bf16[192,512]{1,0:T(8,128)(2,1)S(1)} %get-tuple-element.51), channel_id=1, source_target_pairs={{0,8},{8,0},{16,24},{24,16},{1,9},{9,1},{17,25},{25,17},{2,10},{10... | collective-permute-start | bytes 589832 | tf_op jit(solution)/shard_map/ppermute | solution.py:189
  31.6 10.8 %all-to-all-start = ((f32[8,8,128]{2,1,0:T(8,128)}), f32[8,8,128]{2,1,0:T(8,128)S(1)}, u32[]{:S(2)}, u32[]{:S(2)}) async-start(f32[8,8,128]{2,1,0:T(8,128)} %get-tuple-element.48), calls=%async_computation | async-start | bytes 65536 | tf_op jit(solution)/shard_map/all_to_all | solution.py:192

commit v5 on v2

--- a/solution.py
+++ b/solution.py
@@ -11,7 +11,6 @@
 F32 = jnp.float32
 BF16 = jnp.bfloat16
 ORDER = (6, 1, 7, 2, 4, 5, 3, 0)
-LATE = 6
 
 
 def kernel_call(body, outs, operands, name, flops=0, scratch=(), stay=()):
@@ -192,16 +191,14 @@
         scratch=(pltpu.SemaphoreType.DMA(()),),
     )
     if order:
-        packed[LATE], weight = lax.optimization_barrier((packed[LATE], weight))
         arrived = [swap(rows, "expert", k) if k else rows for k, rows in zip(order, packed)]
     else:
         arrived = [exchange(packed[0])]
     replicas = [*range(2, n_dp), 1, 0]
-    held, step = {0: stored}, n_dp // 2
-    while step:
-        held |= {k | step: swap(array, "dp", step) for k, array in held.items()}
-        step //= 2
-    all_stored = [held[k] for k in replicas]
+    late, weight = lax.optimization_barrier((stored, weight))
+    all_stored = [
+        swap(stored if k == replicas[0] else late, "dp", k) if k else stored for k in replicas
+    ]
 
     rows, prob, *weighted = kernel_call(
         functools.partial(weigh_body, replicas, order),

time: 44.4 us -> 42.9 us (0.966)
  starting transfers between devices: 25.2 us -> 20.6 us
  waiting for transfers between devices: 9.86 us -> 12.9 us
    ppermute x13, waiting for transfers between devices: 5.19 us -> 9.58 us  [swap(): return lax.ppermute(array, axis, [(r, r ^ k) for r in range(size)])]
    ppermute x13, starting transfers between devices: 20.2 us -> 16.3 us  [swap(): return lax.ppermute(array, axis, [(r, r ^ k) for r in range(size)])]
    all_to_all x1, waiting for transfers between devices: 4.67 us -> 3.36 us  [exchange(): lax.all_to_all(array, 'expert', split_axis=0, concat_axis=0, tiled=True)]
    all_to_all x1, starting transfers between devices: 5.03 us -> 4.38 us  [exchange(): lax.all_to_all(array, 'expert', split_axis=0, concat_axis=0, tiled=True)]
  transfers between devices with their start and end apart: 14 -> 14, of which waited for: 3 -> 7; matrix products, arithmetic and copies ran while one was open for 0% -> 0% of each run, Pallas kernels for 18% -> 15%
where the time goes in v5:
time: 42.9 us; the launch traced here: 42.7 us
  starting transfers between devices  20.6 us (48%)
  waiting for transfers between devices  12.9 us (30%)
  Pallas kernels  8.42 us (20%)
  between operations  0.7 us (2%)
    ppermute x13, starting transfers between devices, swap(): return lax.ppermute(array, axis, [(r, r ^ k) for r in range(size)])  16.3 us
    ppermute x13, waiting for transfers between devices, swap(): return lax.ppermute(array, axis, [(r, r ^ k) for r in range(size)])  9.58 us
    pallas_call x6, Pallas kernels, kernel_call(): pl.pallas_call(body, out_shape=outs, in_specs=[hbm if i in stay else vmem...  8.42 us
    all_to_all x1, starting transfers between devices, exchange(): lax.all_to_all(array, 'expert', split_axis=0, concat_axis=0, tiled=True)  4.38 us
    all_to_all x1, waiting for transfers between devices, exchange(): lax.all_to_all(array, 'expert', split_axis=0, concat_axis=0, tiled=True)  3.36 us
  transfers between devices with their start and end apart: 14, of which 7 were waited for; matrix products, arithmetic and copies ran while one was open for 0% of the time, Pallas kernels for 15%

profile of v5, /device:TPU:0, one launch (start us, length us, event | category | flops | bytes accessed | tf_op | source)
XLA Modules:
  0.0 42.7 jit_solution(12986783480072525118)
XLA Ops:
  0.6 1.5 %place.1 = (bf16[24,2176]{1,0:T(8,128)(2,1)S(1)}, bf16[24,2176]{1,0:T(8,128)(2,1)S(1)}, bf16[24,2176]{1,0:T(8,128)(2,1)S(1)}, bf16[24,2176]{1,0:T(8,128)(2,1)S(1...) custom-call(s32[1,128]{1,0:T(1,128)} %bitcast.12, ...), custom_call_target="tpu_custom_call" | custom-call | flops 100663296 | bytes 1361152 | tf_op jit(solution)/shard_map/place/pallas_call | solution.py:23
  2.1 5.1 %collective-permute-start = (bf16[24,2176]{1,0:T(8,128)(2,1)S(1)}, bf16[24,2176]{1,0:T(8,128)(2,1)S(1)}, u32[]{:S(2)}, u32[]{:S(2)}) collective-permute-start(bf16[24,2176]{1,0:T(8,128)(2,1)S(1)} %get-tuple-element.25), channel_id=1, source_target_pairs={{0,6},{1,7},{2,4},{3,5},{4,2},{5,3},{6,0},{7,1},{8,14},{9,15},{10,... | collective-permute-start | bytes 313352 | tf_op jit(solution)/shard_map/ppermute | solution.py:165
  7.2 1.5 %collective-permute-start.10 = (bf16[192,768]{1,0:T(8,128)(2,1)}, bf16[192,768]{1,0:T(8,128)(2,1)S(1)}, u32[]{:S(2)}, u32[]{:S(2)}) collective-permute-start(bf16[192,768]{1,0:T(8,128)(2,1)} %bitcast.7), channel_id=1, source_target_pairs={{0,16},{8,24},{16,0},{24,8},{1,17},{9,25},{17,1},{25,9},{2,18},{10... | collective-permute-start | bytes 884744 | tf_op jit(solution)/shard_map/ppermute | solution.py:165
  8.7 1.5 %collective-permute-start.1 = (bf16[24,2176]{1,0:T(8,128)(2,1)S(1)}, bf16[24,2176]{1,0:T(8,128)(2,1)S(1)}, u32[]{:S(2)}, u32[]{:S(2)}) collective-permute-start(bf16[24,2176]{1,0:T(8,128)(2,1)S(1)} %get-tuple-element.26), channel_id=1, source_target_pairs={{0,1},{1,0},{2,3},{3,2},{4,5},{5,4},{6,7},{7,6},{8,9},{9,8},{10,11... | collective-permute-start | bytes 313352 | tf_op jit(solution)/shard_map/ppermute | solution.py:165
  10.2 0.2 collective-permute-start.2
  10.4 0.0 collective-permute-start.3
  10.4 0.0 collective-permute-done.refs_0_
  10.4 4.2 %collective-permute-start.4 = (bf16[24,2176]{1,0:T(8,128)(2,1)S(1)}, bf16[24,2176]{1,0:T(8,128)(2,1)S(1)}, u32[]{:S(2)}, u32[]{:S(2)}) collective-permute-start(bf16[24,2176]{1,0:T(8,128)(2,1)S(1)} %get-tuple-element.29), channel_id=1, source_target_pairs={{0,4},{1,5},{2,6},{3,7},{4,0},{5,1},{6,2},{7,3},{8,12},{9,13},{10,... | collective-permute-start | bytes 313352 | tf_op jit(solution)/shard_map/ppermute | solution.py:165
  14.6 0.0 collective-permute-done.1.refs_1_
  14.6 1.0 %collective-permute-start.5 = (bf16[24,2176]{1,0:T(8,128)(2,1)S(1)}, bf16[24,2176]{1,0:T(8,128)(2,1)S(1)}, u32[]{:S(2)}, u32[]{:S(2)}) collective-permute-start(bf16[24,2176]{1,0:T(8,128)(2,1)S(1)} %get-tuple-element.30), channel_id=1, source_target_pairs={{0,5},{1,4},{2,7},{3,6},{4,1},{5,0},{6,3},{7,2},{8,13},{9,12},{10,... | collective-permute-start | bytes 313352 | tf_op jit(solution)/shard_map/ppermute | solution.py:165
  15.6 3.3 %collective-permute-done.2.refs_2_ = bf16[24,2176]{1,0:T(8,128)(2,1)S(1)} collective-permute-done((bf16[24,2176]{1,0:T(8,128)(2,1)S(1)}, bf16[24,2176]{1,0:T(8,128)(2,1)S(1)}, u32[]{:S(2)}, u32[]{:S(2)}) %collective-permute-start.2) | collective-permute-done | bytes 104480 | tf_op jit(solution)/shard_map/ppermute | solution.py:165
  18.9 0.0 collective-permute-start.6
  18.9 1.9 %fetch.1.weight_ref = bf16[768,2048]{1,0:T(8,128)(2,1)S(1)} custom-call(bf16[768,2048]{1,0:T(8,128)(2,1)} %bitcast.14), custom_call_target="tpu_custom_call" | custom-call | flops 603979776 | bytes 6291456 | tf_op jit(solution)/shard_map/fetch/pallas_call | solution.py:23
  20.9 0.0 collective-permute-done.3.refs_3_
  20.9 0.1 collective-permute-start.11
  21.0 2.9 %collective-permute-done.4.refs_4_ = bf16[24,2176]{1,0:T(8,128)(2,1)S(1)} collective-permute-done((bf16[24,2176]{1,0:T(8,128)(2,1)S(1)}, bf16[24,2176]{1,0:T(8,128)(2,1)S(1)}, u32[]{:S(2)}, u32[]{:S(2)}) %collective-permute-start.4) | collective-permute-done | bytes 104480 | tf_op jit(solution)/shard_map/ppermute | solution.py:165
  23.9 0.5 %collective-permute-start.12 = (bf16[192,768]{1,0:T(8,128)(2,1)S(1)}, bf16[192,768]{1,0:T(8,128)(2,1)S(1)}, u32[]{:S(2)}, u32[]{:S(2)}) collective-permute-start(bf16[192,768]{1,0:T(8,128)(2,1)S(1)} %bitcast.9), channel_id=1, source_target_pairs={{0,8},{8,0},{16,24},{24,16},{1,9},{9,1},{17,25},{25,17},{2,10},{10... | collective-permute-start | bytes 884744 | tf_op jit(solution)/shard_map/ppermute | solution.py:165
  24.4 1.7 %collective-permute-done.5.refs_5_ = bf16[24,2176]{1,0:T(8,128)(2,1)S(1)} collective-permute-done((bf16[24,2176]{1,0:T(8,128)(2,1)S(1)}, bf16[24,2176]{1,0:T(8,128)(2,1)S(1)}, u32[]{:S(2)}, u32[]{:S(2)}) %collective-permute-start.5) | collective-permute-done | bytes 104480 | tf_op jit(solution)/shard_map/ppermute | solution.py:165
  26.1 0.3 collective-permute-done.6.refs_6_
  26.4 0.5 %weigh.1 = (bf16[192,2048]{1,0:T(8,128)(2,1)S(1)}, f32[192,128]{1,0:T(8,128)S(1)}, bf16[192,512]{1,0:T(8,128)(2,1)S(1)}, bf16[192,512]{1,0:T(8,128)(2,1)S(1)}, b...) custom-call(bf16[24,2176]{1,0:T(8,128)(2,1)S(1)} %collective-permute-done.refs_0_, ...), custom_call_target="tpu_custom_call" | custom-call | flops 786432 | bytes 2506752 | tf_op jit(solution)/shard_map/weigh/pallas_call | solution.py:23
  26.8 1.6 %collective-permute-start.7 = (bf16[192,512]{1,0:T(8,128)(2,1)S(1)}, bf16[192,512]{1,0:T(8,128)(2,1)S(1)}, u32[]{:S(2)}, u32[]{:S(2)}) collective-permute-start(bf16[192,512]{1,0:T(8,128)(2,1)S(1)} %get-tuple-element.40), channel_id=1, source_target_pairs={{0,16},{8,24},{16,0},{24,8},{1,17},{9,25},{17,1},{25,9},{2,18},{10... | collective-permute-start | bytes 589832 | tf_op jit(solution)/shard_map/ppermute | solution.py:165
  28.5 0.0 collective-permute-start.8
  28.5 0.6 %collective-permute-start.9 = (bf16[192,512]{1,0:T(8,128)(2,1)S(1)}, bf16[192,512]{1,0:T(8,128)(2,1)S(1)}, u32[]{:S(2)}, u32[]{:S(2)}) collective-permute-start(bf16[192,512]{1,0:T(8,128)(2,1)S(1)} %get-tuple-element.42), channel_id=1, source_target_pairs={{0,8},{8,0},{16,24},{24,16},{1,9},{9,1},{17,25},{25,17},{2,10},{10... | collective-permute-start | bytes 589832 | tf_op jit(solution)/shard_map/ppermute | solution.py:165
  29.1 2.0 %act.1 = (bf16[192,768]{1,0:T(8,128)(2,1)}, f32[8,8,128]{2,1,0:T(8,128)}) custom-call(bf16[192,2048]{1,0:T(8,128)(2,1)S(1)} %get-tuple-element.33.rows_ref, f32[192,128]{1,0:T(8,128)S(1)} %get-tuple-element.34.prob_ref, bf16[768,2048]{1,0:T(8,128)(2,1)S(1)} %fetch.1.weight_ref, bf16[192,768]{1,0:T(8,128)(2,1)S(1)} %bitcast.10), custom_call_target="tpu_custom_call" | custom-call | flops 603979776 | bytes 4653056 | tf_op jit(solution)/shard_map/act/pallas_call | solution.py:23
  31.0 4.4 %all-to-all-start = ((f32[8,8,128]{2,1,0:T(8,128)}), f32[8,8,128]{2,1,0:T(8,128)S(1)}, u32[]{:S(2)}, u32[]{:S(2)}) async-start(f32[8,8,128]{2,1,0:T(8,128)} %get-tuple-element.39), calls=%async_computation | async-start | bytes 65536 | tf_op jit(solution)/shard_map/all_to_all | solution.py:168
  35.4 0.0 collective-permute-done.12.refs_6_
  35.4 1.0 %collective-permute-done.7.refs_0_ = bf16[192,512]{1,0:T(8,128)(2,1)S(1)} collective-permute-done((bf16[192,512]{1,0:T(8,128)(2,1)S(1)}, bf16[192,512]{1,0:T(8,128)(2,1)S(1)}, u32[]{:S(2)}, u32[]{:S(2)}) %collective-permute-start.7) | collective-permute-done | bytes 196640 | tf_op jit(solution)/shard_map/ppermute | solution.py:165
  36.4 0.4 collective-permute-done.8.refs_1_
  36.8 0.0 collective-permute-done.9.refs_2_
  36.8 2.0 %gradient.1 = f32[512,768]{1,0:T(8,128)} custom-call(bf16[192,512]{1,0:T(8,128)(2,1)S(1)} %collective-permute-done.7.refs_0_, bf16[192,512]{1,0:T(8,128)(2,1)S(1)} %collective-permute-done.8.refs_1_, bf16[192,512]{1,0:T(8,128)(2,1)S(1)} %collective-permute-done.9.refs_2_, bf16[192,512]{1,0:T(8,128)(2,1)S(1)} %get-tuple-element.43.refs_3_, ...), custom_call_target="tpu_custom_call" | custom-call | flops 603979776 | bytes 3538944 | tf_op jit(solution)/shard_map/gradient/pallas_call | solution.py:23
  38.7 3.4 %all-to-all-done.table_ref = f32[8,8,128]{2,1,0:T(8,128)S(1)} async-done(((f32[8,8,128]{2,1,0:T(8,128)}), f32[8,8,128]{2,1,0:T(8,128)S(1)}, u32[]{:S(2)}, u32[]{:S(2)}) %all-to-all-start) | async-done | bytes 32800 | tf_op jit(solution)/shard_map/all_to_all | solution.py:168
  42.1 0.6 %pick.1 = f32[1,128]{1,0:T(1,128)} custom-call(s32[1,128]{1,0:T(1,128)S(1)} %bitcast.13, s32[1,128]{1,0:T(1,128)S(1)} %get-tuple-element.35.within_ref, f32[8,8,128]{2,1,0:T(8,128)S(1)} %all-to-all-done.table_ref), custom_call_target="tpu_custom_call" | custom-call | bytes 34304 | tf_op jit(solution)/shard_map/pick/pallas_call | solution.py:23
  (6 shorter events, 0.0 us)
Async XLA Ops:
  2.1 8.3 %collective-permute-start = (bf16[24,2176]{1,0:T(8,128)(2,1)S(1)}, bf16[24,2176]{1,0:T(8,128)(2,1)S(1)}, u32[]{:S(2)}, u32[]{:S(2)}) collective-permute-start(bf16[24,2176]{1,0:T(8,128)(2,1)S(1)} %get-tuple-element.25), channel_id=1, source_target_pairs={{0,6},{1,7},{2,4},{3,5},{4,2},{5,3},{6,0},{7,1},{8,14},{9,15},{10,... | collective-permute-start | bytes 313352 | tf_op jit(solution)/shard_map/ppermute | solution.py:165
  7.2 21.2 %collective-permute-start.10 = (bf16[192,768]{1,0:T(8,128)(2,1)}, bf16[192,768]{1,0:T(8,128)(2,1)S(1)}, u32[]{:S(2)}, u32[]{:S(2)}) collective-permute-start(bf16[192,768]{1,0:T(8,128)(2,1)} %bitcast.7), channel_id=1, source_target_pairs={{0,16},{8,24},{16,0},{24,8},{1,17},{9,25},{17,1},{25,9},{2,18},{10... | collective-permute-start | bytes 884744 | tf_op jit(solution)/shard_map/ppermute | solution.py:165
  8.7 5.9 %collective-permute-start.1 = (bf16[24,2176]{1,0:T(8,128)(2,1)S(1)}, bf16[24,2176]{1,0:T(8,128)(2,1)S(1)}, u32[]{:S(2)}, u32[]{:S(2)}) collective-permute-start(bf16[24,2176]{1,0:T(8,128)(2,1)S(1)} %get-tuple-element.26), channel_id=1, source_target_pairs={{0,1},{1,0},{2,3},{3,2},{4,5},{5,4},{6,7},{7,6},{8,9},{9,8},{10,11... | collective-permute-start | bytes 313352 | tf_op jit(solution)/shard_map/ppermute | solution.py:165
  10.2 8.7 %collective-permute-start.2 = (bf16[24,2176]{1,0:T(8,128)(2,1)S(1)}, bf16[24,2176]{1,0:T(8,128)(2,1)S(1)}, u32[]{:S(2)}, u32[]{:S(2)}) collective-permute-start(bf16[24,2176]{1,0:T(8,128)(2,1)S(1)} %get-tuple-element.27), channel_id=1, source_target_pairs={{0,7},{1,6},{2,5},{3,4},{4,3},{5,2},{6,1},{7,0},{8,15},{9,14},{10,... | collective-permute-start | bytes 313352 | tf_op jit(solution)/shard_map/ppermute | solution.py:165
  10.4 10.4 %collective-permute-start.3 = (bf16[24,2176]{1,0:T(8,128)(2,1)S(1)}, bf16[24,2176]{1,0:T(8,128)(2,1)S(1)}, u32[]{:S(2)}, u32[]{:S(2)}) collective-permute-start(bf16[24,2176]{1,0:T(8,128)(2,1)S(1)} %get-tuple-element.28), channel_id=1, source_target_pairs={{0,2},{1,3},{2,0},{3,1},{4,6},{5,7},{6,4},{7,5},{8,10},{9,11},{10,... | collective-permute-start | bytes 313352 | tf_op jit(solution)/shard_map/ppermute | solution.py:165
  10.4 13.4 %collective-permute-start.4 = (bf16[24,2176]{1,0:T(8,128)(2,1)S(1)}, bf16[24,2176]{1,0:T(8,128)(2,1)S(1)}, u32[]{:S(2)}, u32[]{:S(2)}) collective-permute-start(bf16[24,2176]{1,0:T(8,128)(2,1)S(1)} %get-tuple-element.29), channel_id=1, source_target_pairs={{0,4},{1,5},{2,6},{3,7},{4,0},{5,1},{6,2},{7,3},{8,12},{9,13},{10,... | collective-permute-start | bytes 313352 | tf_op jit(solution)/shard_map/ppermute | solution.py:165
  14.6 11.5 %collective-permute-start.5 = (bf16[24,2176]{1,0:T(8,128)(2,1)S(1)}, bf16[24,2176]{1,0:T(8,128)(2,1)S(1)}, u32[]{:S(2)}, u32[]{:S(2)}) collective-permute-start(bf16[24,2176]{1,0:T(8,128)(2,1)S(1)} %get-tuple-element.30), channel_id=1, source_target_pairs={{0,5},{1,4},{2,7},{3,6},{4,1},{5,0},{6,3},{7,2},{8,13},{9,12},{10,... | collective-permute-start | bytes 313352 | tf_op jit(solution)/shard_map/ppermute | solution.py:165
  18.9 2.0 %copy-start = (bf16[1,1,192,768]{3,2,1,0:T(8,128)(2,1)S(1)}, bf16[1,1,192,768]{3,2,1,0:T(8,128)(2,1)}, u32[]{:S(2)}) copy-start(bf16[1,1,192,768]{3,2,1,0:T(8,128)(2,1)} %param.8) | copy-start | bytes 884740
  18.9 7.5 %collective-permute-start.6 = (bf16[24,2176]{1,0:T(8,128)(2,1)S(1)}, bf16[24,2176]{1,0:T(8,128)(2,1)S(1)}, u32[]{:S(2)}, u32[]{:S(2)}) collective-permute-start(bf16[24,2176]{1,0:T(8,128)(2,1)S(1)} %get-tuple-element.31), channel_id=1, source_target_pairs={{0,3},{1,2},{2,1},{3,0},{4,7},{5,6},{6,5},{7,4},{8,11},{9,10},{10,... | collective-permute-start | bytes 313352 | tf_op jit(solution)/shard_map/ppermute | solution.py:165
  20.9 14.5 %collective-permute-start.11 = (bf16[192,768]{1,0:T(8,128)(2,1)S(1)}, bf16[192,768]{1,0:T(8,128)(2,1)S(1)}, u32[]{:S(2)}, u32[]{:S(2)}) collective-permute-start(bf16[192,768]{1,0:T(8,128)(2,1)S(1)} %bitcast.8), channel_id=1, source_target_pairs={{0,24},{8,16},{16,8},{24,0},{1,25},{9,17},{17,9},{25,1},{2,26},{10... | collective-permute-start | bytes 884744 | tf_op jit(solution)/shard_map/ppermute | solution.py:165
  23.9 11.5 %collective-permute-start.12 = (bf16[192,768]{1,0:T(8,128)(2,1)S(1)}, bf16[192,768]{1,0:T(8,128)(2,1)S(1)}, u32[]{:S(2)}, u32[]{:S(2)}) collective-permute-start(bf16[192,768]{1,0:T(8,128)(2,1)S(1)} %bitcast.9), channel_id=1, source_target_pairs={{0,8},{8,0},{16,24},{24,16},{1,9},{9,1},{17,25},{25,17},{2,10},{10... | collective-permute-start | bytes 884744 | tf_op jit(solution)/shard_map/ppermute | solution.py:165
  26.8 9.6 %collective-permute-start.7 = (bf16[192,512]{1,0:T(8,128)(2,1)S(1)}, bf16[192,512]{1,0:T(8,128)(2,1)S(1)}, u32[]{:S(2)}, u32[]{:S(2)}) collective-permute-start(bf16[192,512]{1,0:T(8,128)(2,1)S(1)} %get-tuple-element.40), channel_id=1, source_target_pairs={{0,16},{8,24},{16,0},{24,8},{1,17},{9,25},{17,1},{25,9},{2,18},{10... | collective-permute-start | bytes 589832 | tf_op jit(solution)/shard_map/ppermute | solution.py:165
  28.5 8.3 %collective-permute-start.8 = (bf16[192,512]{1,0:T(8,128)(2,1)S(1)}, bf16[192,512]{1,0:T(8,128)(2,1)S(1)}, u32[]{:S(2)}, u32[]{:S(2)}) collective-permute-start(bf16[192,512]{1,0:T(8,128)(2,1)S(1)} %get-tuple-element.41), channel_id=1, source_target_pairs={{0,24},{8,16},{16,8},{24,0},{1,25},{9,17},{17,9},{25,1},{2,26},{10... | collective-permute-start | bytes 589832 | tf_op jit(solution)/shard_map/ppermute | solution.py:165
  28.5 8.3 %collective-permute-start.9 = (bf16[192,512]{1,0:T(8,128)(2,1)S(1)}, bf16[192,512]{1,0:T(8,128)(2,1)S(1)}, u32[]{:S(2)}, u32[]{:S(2)}) collective-permute-start(bf16[192,512]{1,0:T(8,128)(2,1)S(1)} %get-tuple-element.42), channel_id=1, source_target_pairs={{0,8},{8,0},{16,24},{24,16},{1,9},{9,1},{17,25},{25,17},{2,10},{10... | collective-permute-start | bytes 589832 | tf_op jit(solution)/shard_map/ppermute | solution.py:165
  29.1 13.1 %copy-start.1 = (s32[128,1]{0,1:T(1,128)S(1)}, s32[128,1]{0,1:T(1,128)}, u32[]{:S(2)}) copy-start(s32[128,1]{0,1:T(1,128)} %param.7) | copy-start | bytes 1540
  31.0 11.1 %all-to-all-start = ((f32[8,8,128]{2,1,0:T(8,128)}), f32[8,8,128]{2,1,0:T(8,128)S(1)}, u32[]{:S(2)}, u32[]{:S(2)}) async-start(f32[8,8,128]{2,1,0:T(8,128)} %get-tuple-element.39), calls=%async_computation | async-start | bytes 65536 | tf_op jit(solution)/shard_map/all_to_all | solution.py:168

commit v6 on v5

--- a/solution.py
+++ b/solution.py
@@ -10,7 +10,7 @@
 LANES = 128
 F32 = jnp.float32
 BF16 = jnp.bfloat16
-ORDER = (6, 1, 7, 2, 4, 5, 3, 0)
+ORDER = (6, 1, 2, 7, 4, 5, 3, 0)
 
 
 def kernel_call(body, outs, operands, name, flops=0, scratch=(), stay=()):

time: 42.9 us -> 42.8 us (level)
  starting transfers between devices: 20.6 us -> 18.5 us
  waiting for transfers between devices: 12.9 us -> 15 us
    ppermute x13, waiting for transfers between devices: 9.58 us -> 11.5 us  [swap(): return lax.ppermute(array, axis, [(r, r ^ k) for r in range(size)])]
    ppermute x13, starting transfers between devices: 16.3 us -> 15.1 us  [swap(): return lax.ppermute(array, axis, [(r, r ^ k) for r in range(size)])]
    all_to_all x1, starting transfers between devices: 4.38 us -> 3.33 us  [exchange(): lax.all_to_all(array, 'expert', split_axis=0, concat_axis=0, tiled=True)]
  transfers between devices with their start and end apart: 14 -> 14, of which waited for: 7 -> 6; matrix products, arithmetic and copies ran while one was open for 0% -> 0% of each run, Pallas kernels for 15% -> 15%
where the time goes in v6:
time: 42.8 us; the launch traced here: 42.6 us
  starting transfers between devices  18.5 us (43%)
  waiting for transfers between devices  15 us (35%)
  Pallas kernels  8.42 us (20%)
  between operations  0.72 us (2%)
    ppermute x13, starting transfers between devices, swap(): return lax.ppermute(array, axis, [(r, r ^ k) for r in range(size)])  15.1 us
    ppermute x13, waiting for transfers between devices, swap(): return lax.ppermute(array, axis, [(r, r ^ k) for r in range(size)])  11.5 us
    pallas_call x6, Pallas kernels, kernel_call(): pl.pallas_call(body, out_shape=outs, in_specs=[hbm if i in stay else vmem...  8.42 us
    all_to_all x1, waiting for transfers between devices, exchange(): lax.all_to_all(array, 'expert', split_axis=0, concat_axis=0, tiled=True)  3.48 us
    all_to_all x1, starting transfers between devices, exchange(): lax.all_to_all(array, 'expert', split_axis=0, concat_axis=0, tiled=True)  3.33 us
  transfers between devices with their start and end apart: 14, of which 6 were waited for; matrix products, arithmetic and copies ran while one was open for 0% of the time, Pallas kernels for 15%

profile of v6, /device:TPU:0, one launch (start us, length us, event | category | flops | bytes accessed | tf_op | source)
XLA Modules:
  0.0 42.6 jit_solution(11691967139363117)
XLA Ops:
  0.6 1.5 %place.1 = (bf16[24,2176]{1,0:T(8,128)(2,1)S(1)}, bf16[24,2176]{1,0:T(8,128)(2,1)S(1)}, bf16[24,2176]{1,0:T(8,128)(2,1)S(1)}, bf16[24,2176]{1,0:T(8,128)(2,1)S(1...) custom-call(s32[1,128]{1,0:T(1,128)} %bitcast.12, ...), custom_call_target="tpu_custom_call" | custom-call | flops 100663296 | bytes 1361152 | tf_op jit(solution)/shard_map/place/pallas_call | solution.py:23
  2.1 5.1 %collective-permute-start = (bf16[24,2176]{1,0:T(8,128)(2,1)S(1)}, bf16[24,2176]{1,0:T(8,128)(2,1)S(1)}, u32[]{:S(2)}, u32[]{:S(2)}) collective-permute-start(bf16[24,2176]{1,0:T(8,128)(2,1)S(1)} %get-tuple-element.25), channel_id=1, source_target_pairs={{0,6},{1,7},{2,4},{3,5},{4,2},{5,3},{6,0},{7,1},{8,14},{9,15},{10,... | collective-permute-start | bytes 313352 | tf_op jit(solution)/shard_map/ppermute | solution.py:165
  7.2 1.5 %collective-permute-start.10 = (bf16[192,768]{1,0:T(8,128)(2,1)}, bf16[192,768]{1,0:T(8,128)(2,1)S(1)}, u32[]{:S(2)}, u32[]{:S(2)}) collective-permute-start(bf16[192,768]{1,0:T(8,128)(2,1)} %bitcast.7), channel_id=1, source_target_pairs={{0,16},{8,24},{16,0},{24,8},{1,17},{9,25},{17,1},{25,9},{2,18},{10... | collective-permute-start | bytes 884744 | tf_op jit(solution)/shard_map/ppermute | solution.py:165
  8.7 1.5 %collective-permute-start.1 = (bf16[24,2176]{1,0:T(8,128)(2,1)S(1)}, bf16[24,2176]{1,0:T(8,128)(2,1)S(1)}, u32[]{:S(2)}, u32[]{:S(2)}) collective-permute-start(bf16[24,2176]{1,0:T(8,128)(2,1)S(1)} %get-tuple-element.26), channel_id=1, source_target_pairs={{0,1},{1,0},{2,3},{3,2},{4,5},{5,4},{6,7},{7,6},{8,9},{9,8},{10,11... | collective-permute-start | bytes 313352 | tf_op jit(solution)/shard_map/ppermute | solution.py:165
  10.2 0.0 collective-permute-start.2
  10.2 0.9 %collective-permute-start.3 = (bf16[24,2176]{1,0:T(8,128)(2,1)S(1)}, bf16[24,2176]{1,0:T(8,128)(2,1)S(1)}, u32[]{:S(2)}, u32[]{:S(2)}) collective-permute-start(bf16[24,2176]{1,0:T(8,128)(2,1)S(1)} %get-tuple-element.28), channel_id=1, source_target_pairs={{0,7},{1,6},{2,5},{3,4},{4,3},{5,2},{6,1},{7,0},{8,15},{9,14},{10,... | collective-permute-start | bytes 313352 | tf_op jit(solution)/shard_map/ppermute | solution.py:165
  11.1 0.0 collective-permute-done.refs_0_
  11.1 2.6 %collective-permute-start.4 = (bf16[24,2176]{1,0:T(8,128)(2,1)S(1)}, bf16[24,2176]{1,0:T(8,128)(2,1)S(1)}, u32[]{:S(2)}, u32[]{:S(2)}) collective-permute-start(bf16[24,2176]{1,0:T(8,128)(2,1)S(1)} %get-tuple-element.29), channel_id=1, source_target_pairs={{0,4},{1,5},{2,6},{3,7},{4,0},{5,1},{6,2},{7,3},{8,12},{9,13},{10,... | collective-permute-start | bytes 313352 | tf_op jit(solution)/shard_map/ppermute | solution.py:165
  13.7 0.0 collective-permute-done.1.refs_1_
  13.7 1.3 %collective-permute-start.5 = (bf16[24,2176]{1,0:T(8,128)(2,1)S(1)}, bf16[24,2176]{1,0:T(8,128)(2,1)S(1)}, u32[]{:S(2)}, u32[]{:S(2)}) collective-permute-start(bf16[24,2176]{1,0:T(8,128)(2,1)S(1)} %get-tuple-element.30), channel_id=1, source_target_pairs={{0,5},{1,4},{2,7},{3,6},{4,1},{5,0},{6,3},{7,2},{8,13},{9,12},{10,... | collective-permute-start | bytes 313352 | tf_op jit(solution)/shard_map/ppermute | solution.py:165
  15.0 2.3 %collective-permute-done.2.refs_2_ = bf16[24,2176]{1,0:T(8,128)(2,1)S(1)} collective-permute-done((bf16[24,2176]{1,0:T(8,128)(2,1)S(1)}, bf16[24,2176]{1,0:T(8,128)(2,1)S(1)}, u32[]{:S(2)}, u32[]{:S(2)}) %collective-permute-start.2) | collective-permute-done | bytes 104480 | tf_op jit(solution)/shard_map/ppermute | solution.py:165
  17.3 0.0 collective-permute-start.6
  17.3 1.9 %fetch.1.weight_ref = bf16[768,2048]{1,0:T(8,128)(2,1)S(1)} custom-call(bf16[768,2048]{1,0:T(8,128)(2,1)} %bitcast.14), custom_call_target="tpu_custom_call" | custom-call | flops 603979776 | bytes 6291456 | tf_op jit(solution)/shard_map/fetch/pallas_call | solution.py:23
  19.2 0.0 collective-permute-done.3.refs_3_
  19.2 0.1 collective-permute-start.11
  19.3 5.9 %collective-permute-done.4.refs_4_ = bf16[24,2176]{1,0:T(8,128)(2,1)S(1)} collective-permute-done((bf16[24,2176]{1,0:T(8,128)(2,1)S(1)}, bf16[24,2176]{1,0:T(8,128)(2,1)S(1)}, u32[]{:S(2)}, u32[]{:S(2)}) %collective-permute-start.4) | collective-permute-done | bytes 104480 | tf_op jit(solution)/shard_map/ppermute | solution.py:165
  25.2 2.2 %collective-permute-done.5.refs_5_ = bf16[24,2176]{1,0:T(8,128)(2,1)S(1)} collective-permute-done((bf16[24,2176]{1,0:T(8,128)(2,1)S(1)}, bf16[24,2176]{1,0:T(8,128)(2,1)S(1)}, u32[]{:S(2)}, u32[]{:S(2)}) %collective-permute-start.5) | collective-permute-done | bytes 104480 | tf_op jit(solution)/shard_map/ppermute | solution.py:165
  27.3 0.0 collective-permute-done.6.refs_6_
  27.4 0.5 %weigh.1 = (bf16[192,2048]{1,0:T(8,128)(2,1)S(1)}, f32[192,128]{1,0:T(8,128)S(1)}, bf16[192,512]{1,0:T(8,128)(2,1)S(1)}, bf16[192,512]{1,0:T(8,128)(2,1)S(1)}, b...) custom-call(bf16[24,2176]{1,0:T(8,128)(2,1)S(1)} %collective-permute-done.refs_0_, ...), custom_call_target="tpu_custom_call" | custom-call | flops 786432 | bytes 2506752 | tf_op jit(solution)/shard_map/weigh/pallas_call | solution.py:23
  27.8 0.6 %collective-permute-start.7 = (bf16[192,512]{1,0:T(8,128)(2,1)S(1)}, bf16[192,512]{1,0:T(8,128)(2,1)S(1)}, u32[]{:S(2)}, u32[]{:S(2)}) collective-permute-start(bf16[192,512]{1,0:T(8,128)(2,1)S(1)} %get-tuple-element.40), channel_id=1, source_target_pairs={{0,16},{8,24},{16,0},{24,8},{1,17},{9,25},{17,1},{25,9},{2,18},{10... | collective-permute-start | bytes 589832 | tf_op jit(solution)/shard_map/ppermute | solution.py:165
  28.4 0.2 collective-permute-start.8
  28.6 0.0 collective-permute-done.10.refs_4_
  28.6 1.5 %collective-permute-start.9 = (bf16[192,512]{1,0:T(8,128)(2,1)S(1)}, bf16[192,512]{1,0:T(8,128)(2,1)S(1)}, u32[]{:S(2)}, u32[]{:S(2)}) collective-permute-start(bf16[192,512]{1,0:T(8,128)(2,1)S(1)} %get-tuple-element.42), channel_id=1, source_target_pairs={{0,8},{8,0},{16,24},{24,16},{1,9},{9,1},{17,25},{25,17},{2,10},{10... | collective-permute-start | bytes 589832 | tf_op jit(solution)/shard_map/ppermute | solution.py:165
  30.0 2.0 %act.1 = (bf16[192,768]{1,0:T(8,128)(2,1)}, f32[8,8,128]{2,1,0:T(8,128)}) custom-call(bf16[192,2048]{1,0:T(8,128)(2,1)S(1)} %get-tuple-element.33.rows_ref, f32[192,128]{1,0:T(8,128)S(1)} %get-tuple-element.34.prob_ref, bf16[768,2048]{1,0:T(8,128)(2,1)S(1)} %fetch.1.weight_ref, bf16[192,768]{1,0:T(8,128)(2,1)S(1)} %bitcast.10), custom_call_target="tpu_custom_call" | custom-call | flops 603979776 | bytes 4653056 | tf_op jit(solution)/shard_map/act/pallas_call | solution.py:23
  32.0 3.3 %all-to-all-start = ((f32[8,8,128]{2,1,0:T(8,128)}), f32[8,8,128]{2,1,0:T(8,128)S(1)}, u32[]{:S(2)}, u32[]{:S(2)}) async-start(f32[8,8,128]{2,1,0:T(8,128)} %get-tuple-element.39), calls=%async_computation | async-start | bytes 65536 | tf_op jit(solution)/shard_map/all_to_all | solution.py:168
  35.4 0.0 collective-permute-done.11.refs_5_
  35.4 0.0 collective-permute-done.12.refs_6_
  35.4 0.3 collective-permute-done.7.refs_0_
  35.7 0.8 %collective-permute-done.8.refs_1_ = bf16[192,512]{1,0:T(8,128)(2,1)S(1)} collective-permute-done((bf16[192,512]{1,0:T(8,128)(2,1)S(1)}, bf16[192,512]{1,0:T(8,128)(2,1)S(1)}, u32[]{:S(2)}, u32[]{:S(2)}) %collective-permute-start.8) | collective-permute-done | bytes 196640 | tf_op jit(solution)/shard_map/ppermute | solution.py:165
  36.5 2.0 %gradient.1 = f32[512,768]{1,0:T(8,128)} custom-call(bf16[192,512]{1,0:T(8,128)(2,1)S(1)} %collective-permute-done.7.refs_0_, bf16[192,512]{1,0:T(8,128)(2,1)S(1)} %collective-permute-done.8.refs_1_, bf16[192,512]{1,0:T(8,128)(2,1)S(1)} %collective-permute-done.9.refs_2_, bf16[192,512]{1,0:T(8,128)(2,1)S(1)} %get-tuple-element.43.refs_3_, ...), custom_call_target="tpu_custom_call" | custom-call | flops 603979776 | bytes 3538944 | tf_op jit(solution)/shard_map/gradient/pallas_call | solution.py:23
  38.5 3.5 %all-to-all-done.table_ref = f32[8,8,128]{2,1,0:T(8,128)S(1)} async-done(((f32[8,8,128]{2,1,0:T(8,128)}), f32[8,8,128]{2,1,0:T(8,128)S(1)}, u32[]{:S(2)}, u32[]{:S(2)}) %all-to-all-start) | async-done | bytes 32800 | tf_op jit(solution)/shard_map/all_to_all | solution.py:168
  42.0 0.6 %pick.1 = f32[1,128]{1,0:T(1,128)} custom-call(s32[1,128]{1,0:T(1,128)S(1)} %bitcast.13, s32[1,128]{1,0:T(1,128)S(1)} %get-tuple-element.35.within_ref, f32[8,8,128]{2,1,0:T(8,128)S(1)} %all-to-all-done.table_ref), custom_call_target="tpu_custom_call" | custom-call | bytes 34304 | tf_op jit(solution)/shard_map/pick/pallas_call | solution.py:23
  (6 shorter events, 0.0 us)
Async XLA Ops:
  2.1 9.0 %collective-permute-start = (bf16[24,2176]{1,0:T(8,128)(2,1)S(1)}, bf16[24,2176]{1,0:T(8,128)(2,1)S(1)}, u32[]{:S(2)}, u32[]{:S(2)}) collective-permute-start(bf16[24,2176]{1,0:T(8,128)(2,1)S(1)} %get-tuple-element.25), channel_id=1, source_target_pairs={{0,6},{1,7},{2,4},{3,5},{4,2},{5,3},{6,0},{7,1},{8,14},{9,15},{10,... | collective-permute-start | bytes 313352 | tf_op jit(solution)/shard_map/ppermute | solution.py:165
  7.2 21.3 %collective-permute-start.10 = (bf16[192,768]{1,0:T(8,128)(2,1)}, bf16[192,768]{1,0:T(8,128)(2,1)S(1)}, u32[]{:S(2)}, u32[]{:S(2)}) collective-permute-start(bf16[192,768]{1,0:T(8,128)(2,1)} %bitcast.7), channel_id=1, source_target_pairs={{0,16},{8,24},{16,0},{24,8},{1,17},{9,25},{17,1},{25,9},{2,18},{10... | collective-permute-start | bytes 884744 | tf_op jit(solution)/shard_map/ppermute | solution.py:165
  8.7 5.0 %collective-permute-start.1 = (bf16[24,2176]{1,0:T(8,128)(2,1)S(1)}, bf16[24,2176]{1,0:T(8,128)(2,1)S(1)}, u32[]{:S(2)}, u32[]{:S(2)}) collective-permute-start(bf16[24,2176]{1,0:T(8,128)(2,1)S(1)} %get-tuple-element.26), channel_id=1, source_target_pairs={{0,1},{1,0},{2,3},{3,2},{4,5},{5,4},{6,7},{7,6},{8,9},{9,8},{10,11... | collective-permute-start | bytes 313352 | tf_op jit(solution)/shard_map/ppermute | solution.py:165
  10.2 7.0 %collective-permute-start.2 = (bf16[24,2176]{1,0:T(8,128)(2,1)S(1)}, bf16[24,2176]{1,0:T(8,128)(2,1)S(1)}, u32[]{:S(2)}, u32[]{:S(2)}) collective-permute-start(bf16[24,2176]{1,0:T(8,128)(2,1)S(1)} %get-tuple-element.27), channel_id=1, source_target_pairs={{0,2},{1,3},{2,0},{3,1},{4,6},{5,7},{6,4},{7,5},{8,10},{9,11},{10,... | collective-permute-start | bytes 313352 | tf_op jit(solution)/shard_map/ppermute | solution.py:165
  10.2 9.0 %collective-permute-start.3 = (bf16[24,2176]{1,0:T(8,128)(2,1)S(1)}, bf16[24,2176]{1,0:T(8,128)(2,1)S(1)}, u32[]{:S(2)}, u32[]{:S(2)}) collective-permute-start(bf16[24,2176]{1,0:T(8,128)(2,1)S(1)} %get-tuple-element.28), channel_id=1, source_target_pairs={{0,7},{1,6},{2,5},{3,4},{4,3},{5,2},{6,1},{7,0},{8,15},{9,14},{10,... | collective-permute-start | bytes 313352 | tf_op jit(solution)/shard_map/ppermute | solution.py:165
  11.1 14.1 %collective-permute-start.4 = (bf16[24,2176]{1,0:T(8,128)(2,1)S(1)}, bf16[24,2176]{1,0:T(8,128)(2,1)S(1)}, u32[]{:S(2)}, u32[]{:S(2)}) collective-permute-start(bf16[24,2176]{1,0:T(8,128)(2,1)S(1)} %get-tuple-element.29), channel_id=1, source_target_pairs={{0,4},{1,5},{2,6},{3,7},{4,0},{5,1},{6,2},{7,3},{8,12},{9,13},{10,... | collective-permute-start | bytes 313352 | tf_op jit(solution)/shard_map/ppermute | solution.py:165
  13.7 13.6 %collective-permute-start.5 = (bf16[24,2176]{1,0:T(8,128)(2,1)S(1)}, bf16[24,2176]{1,0:T(8,128)(2,1)S(1)}, u32[]{:S(2)}, u32[]{:S(2)}) collective-permute-start(bf16[24,2176]{1,0:T(8,128)(2,1)S(1)} %get-tuple-element.30), channel_id=1, source_target_pairs={{0,5},{1,4},{2,7},{3,6},{4,1},{5,0},{6,3},{7,2},{8,13},{9,12},{10,... | collective-permute-start | bytes 313352 | tf_op jit(solution)/shard_map/ppermute | solution.py:165
  17.3 2.0 %copy-start = (bf16[1,1,192,768]{3,2,1,0:T(8,128)(2,1)S(1)}, bf16[1,1,192,768]{3,2,1,0:T(8,128)(2,1)}, u32[]{:S(2)}) copy-start(bf16[1,1,192,768]{3,2,1,0:T(8,128)(2,1)} %param.8) | copy-start | bytes 884740
  17.3 10.1 %collective-permute-start.6 = (bf16[24,2176]{1,0:T(8,128)(2,1)S(1)}, bf16[24,2176]{1,0:T(8,128)(2,1)S(1)}, u32[]{:S(2)}, u32[]{:S(2)}) collective-permute-start(bf16[24,2176]{1,0:T(8,128)(2,1)S(1)} %get-tuple-element.31), channel_id=1, source_target_pairs={{0,3},{1,2},{2,1},{3,0},{4,7},{5,6},{6,5},{7,4},{8,11},{9,10},{10,... | collective-permute-start | bytes 313352 | tf_op jit(solution)/shard_map/ppermute | solution.py:165
  19.2 16.1 %collective-permute-start.11 = (bf16[192,768]{1,0:T(8,128)(2,1)S(1)}, bf16[192,768]{1,0:T(8,128)(2,1)S(1)}, u32[]{:S(2)}, u32[]{:S(2)}) collective-permute-start(bf16[192,768]{1,0:T(8,128)(2,1)S(1)} %bitcast.8), channel_id=1, source_target_pairs={{0,24},{8,16},{16,8},{24,0},{1,25},{9,17},{17,9},{25,1},{2,26},{10... | collective-permute-start | bytes 884744 | tf_op jit(solution)/shard_map/ppermute | solution.py:165
  25.2 10.2 %collective-permute-start.12 = (bf16[192,768]{1,0:T(8,128)(2,1)S(1)}, bf16[192,768]{1,0:T(8,128)(2,1)S(1)}, u32[]{:S(2)}, u32[]{:S(2)}) collective-permute-start(bf16[192,768]{1,0:T(8,128)(2,1)S(1)} %bitcast.9), channel_id=1, source_target_pairs={{0,8},{8,0},{16,24},{24,16},{1,9},{9,1},{17,25},{25,17},{2,10},{10... | collective-permute-start | bytes 884744 | tf_op jit(solution)/shard_map/ppermute | solution.py:165
  27.8 7.9 %collective-permute-start.7 = (bf16[192,512]{1,0:T(8,128)(2,1)S(1)}, bf16[192,512]{1,0:T(8,128)(2,1)S(1)}, u32[]{:S(2)}, u32[]{:S(2)}) collective-permute-start(bf16[192,512]{1,0:T(8,128)(2,1)S(1)} %get-tuple-element.40), channel_id=1, source_target_pairs={{0,16},{8,24},{16,0},{24,8},{1,17},{9,25},{17,1},{25,9},{2,18},{10... | collective-permute-start | bytes 589832 | tf_op jit(solution)/shard_map/ppermute | solution.py:165
  28.4 8.1 %collective-permute-start.8 = (bf16[192,512]{1,0:T(8,128)(2,1)S(1)}, bf16[192,512]{1,0:T(8,128)(2,1)S(1)}, u32[]{:S(2)}, u32[]{:S(2)}) collective-permute-start(bf16[192,512]{1,0:T(8,128)(2,1)S(1)} %get-tuple-element.41), channel_id=1, source_target_pairs={{0,24},{8,16},{16,8},{24,0},{1,25},{9,17},{17,9},{25,1},{2,26},{10... | collective-permute-start | bytes 589832 | tf_op jit(solution)/shard_map/ppermute | solution.py:165
  28.6 8.0 %collective-permute-start.9 = (bf16[192,512]{1,0:T(8,128)(2,1)S(1)}, bf16[192,512]{1,0:T(8,128)(2,1)S(1)}, u32[]{:S(2)}, u32[]{:S(2)}) collective-permute-start(bf16[192,512]{1,0:T(8,128)(2,1)S(1)} %get-tuple-element.42), channel_id=1, source_target_pairs={{0,8},{8,0},{16,24},{24,16},{1,9},{9,1},{17,25},{25,17},{2,10},{10... | collective-permute-start | bytes 589832 | tf_op jit(solution)/shard_map/ppermute | solution.py:165
  30.0 12.0 %copy-start.1 = (s32[128,1]{0,1:T(1,128)S(1)}, s32[128,1]{0,1:T(1,128)}, u32[]{:S(2)}) copy-start(s32[128,1]{0,1:T(1,128)} %param.7) | copy-start | bytes 1540
  32.0 10.0 %all-to-all-start = ((f32[8,8,128]{2,1,0:T(8,128)}), f32[8,8,128]{2,1,0:T(8,128)S(1)}, u32[]{:S(2)}, u32[]{:S(2)}) async-start(f32[8,8,128]{2,1,0:T(8,128)} %get-tuple-element.39), calls=%async_computation | async-start | bytes 65536 | tf_op jit(solution)/shard_map/all_to_all | solution.py:168

commit v7 on v6

--- a/solution.py
+++ b/solution.py
@@ -10,7 +10,7 @@
 LANES = 128
 F32 = jnp.float32
 BF16 = jnp.bfloat16
-ORDER = (6, 1, 2, 7, 4, 5, 3, 0)
+ORDER = (6, 1, 2, 7, 5, 4, 3, 0)
 
 
 def kernel_call(body, outs, operands, name, flops=0, scratch=(), stay=()):

time: 42.8 us -> 41.9 us (0.979)
  waiting for transfers between devices: 15 us -> 14.1 us
    all_to_all x1, waiting for transfers between devices: 3.48 us -> 2.17 us  [exchange(): lax.all_to_all(array, 'expert', split_axis=0, concat_axis=0, tiled=True)]
    ppermute x13, waiting for transfers between devices: 11.5 us -> 11.9 us  [swap(): return lax.ppermute(array, axis, [(r, r ^ k) for r in range(size)])]
where the time goes in v7:
time: 41.9 us; the launch traced here: 41.7 us
  starting transfers between devices  18.5 us (44%)
  waiting for transfers between devices  14.1 us (34%)
  Pallas kernels  8.42 us (20%)
  between operations  0.72 us (2%)
    ppermute x13, starting transfers between devices, swap(): return lax.ppermute(array, axis, [(r, r ^ k) for r in range(size)])  15.1 us
    ppermute x13, waiting for transfers between devices, swap(): return lax.ppermute(array, axis, [(r, r ^ k) for r in range(size)])  11.9 us
    pallas_call x6, Pallas kernels, kernel_call(): pl.pallas_call(body, out_shape=outs, in_specs=[hbm if i in stay else vmem...  8.42 us
    all_to_all x1, starting transfers between devices, exchange(): lax.all_to_all(array, 'expert', split_axis=0, concat_axis=0, tiled=True)  3.33 us
    all_to_all x1, waiting for transfers between devices, exchange(): lax.all_to_all(array, 'expert', split_axis=0, concat_axis=0, tiled=True)  2.17 us
  transfers between devices with their start and end apart: 14, of which 6 were waited for; matrix products, arithmetic and copies ran while one was open for 0% of the time, Pallas kernels for 15%

profile of v7, /device:TPU:0, one launch (start us, length us, event | category | flops | bytes accessed | tf_op | source)
XLA Modules:
  0.0 41.7 jit_solution(1731806598795975874)
XLA Ops:
  0.6 1.5 %place.1 = (bf16[24,2176]{1,0:T(8,128)(2,1)S(1)}, bf16[24,2176]{1,0:T(8,128)(2,1)S(1)}, bf16[24,2176]{1,0:T(8,128)(2,1)S(1)}, bf16[24,2176]{1,0:T(8,128)(2,1)S(1...) custom-call(s32[1,128]{1,0:T(1,128)} %bitcast.12, ...), custom_call_target="tpu_custom_call" | custom-call | flops 100663296 | bytes 1361152 | tf_op jit(solution)/shard_map/place/pallas_call | solution.py:23
  2.1 5.1 %collective-permute-start = (bf16[24,2176]{1,0:T(8,128)(2,1)S(1)}, bf16[24,2176]{1,0:T(8,128)(2,1)S(1)}, u32[]{:S(2)}, u32[]{:S(2)}) collective-permute-start(bf16[24,2176]{1,0:T(8,128)(2,1)S(1)} %get-tuple-element.25), channel_id=1, source_target_pairs={{0,6},{1,7},{2,4},{3,5},{4,2},{5,3},{6,0},{7,1},{8,14},{9,15},{10,... | collective-permute-start | bytes 313352 | tf_op jit(solution)/shard_map/ppermute | solution.py:165
  7.2 1.5 %collective-permute-start.10 = (bf16[192,768]{1,0:T(8,128)(2,1)}, bf16[192,768]{1,0:T(8,128)(2,1)S(1)}, u32[]{:S(2)}, u32[]{:S(2)}) collective-permute-start(bf16[192,768]{1,0:T(8,128)(2,1)} %bitcast.7), channel_id=1, source_target_pairs={{0,16},{8,24},{16,0},{24,8},{1,17},{9,25},{17,1},{25,9},{2,18},{10... | collective-permute-start | bytes 884744 | tf_op jit(solution)/shard_map/ppermute | solution.py:165
  8.7 1.5 %collective-permute-start.1 = (bf16[24,2176]{1,0:T(8,128)(2,1)S(1)}, bf16[24,2176]{1,0:T(8,128)(2,1)S(1)}, u32[]{:S(2)}, u32[]{:S(2)}) collective-permute-start(bf16[24,2176]{1,0:T(8,128)(2,1)S(1)} %get-tuple-element.26), channel_id=1, source_target_pairs={{0,1},{1,0},{2,3},{3,2},{4,5},{5,4},{6,7},{7,6},{8,9},{9,8},{10,11... | collective-permute-start | bytes 313352 | tf_op jit(solution)/shard_map/ppermute | solution.py:165
  10.2 0.0 collective-permute-start.2
  10.2 0.9 %collective-permute-start.3 = (bf16[24,2176]{1,0:T(8,128)(2,1)S(1)}, bf16[24,2176]{1,0:T(8,128)(2,1)S(1)}, u32[]{:S(2)}, u32[]{:S(2)}) collective-permute-start(bf16[24,2176]{1,0:T(8,128)(2,1)S(1)} %get-tuple-element.28), channel_id=1, source_target_pairs={{0,7},{1,6},{2,5},{3,4},{4,3},{5,2},{6,1},{7,0},{8,15},{9,14},{10,... | collective-permute-start | bytes 313352 | tf_op jit(solution)/shard_map/ppermute | solution.py:165
  11.1 0.0 collective-permute-done.refs_0_
  11.1 3.5 %collective-permute-start.4 = (bf16[24,2176]{1,0:T(8,128)(2,1)S(1)}, bf16[24,2176]{1,0:T(8,128)(2,1)S(1)}, u32[]{:S(2)}, u32[]{:S(2)}) collective-permute-start(bf16[24,2176]{1,0:T(8,128)(2,1)S(1)} %get-tuple-element.29), channel_id=1, source_target_pairs={{0,5},{1,4},{2,7},{3,6},{4,1},{5,0},{6,3},{7,2},{8,13},{9,12},{10,... | collective-permute-start | bytes 313352 | tf_op jit(solution)/shard_map/ppermute | solution.py:165
  14.6 0.0 collective-permute-done.1.refs_1_
  14.6 0.3 collective-permute-start.5
  15.0 2.1 %collective-permute-done.2.refs_2_ = bf16[24,2176]{1,0:T(8,128)(2,1)S(1)} collective-permute-done((bf16[24,2176]{1,0:T(8,128)(2,1)S(1)}, bf16[24,2176]{1,0:T(8,128)(2,1)S(1)}, u32[]{:S(2)}, u32[]{:S(2)}) %collective-permute-start.2) | collective-permute-done | bytes 104480 | tf_op jit(solution)/shard_map/ppermute | solution.py:165
  17.1 0.0 collective-permute-start.6
  17.1 1.9 %fetch.1.weight_ref = bf16[768,2048]{1,0:T(8,128)(2,1)S(1)} custom-call(bf16[768,2048]{1,0:T(8,128)(2,1)} %bitcast.14), custom_call_target="tpu_custom_call" | custom-call | flops 603979776 | bytes 6291456 | tf_op jit(solution)/shard_map/fetch/pallas_call | solution.py:23
  19.1 0.0 collective-permute-done.3.refs_3_
  19.1 0.1 collective-permute-start.11
  19.2 6.7 %collective-permute-done.4.refs_4_ = bf16[24,2176]{1,0:T(8,128)(2,1)S(1)} collective-permute-done((bf16[24,2176]{1,0:T(8,128)(2,1)S(1)}, bf16[24,2176]{1,0:T(8,128)(2,1)S(1)}, u32[]{:S(2)}, u32[]{:S(2)}) %collective-permute-start.4) | collective-permute-done | bytes 104480 | tf_op jit(solution)/shard_map/ppermute | solution.py:165
  25.9 0.0 collective-permute-start.12
  25.9 0.5 %collective-permute-done.5.refs_5_ = bf16[24,2176]{1,0:T(8,128)(2,1)S(1)} collective-permute-done((bf16[24,2176]{1,0:T(8,128)(2,1)S(1)}, bf16[24,2176]{1,0:T(8,128)(2,1)S(1)}, u32[]{:S(2)}, u32[]{:S(2)}) %collective-permute-start.5) | collective-permute-done | bytes 104480 | tf_op jit(solution)/shard_map/ppermute | solution.py:165
  26.4 0.0 collective-permute-done.6.refs_6_
  26.4 0.5 %weigh.1 = (bf16[192,2048]{1,0:T(8,128)(2,1)S(1)}, f32[192,128]{1,0:T(8,128)S(1)}, bf16[192,512]{1,0:T(8,128)(2,1)S(1)}, bf16[192,512]{1,0:T(8,128)(2,1)S(1)}, b...) custom-call(bf16[24,2176]{1,0:T(8,128)(2,1)S(1)} %collective-permute-done.refs_0_, ...), custom_call_target="tpu_custom_call" | custom-call | flops 786432 | bytes 2506752 | tf_op jit(solution)/shard_map/weigh/pallas_call | solution.py:23
  26.9 0.6 %collective-permute-start.7 = (bf16[192,512]{1,0:T(8,128)(2,1)S(1)}, bf16[192,512]{1,0:T(8,128)(2,1)S(1)}, u32[]{:S(2)}, u32[]{:S(2)}) collective-permute-start(bf16[192,512]{1,0:T(8,128)(2,1)S(1)} %get-tuple-element.40), channel_id=1, source_target_pairs={{0,16},{8,24},{16,0},{24,8},{1,17},{9,25},{17,1},{25,9},{2,18},{10... | collective-permute-start | bytes 589832 | tf_op jit(solution)/shard_map/ppermute | solution.py:165
  27.5 0.8 %collective-permute-start.8 = (bf16[192,512]{1,0:T(8,128)(2,1)S(1)}, bf16[192,512]{1,0:T(8,128)(2,1)S(1)}, u32[]{:S(2)}, u32[]{:S(2)}) collective-permute-start(bf16[192,512]{1,0:T(8,128)(2,1)S(1)} %get-tuple-element.41), channel_id=1, source_target_pairs={{0,24},{8,16},{16,8},{24,0},{1,25},{9,17},{17,9},{25,1},{2,26},{10... | collective-permute-start | bytes 589832 | tf_op jit(solution)/shard_map/ppermute | solution.py:165
  28.3 0.8 %collective-permute-start.9 = (bf16[192,512]{1,0:T(8,128)(2,1)S(1)}, bf16[192,512]{1,0:T(8,128)(2,1)S(1)}, u32[]{:S(2)}, u32[]{:S(2)}) collective-permute-start(bf16[192,512]{1,0:T(8,128)(2,1)S(1)} %get-tuple-element.42), channel_id=1, source_target_pairs={{0,8},{8,0},{16,24},{24,16},{1,9},{9,1},{17,25},{25,17},{2,10},{10... | collective-permute-start | bytes 589832 | tf_op jit(solution)/shard_map/ppermute | solution.py:165
  29.1 2.0 %act.1 = (bf16[192,768]{1,0:T(8,128)(2,1)}, f32[8,8,128]{2,1,0:T(8,128)}) custom-call(bf16[192,2048]{1,0:T(8,128)(2,1)S(1)} %get-tuple-element.33.rows_ref, f32[192,128]{1,0:T(8,128)S(1)} %get-tuple-element.34.prob_ref, bf16[768,2048]{1,0:T(8,128)(2,1)S(1)} %fetch.1.weight_ref, bf16[192,768]{1,0:T(8,128)(2,1)S(1)} %bitcast.10), custom_call_target="tpu_custom_call" | custom-call | flops 603979776 | bytes 4653056 | tf_op jit(solution)/shard_map/act/pallas_call | solution.py:23
  31.1 3.3 %all-to-all-start = ((f32[8,8,128]{2,1,0:T(8,128)}), f32[8,8,128]{2,1,0:T(8,128)S(1)}, u32[]{:S(2)}, u32[]{:S(2)}) async-start(f32[8,8,128]{2,1,0:T(8,128)} %get-tuple-element.39), calls=%async_computation | async-start | bytes 65536 | tf_op jit(solution)/shard_map/all_to_all | solution.py:168
  34.4 0.0 collective-permute-done.11.refs_5_
  34.4 0.0 collective-permute-done.12.refs_6_
  34.4 0.3 collective-permute-done.7.refs_0_
  34.7 2.2 %collective-permute-done.8.refs_1_ = bf16[192,512]{1,0:T(8,128)(2,1)S(1)} collective-permute-done((bf16[192,512]{1,0:T(8,128)(2,1)S(1)}, bf16[192,512]{1,0:T(8,128)(2,1)S(1)}, u32[]{:S(2)}, u32[]{:S(2)}) %collective-permute-start.8) | collective-permute-done | bytes 196640 | tf_op jit(solution)/shard_map/ppermute | solution.py:165
  37.0 2.0 %gradient.1 = f32[512,768]{1,0:T(8,128)} custom-call(bf16[192,512]{1,0:T(8,128)(2,1)S(1)} %collective-permute-done.7.refs_0_, bf16[192,512]{1,0:T(8,128)(2,1)S(1)} %collective-permute-done.8.refs_1_, bf16[192,512]{1,0:T(8,128)(2,1)S(1)} %collective-permute-done.9.refs_2_, bf16[192,512]{1,0:T(8,128)(2,1)S(1)} %get-tuple-element.43.refs_3_, ...), custom_call_target="tpu_custom_call" | custom-call | flops 603979776 | bytes 3538944 | tf_op jit(solution)/shard_map/gradient/pallas_call | solution.py:23
  38.9 2.2 %all-to-all-done.table_ref = f32[8,8,128]{2,1,0:T(8,128)S(1)} async-done(((f32[8,8,128]{2,1,0:T(8,128)}), f32[8,8,128]{2,1,0:T(8,128)S(1)}, u32[]{:S(2)}, u32[]{:S(2)}) %all-to-all-start) | async-done | bytes 32800 | tf_op jit(solution)/shard_map/all_to_all | solution.py:168
  41.1 0.6 %pick.1 = f32[1,128]{1,0:T(1,128)} custom-call(s32[1,128]{1,0:T(1,128)S(1)} %bitcast.13, s32[1,128]{1,0:T(1,128)S(1)} %get-tuple-element.35.within_ref, f32[8,8,128]{2,1,0:T(8,128)S(1)} %all-to-all-done.table_ref), custom_call_target="tpu_custom_call" | custom-call | bytes 34304 | tf_op jit(solution)/shard_map/pick/pallas_call | solution.py:23
  (6 shorter events, 0.0 us)
Async XLA Ops:
  2.1 9.0 %collective-permute-start = (bf16[24,2176]{1,0:T(8,128)(2,1)S(1)}, bf16[24,2176]{1,0:T(8,128)(2,1)S(1)}, u32[]{:S(2)}, u32[]{:S(2)}) collective-permute-start(bf16[24,2176]{1,0:T(8,128)(2,1)S(1)} %get-tuple-element.25), channel_id=1, source_target_pairs={{0,6},{1,7},{2,4},{3,5},{4,2},{5,3},{6,0},{7,1},{8,14},{9,15},{10,... | collective-permute-start | bytes 313352 | tf_op jit(solution)/shard_map/ppermute | solution.py:165
  7.2 21.1 %collective-permute-start.10 = (bf16[192,768]{1,0:T(8,128)(2,1)}, bf16[192,768]{1,0:T(8,128)(2,1)S(1)}, u32[]{:S(2)}, u32[]{:S(2)}) collective-permute-start(bf16[192,768]{1,0:T(8,128)(2,1)} %bitcast.7), channel_id=1, source_target_pairs={{0,16},{8,24},{16,0},{24,8},{1,17},{9,25},{17,1},{25,9},{2,18},{10... | collective-permute-start | bytes 884744 | tf_op jit(solution)/shard_map/ppermute | solution.py:165
  8.7 5.9 %collective-permute-start.1 = (bf16[24,2176]{1,0:T(8,128)(2,1)S(1)}, bf16[24,2176]{1,0:T(8,128)(2,1)S(1)}, u32[]{:S(2)}, u32[]{:S(2)}) collective-permute-start(bf16[24,2176]{1,0:T(8,128)(2,1)S(1)} %get-tuple-element.26), channel_id=1, source_target_pairs={{0,1},{1,0},{2,3},{3,2},{4,5},{5,4},{6,7},{7,6},{8,9},{9,8},{10,11... | collective-permute-start | bytes 313352 | tf_op jit(solution)/shard_map/ppermute | solution.py:165
  10.2 6.9 %collective-permute-start.2 = (bf16[24,2176]{1,0:T(8,128)(2,1)S(1)}, bf16[24,2176]{1,0:T(8,128)(2,1)S(1)}, u32[]{:S(2)}, u32[]{:S(2)}) collective-permute-start(bf16[24,2176]{1,0:T(8,128)(2,1)S(1)} %get-tuple-element.27), channel_id=1, source_target_pairs={{0,2},{1,3},{2,0},{3,1},{4,6},{5,7},{6,4},{7,5},{8,10},{9,11},{10,... | collective-permute-start | bytes 313352 | tf_op jit(solution)/shard_map/ppermute | solution.py:165
  10.2 8.8 %collective-permute-start.3 = (bf16[24,2176]{1,0:T(8,128)(2,1)S(1)}, bf16[24,2176]{1,0:T(8,128)(2,1)S(1)}, u32[]{:S(2)}, u32[]{:S(2)}) collective-permute-start(bf16[24,2176]{1,0:T(8,128)(2,1)S(1)} %get-tuple-element.28), channel_id=1, source_target_pairs={{0,7},{1,6},{2,5},{3,4},{4,3},{5,2},{6,1},{7,0},{8,15},{9,14},{10,... | collective-permute-start | bytes 313352 | tf_op jit(solution)/shard_map/ppermute | solution.py:165
  11.1 14.8 %collective-permute-start.4 = (bf16[24,2176]{1,0:T(8,128)(2,1)S(1)}, bf16[24,2176]{1,0:T(8,128)(2,1)S(1)}, u32[]{:S(2)}, u32[]{:S(2)}) collective-permute-start(bf16[24,2176]{1,0:T(8,128)(2,1)S(1)} %get-tuple-element.29), channel_id=1, source_target_pairs={{0,5},{1,4},{2,7},{3,6},{4,1},{5,0},{6,3},{7,2},{8,13},{9,12},{10,... | collective-permute-start | bytes 313352 | tf_op jit(solution)/shard_map/ppermute | solution.py:165
  14.6 11.8 %collective-permute-start.5 = (bf16[24,2176]{1,0:T(8,128)(2,1)S(1)}, bf16[24,2176]{1,0:T(8,128)(2,1)S(1)}, u32[]{:S(2)}, u32[]{:S(2)}) collective-permute-start(bf16[24,2176]{1,0:T(8,128)(2,1)S(1)} %get-tuple-element.30), channel_id=1, source_target_pairs={{0,4},{1,5},{2,6},{3,7},{4,0},{5,1},{6,2},{7,3},{8,12},{9,13},{10,... | collective-permute-start | bytes 313352 | tf_op jit(solution)/shard_map/ppermute | solution.py:165
  17.1 2.0 %copy-start = (bf16[1,1,192,768]{3,2,1,0:T(8,128)(2,1)S(1)}, bf16[1,1,192,768]{3,2,1,0:T(8,128)(2,1)}, u32[]{:S(2)}) copy-start(bf16[1,1,192,768]{3,2,1,0:T(8,128)(2,1)} %param.8) | copy-start | bytes 884740
  17.1 9.3 %collective-permute-start.6 = (bf16[24,2176]{1,0:T(8,128)(2,1)S(1)}, bf16[24,2176]{1,0:T(8,128)(2,1)S(1)}, u32[]{:S(2)}, u32[]{:S(2)}) collective-permute-start(bf16[24,2176]{1,0:T(8,128)(2,1)S(1)} %get-tuple-element.31), channel_id=1, source_target_pairs={{0,3},{1,2},{2,1},{3,0},{4,7},{5,6},{6,5},{7,4},{8,11},{9,10},{10,... | collective-permute-start | bytes 313352 | tf_op jit(solution)/shard_map/ppermute | solution.py:165
  19.1 15.3 %collective-permute-start.11 = (bf16[192,768]{1,0:T(8,128)(2,1)S(1)}, bf16[192,768]{1,0:T(8,128)(2,1)S(1)}, u32[]{:S(2)}, u32[]{:S(2)}) collective-permute-start(bf16[192,768]{1,0:T(8,128)(2,1)S(1)} %bitcast.8), channel_id=1, source_target_pairs={{0,24},{8,16},{16,8},{24,0},{1,25},{9,17},{17,9},{25,1},{2,26},{10... | collective-permute-start | bytes 884744 | tf_op jit(solution)/shard_map/ppermute | solution.py:165
  25.9 8.6 %collective-permute-start.12 = (bf16[192,768]{1,0:T(8,128)(2,1)S(1)}, bf16[192,768]{1,0:T(8,128)(2,1)S(1)}, u32[]{:S(2)}, u32[]{:S(2)}) collective-permute-start(bf16[192,768]{1,0:T(8,128)(2,1)S(1)} %bitcast.9), channel_id=1, source_target_pairs={{0,8},{8,0},{16,24},{24,16},{1,9},{9,1},{17,25},{25,17},{2,10},{10... | collective-permute-start | bytes 884744 | tf_op jit(solution)/shard_map/ppermute | solution.py:165
  26.9 7.8 %collective-permute-start.7 = (bf16[192,512]{1,0:T(8,128)(2,1)S(1)}, bf16[192,512]{1,0:T(8,128)(2,1)S(1)}, u32[]{:S(2)}, u32[]{:S(2)}) collective-permute-start(bf16[192,512]{1,0:T(8,128)(2,1)S(1)} %get-tuple-element.40), channel_id=1, source_target_pairs={{0,16},{8,24},{16,0},{24,8},{1,17},{9,25},{17,1},{25,9},{2,18},{10... | collective-permute-start | bytes 589832 | tf_op jit(solution)/shard_map/ppermute | solution.py:165
  27.5 9.5 %collective-permute-start.8 = (bf16[192,512]{1,0:T(8,128)(2,1)S(1)}, bf16[192,512]{1,0:T(8,128)(2,1)S(1)}, u32[]{:S(2)}, u32[]{:S(2)}) collective-permute-start(bf16[192,512]{1,0:T(8,128)(2,1)S(1)} %get-tuple-element.41), channel_id=1, source_target_pairs={{0,24},{8,16},{16,8},{24,0},{1,25},{9,17},{17,9},{25,1},{2,26},{10... | collective-permute-start | bytes 589832 | tf_op jit(solution)/shard_map/ppermute | solution.py:165
  28.3 8.7 %collective-permute-start.9 = (bf16[192,512]{1,0:T(8,128)(2,1)S(1)}, bf16[192,512]{1,0:T(8,128)(2,1)S(1)}, u32[]{:S(2)}, u32[]{:S(2)}) collective-permute-start(bf16[192,512]{1,0:T(8,128)(2,1)S(1)} %get-tuple-element.42), channel_id=1, source_target_pairs={{0,8},{8,0},{16,24},{24,16},{1,9},{9,1},{17,25},{25,17},{2,10},{10... | collective-permute-start | bytes 589832 | tf_op jit(solution)/shard_map/ppermute | solution.py:165
  29.1 12.0 %copy-start.1 = (s32[128,1]{0,1:T(1,128)S(1)}, s32[128,1]{0,1:T(1,128)}, u32[]{:S(2)}) copy-start(s32[128,1]{0,1:T(1,128)} %param.7) | copy-start | bytes 1540
  31.1 10.0 %all-to-all-start = ((f32[8,8,128]{2,1,0:T(8,128)}), f32[8,8,128]{2,1,0:T(8,128)S(1)}, u32[]{:S(2)}, u32[]{:S(2)}) async-start(f32[8,8,128]{2,1,0:T(8,128)} %get-tuple-element.39), calls=%async_computation | async-start | bytes 65536 | tf_op jit(solution)/shard_map/all_to_all | solution.py:168

commit v8 on v7

--- a/solution.py
+++ b/solution.py
@@ -10,7 +10,7 @@
 LANES = 128
 F32 = jnp.float32
 BF16 = jnp.bfloat16
-ORDER = (6, 1, 2, 7, 5, 4, 3, 0)
+ORDER = (7, 1, 2, 6, 5, 4, 3, 0)
 
 
 def kernel_call(body, outs, operands, name, flops=0, scratch=(), stay=()):

time: 41.9 us -> 42.3 us (level)
  starting transfers between devices: 18.5 us -> 19.2 us
where the time goes in v8:
time: 42.3 us; the launch traced here: 42 us
  starting transfers between devices  19.2 us (45%)
  waiting for transfers between devices  13.7 us (32%)
  Pallas kernels  8.38 us (20%)
  between operations  0.71 us (2%)
    ppermute x13, starting transfers between devices, swap(): return lax.ppermute(array, axis, [(r, r ^ k) for r in range(size)])  15.5 us
    ppermute x13, waiting for transfers between devices, swap(): return lax.ppermute(array, axis, [(r, r ^ k) for r in range(size)])  11.7 us
    pallas_call x6, Pallas kernels, kernel_call(): pl.pallas_call(body, out_shape=outs, in_specs=[hbm if i in stay else vmem...  8.38 us
    all_to_all x1, starting transfers between devices, exchange(): lax.all_to_all(array, 'expert', split_axis=0, concat_axis=0, tiled=True)  3.66 us
    all_to_all x1, waiting for transfers between devices, exchange(): lax.all_to_all(array, 'expert', split_axis=0, concat_axis=0, tiled=True)  2.01 us
  transfers between devices with their start and end apart: 14, of which 6 were waited for; matrix products, arithmetic and copies ran while one was open for 0% of the time, Pallas kernels for 15%

profile of v8, /device:TPU:0, one launch (start us, length us, event | category | flops | bytes accessed | tf_op | source)
XLA Modules:
  0.0 42.0 jit_solution(1569391831079651110)
XLA Ops:
  0.6 1.5 %place.1 = (bf16[24,2176]{1,0:T(8,128)(2,1)S(1)}, bf16[24,2176]{1,0:T(8,128)(2,1)S(1)}, bf16[24,2176]{1,0:T(8,128)(2,1)S(1)}, bf16[24,2176]{1,0:T(8,128)(2,1)S(1...) custom-call(s32[1,128]{1,0:T(1,128)} %bitcast.12, ...), custom_call_target="tpu_custom_call" | custom-call | flops 100663296 | bytes 1361152 | tf_op jit(solution)/shard_map/place/pallas_call | solution.py:23
  2.1 6.0 %collective-permute-start = (bf16[24,2176]{1,0:T(8,128)(2,1)S(1)}, bf16[24,2176]{1,0:T(8,128)(2,1)S(1)}, u32[]{:S(2)}, u32[]{:S(2)}) collective-permute-start(bf16[24,2176]{1,0:T(8,128)(2,1)S(1)} %get-tuple-element.25), channel_id=1, source_target_pairs={{0,7},{1,6},{2,5},{3,4},{4,3},{5,2},{6,1},{7,0},{8,15},{9,14},{10,... | collective-permute-start | bytes 313352 | tf_op jit(solution)/shard_map/ppermute | solution.py:165
  8.2 1.5 %collective-permute-start.10 = (bf16[192,768]{1,0:T(8,128)(2,1)}, bf16[192,768]{1,0:T(8,128)(2,1)S(1)}, u32[]{:S(2)}, u32[]{:S(2)}) collective-permute-start(bf16[192,768]{1,0:T(8,128)(2,1)} %bitcast.7), channel_id=1, source_target_pairs={{0,16},{8,24},{16,0},{24,8},{1,17},{9,25},{17,1},{25,9},{2,18},{10... | collective-permute-start | bytes 884744 | tf_op jit(solution)/shard_map/ppermute | solution.py:165
  9.7 0.5 %collective-permute-start.1 = (bf16[24,2176]{1,0:T(8,128)(2,1)S(1)}, bf16[24,2176]{1,0:T(8,128)(2,1)S(1)}, u32[]{:S(2)}, u32[]{:S(2)}) collective-permute-start(bf16[24,2176]{1,0:T(8,128)(2,1)S(1)} %get-tuple-element.26), channel_id=1, source_target_pairs={{0,1},{1,0},{2,3},{3,2},{4,5},{5,4},{6,7},{7,6},{8,9},{9,8},{10,11... | collective-permute-start | bytes 313352 | tf_op jit(solution)/shard_map/ppermute | solution.py:165
  10.2 0.0 collective-permute-start.2
  10.2 0.9 %collective-permute-start.3 = (bf16[24,2176]{1,0:T(8,128)(2,1)S(1)}, bf16[24,2176]{1,0:T(8,128)(2,1)S(1)}, u32[]{:S(2)}, u32[]{:S(2)}) collective-permute-start(bf16[24,2176]{1,0:T(8,128)(2,1)S(1)} %get-tuple-element.28), channel_id=1, source_target_pairs={{0,6},{1,7},{2,4},{3,5},{4,2},{5,3},{6,0},{7,1},{8,14},{9,15},{10,... | collective-permute-start | bytes 313352 | tf_op jit(solution)/shard_map/ppermute | solution.py:165
  11.1 0.1 collective-permute-done.refs_0_
  11.2 3.5 %collective-permute-start.4 = (bf16[24,2176]{1,0:T(8,128)(2,1)S(1)}, bf16[24,2176]{1,0:T(8,128)(2,1)S(1)}, u32[]{:S(2)}, u32[]{:S(2)}) collective-permute-start(bf16[24,2176]{1,0:T(8,128)(2,1)S(1)} %get-tuple-element.29), channel_id=1, source_target_pairs={{0,5},{1,4},{2,7},{3,6},{4,1},{5,0},{6,3},{7,2},{8,13},{9,12},{10,... | collective-permute-start | bytes 313352 | tf_op jit(solution)/shard_map/ppermute | solution.py:165
  14.6 0.0 collective-permute-done.1.refs_1_
  14.7 0.7 %collective-permute-start.5 = (bf16[24,2176]{1,0:T(8,128)(2,1)S(1)}, bf16[24,2176]{1,0:T(8,128)(2,1)S(1)}, u32[]{:S(2)}, u32[]{:S(2)}) collective-permute-start(bf16[24,2176]{1,0:T(8,128)(2,1)S(1)} %get-tuple-element.30), channel_id=1, source_target_pairs={{0,4},{1,5},{2,6},{3,7},{4,0},{5,1},{6,2},{7,3},{8,12},{9,13},{10,... | collective-permute-start | bytes 313352 | tf_op jit(solution)/shard_map/ppermute | solution.py:165
  15.3 1.9 %collective-permute-done.2.refs_2_ = bf16[24,2176]{1,0:T(8,128)(2,1)S(1)} collective-permute-done((bf16[24,2176]{1,0:T(8,128)(2,1)S(1)}, bf16[24,2176]{1,0:T(8,128)(2,1)S(1)}, u32[]{:S(2)}, u32[]{:S(2)}) %collective-permute-start.2) | collective-permute-done | bytes 104480 | tf_op jit(solution)/shard_map/ppermute | solution.py:165
  17.2 0.1 collective-permute-start.6
  17.3 1.9 %fetch.1.weight_ref = bf16[768,2048]{1,0:T(8,128)(2,1)S(1)} custom-call(bf16[768,2048]{1,0:T(8,128)(2,1)} %bitcast.14), custom_call_target="tpu_custom_call" | custom-call | flops 603979776 | bytes 6291456 | tf_op jit(solution)/shard_map/fetch/pallas_call | solution.py:23
  19.2 0.0 collective-permute-done.3.refs_3_
  19.2 0.1 collective-permute-start.11
  19.3 6.8 %collective-permute-done.4.refs_4_ = bf16[24,2176]{1,0:T(8,128)(2,1)S(1)} collective-permute-done((bf16[24,2176]{1,0:T(8,128)(2,1)S(1)}, bf16[24,2176]{1,0:T(8,128)(2,1)S(1)}, u32[]{:S(2)}, u32[]{:S(2)}) %collective-permute-start.4) | collective-permute-done | bytes 104480 | tf_op jit(solution)/shard_map/ppermute | solution.py:165
  26.1 0.0 collective-permute-start.12
  26.1 0.3 collective-permute-done.5.refs_5_
  26.4 0.0 collective-permute-done.6.refs_6_
  26.4 0.5 %weigh.1 = (bf16[192,2048]{1,0:T(8,128)(2,1)S(1)}, f32[192,128]{1,0:T(8,128)S(1)}, bf16[192,512]{1,0:T(8,128)(2,1)S(1)}, bf16[192,512]{1,0:T(8,128)(2,1)S(1)}, b...) custom-call(bf16[24,2176]{1,0:T(8,128)(2,1)S(1)} %collective-permute-done.refs_0_, ...), custom_call_target="tpu_custom_call" | custom-call | flops 786432 | bytes 2506752 | tf_op jit(solution)/shard_map/weigh/pallas_call | solution.py:23
  26.9 1.1 %collective-permute-start.7 = (bf16[192,512]{1,0:T(8,128)(2,1)S(1)}, bf16[192,512]{1,0:T(8,128)(2,1)S(1)}, u32[]{:S(2)}, u32[]{:S(2)}) collective-permute-start(bf16[192,512]{1,0:T(8,128)(2,1)S(1)} %get-tuple-element.40), channel_id=1, source_target_pairs={{0,16},{8,24},{16,0},{24,8},{1,17},{9,25},{17,1},{25,9},{2,18},{10... | collective-permute-start | bytes 589832 | tf_op jit(solution)/shard_map/ppermute | solution.py:165
  28.0 0.6 %collective-permute-start.8 = (bf16[192,512]{1,0:T(8,128)(2,1)S(1)}, bf16[192,512]{1,0:T(8,128)(2,1)S(1)}, u32[]{:S(2)}, u32[]{:S(2)}) collective-permute-start(bf16[192,512]{1,0:T(8,128)(2,1)S(1)} %get-tuple-element.41), channel_id=1, source_target_pairs={{0,24},{8,16},{16,8},{24,0},{1,25},{9,17},{17,9},{25,1},{2,26},{10... | collective-permute-start | bytes 589832 | tf_op jit(solution)/shard_map/ppermute | solution.py:165
  28.5 0.0 collective-permute-done.10.refs_4_
  28.5 0.6 %collective-permute-start.9 = (bf16[192,512]{1,0:T(8,128)(2,1)S(1)}, bf16[192,512]{1,0:T(8,128)(2,1)S(1)}, u32[]{:S(2)}, u32[]{:S(2)}) collective-permute-start(bf16[192,512]{1,0:T(8,128)(2,1)S(1)} %get-tuple-element.42), channel_id=1, source_target_pairs={{0,8},{8,0},{16,24},{24,16},{1,9},{9,1},{17,25},{25,17},{2,10},{10... | collective-permute-start | bytes 589832 | tf_op jit(solution)/shard_map/ppermute | solution.py:165
  29.1 2.0 %act.1 = (bf16[192,768]{1,0:T(8,128)(2,1)}, f32[8,8,128]{2,1,0:T(8,128)}) custom-call(bf16[192,2048]{1,0:T(8,128)(2,1)S(1)} %get-tuple-element.33.rows_ref, f32[192,128]{1,0:T(8,128)S(1)} %get-tuple-element.34.prob_ref, bf16[768,2048]{1,0:T(8,128)(2,1)S(1)} %fetch.1.weight_ref, bf16[192,768]{1,0:T(8,128)(2,1)S(1)} %bitcast.10), custom_call_target="tpu_custom_call" | custom-call | flops 603979776 | bytes 4653056 | tf_op jit(solution)/shard_map/act/pallas_call | solution.py:23
  31.1 3.7 %all-to-all-start = ((f32[8,8,128]{2,1,0:T(8,128)}), f32[8,8,128]{2,1,0:T(8,128)S(1)}, u32[]{:S(2)}, u32[]{:S(2)}) async-start(f32[8,8,128]{2,1,0:T(8,128)} %get-tuple-element.39), calls=%async_computation | async-start | bytes 65536 | tf_op jit(solution)/shard_map/all_to_all | solution.py:168
  34.8 0.0 collective-permute-done.12.refs_6_
  34.8 2.7 %collective-permute-done.8.refs_1_ = bf16[192,512]{1,0:T(8,128)(2,1)S(1)} collective-permute-done((bf16[192,512]{1,0:T(8,128)(2,1)S(1)}, bf16[192,512]{1,0:T(8,128)(2,1)S(1)}, u32[]{:S(2)}, u32[]{:S(2)}) %collective-permute-start.8) | collective-permute-done | bytes 196640 | tf_op jit(solution)/shard_map/ppermute | solution.py:165
  37.5 0.0 collective-permute-done.9.refs_2_
  37.5 2.0 %gradient.1 = f32[512,768]{1,0:T(8,128)} custom-call(bf16[192,512]{1,0:T(8,128)(2,1)S(1)} %collective-permute-done.7.refs_0_, bf16[192,512]{1,0:T(8,128)(2,1)S(1)} %collective-permute-done.8.refs_1_, bf16[192,512]{1,0:T(8,128)(2,1)S(1)} %collective-permute-done.9.refs_2_, bf16[192,512]{1,0:T(8,128)(2,1)S(1)} %get-tuple-element.43.refs_3_, ...), custom_call_target="tpu_custom_call" | custom-call | flops 603979776 | bytes 3538944 | tf_op jit(solution)/shard_map/gradient/pallas_call | solution.py:23
  39.4 2.0 %all-to-all-done.table_ref = f32[8,8,128]{2,1,0:T(8,128)S(1)} async-done(((f32[8,8,128]{2,1,0:T(8,128)}), f32[8,8,128]{2,1,0:T(8,128)S(1)}, u32[]{:S(2)}, u32[]{:S(2)}) %all-to-all-start) | async-done | bytes 32800 | tf_op jit(solution)/shard_map/all_to_all | solution.py:168
  41.4 0.6 %pick.1 = f32[1,128]{1,0:T(1,128)} custom-call(s32[1,128]{1,0:T(1,128)S(1)} %bitcast.13, s32[1,128]{1,0:T(1,128)S(1)} %get-tuple-element.35.within_ref, f32[8,8,128]{2,1,0:T(8,128)S(1)} %all-to-all-done.table_ref), custom_call_target="tpu_custom_call" | custom-call | bytes 34304 | tf_op jit(solution)/shard_map/pick/pallas_call | solution.py:23
  (6 shorter events, 0.0 us)
Async XLA Ops:
  2.1 9.1 %collective-permute-start = (bf16[24,2176]{1,0:T(8,128)(2,1)S(1)}, bf16[24,2176]{1,0:T(8,128)(2,1)S(1)}, u32[]{:S(2)}, u32[]{:S(2)}) collective-permute-start(bf16[24,2176]{1,0:T(8,128)(2,1)S(1)} %get-tuple-element.25), channel_id=1, source_target_pairs={{0,7},{1,6},{2,5},{3,4},{4,3},{5,2},{6,1},{7,0},{8,15},{9,14},{10,... | collective-permute-start | bytes 313352 | tf_op jit(solution)/shard_map/ppermute | solution.py:165
  8.2 20.4 %collective-permute-start.10 = (bf16[192,768]{1,0:T(8,128)(2,1)}, bf16[192,768]{1,0:T(8,128)(2,1)S(1)}, u32[]{:S(2)}, u32[]{:S(2)}) collective-permute-start(bf16[192,768]{1,0:T(8,128)(2,1)} %bitcast.7), channel_id=1, source_target_pairs={{0,16},{8,24},{16,0},{24,8},{1,17},{9,25},{17,1},{25,9},{2,18},{10... | collective-permute-start | bytes 884744 | tf_op jit(solution)/shard_map/ppermute | solution.py:165
  9.7 5.0 %collective-permute-start.1 = (bf16[24,2176]{1,0:T(8,128)(2,1)S(1)}, bf16[24,2176]{1,0:T(8,128)(2,1)S(1)}, u32[]{:S(2)}, u32[]{:S(2)}) collective-permute-start(bf16[24,2176]{1,0:T(8,128)(2,1)S(1)} %get-tuple-element.26), channel_id=1, source_target_pairs={{0,1},{1,0},{2,3},{3,2},{4,5},{5,4},{6,7},{7,6},{8,9},{9,8},{10,11... | collective-permute-start | bytes 313352 | tf_op jit(solution)/shard_map/ppermute | solution.py:165
  10.2 7.0 %collective-permute-start.2 = (bf16[24,2176]{1,0:T(8,128)(2,1)S(1)}, bf16[24,2176]{1,0:T(8,128)(2,1)S(1)}, u32[]{:S(2)}, u32[]{:S(2)}) collective-permute-start(bf16[24,2176]{1,0:T(8,128)(2,1)S(1)} %get-tuple-element.27), channel_id=1, source_target_pairs={{0,2},{1,3},{2,0},{3,1},{4,6},{5,7},{6,4},{7,5},{8,10},{9,11},{10,... | collective-permute-start | bytes 313352 | tf_op jit(solution)/shard_map/ppermute | solution.py:165
  10.2 9.0 %collective-permute-start.3 = (bf16[24,2176]{1,0:T(8,128)(2,1)S(1)}, bf16[24,2176]{1,0:T(8,128)(2,1)S(1)}, u32[]{:S(2)}, u32[]{:S(2)}) collective-permute-start(bf16[24,2176]{1,0:T(8,128)(2,1)S(1)} %get-tuple-element.28), channel_id=1, source_target_pairs={{0,6},{1,7},{2,4},{3,5},{4,2},{5,3},{6,0},{7,1},{8,14},{9,15},{10,... | collective-permute-start | bytes 313352 | tf_op jit(solution)/shard_map/ppermute | solution.py:165
  11.2 14.9 %collective-permute-start.4 = (bf16[24,2176]{1,0:T(8,128)(2,1)S(1)}, bf16[24,2176]{1,0:T(8,128)(2,1)S(1)}, u32[]{:S(2)}, u32[]{:S(2)}) collective-permute-start(bf16[24,2176]{1,0:T(8,128)(2,1)S(1)} %get-tuple-element.29), channel_id=1, source_target_pairs={{0,5},{1,4},{2,7},{3,6},{4,1},{5,0},{6,3},{7,2},{8,13},{9,12},{10,... | collective-permute-start | bytes 313352 | tf_op jit(solution)/shard_map/ppermute | solution.py:165
  14.7 11.8 %collective-permute-start.5 = (bf16[24,2176]{1,0:T(8,128)(2,1)S(1)}, bf16[24,2176]{1,0:T(8,128)(2,1)S(1)}, u32[]{:S(2)}, u32[]{:S(2)}) collective-permute-start(bf16[24,2176]{1,0:T(8,128)(2,1)S(1)} %get-tuple-element.30), channel_id=1, source_target_pairs={{0,4},{1,5},{2,6},{3,7},{4,0},{5,1},{6,2},{7,3},{8,12},{9,13},{10,... | collective-permute-start | bytes 313352 | tf_op jit(solution)/shard_map/ppermute | solution.py:165
  17.2 2.0 %copy-start = (bf16[1,1,192,768]{3,2,1,0:T(8,128)(2,1)S(1)}, bf16[1,1,192,768]{3,2,1,0:T(8,128)(2,1)}, u32[]{:S(2)}) copy-start(bf16[1,1,192,768]{3,2,1,0:T(8,128)(2,1)} %param.8) | copy-start | bytes 884740
  17.2 9.2 %collective-permute-start.6 = (bf16[24,2176]{1,0:T(8,128)(2,1)S(1)}, bf16[24,2176]{1,0:T(8,128)(2,1)S(1)}, u32[]{:S(2)}, u32[]{:S(2)}) collective-permute-start(bf16[24,2176]{1,0:T(8,128)(2,1)S(1)} %get-tuple-element.31), channel_id=1, source_target_pairs={{0,3},{1,2},{2,1},{3,0},{4,7},{5,6},{6,5},{7,4},{8,11},{9,10},{10,... | collective-permute-start | bytes 313352 | tf_op jit(solution)/shard_map/ppermute | solution.py:165
  19.2 15.5 %collective-permute-start.11 = (bf16[192,768]{1,0:T(8,128)(2,1)S(1)}, bf16[192,768]{1,0:T(8,128)(2,1)S(1)}, u32[]{:S(2)}, u32[]{:S(2)}) collective-permute-start(bf16[192,768]{1,0:T(8,128)(2,1)S(1)} %bitcast.8), channel_id=1, source_target_pairs={{0,24},{8,16},{16,8},{24,0},{1,25},{9,17},{17,9},{25,1},{2,26},{10... | collective-permute-start | bytes 884744 | tf_op jit(solution)/shard_map/ppermute | solution.py:165
  26.1 8.6 %collective-permute-start.12 = (bf16[192,768]{1,0:T(8,128)(2,1)S(1)}, bf16[192,768]{1,0:T(8,128)(2,1)S(1)}, u32[]{:S(2)}, u32[]{:S(2)}) collective-permute-start(bf16[192,768]{1,0:T(8,128)(2,1)S(1)} %bitcast.9), channel_id=1, source_target_pairs={{0,8},{8,0},{16,24},{24,16},{1,9},{9,1},{17,25},{25,17},{2,10},{10... | collective-permute-start | bytes 884744 | tf_op jit(solution)/shard_map/ppermute | solution.py:165
  26.9 7.9 %collective-permute-start.7 = (bf16[192,512]{1,0:T(8,128)(2,1)S(1)}, bf16[192,512]{1,0:T(8,128)(2,1)S(1)}, u32[]{:S(2)}, u32[]{:S(2)}) collective-permute-start(bf16[192,512]{1,0:T(8,128)(2,1)S(1)} %get-tuple-element.40), channel_id=1, source_target_pairs={{0,16},{8,24},{16,0},{24,8},{1,17},{9,25},{17,1},{25,9},{2,18},{10... | collective-permute-start | bytes 589832 | tf_op jit(solution)/shard_map/ppermute | solution.py:165
  28.0 9.5 %collective-permute-start.8 = (bf16[192,512]{1,0:T(8,128)(2,1)S(1)}, bf16[192,512]{1,0:T(8,128)(2,1)S(1)}, u32[]{:S(2)}, u32[]{:S(2)}) collective-permute-start(bf16[192,512]{1,0:T(8,128)(2,1)S(1)} %get-tuple-element.41), channel_id=1, source_target_pairs={{0,24},{8,16},{16,8},{24,0},{1,25},{9,17},{17,9},{25,1},{2,26},{10... | collective-permute-start | bytes 589832 | tf_op jit(solution)/shard_map/ppermute | solution.py:165
  28.5 8.9 %collective-permute-start.9 = (bf16[192,512]{1,0:T(8,128)(2,1)S(1)}, bf16[192,512]{1,0:T(8,128)(2,1)S(1)}, u32[]{:S(2)}, u32[]{:S(2)}) collective-permute-start(bf16[192,512]{1,0:T(8,128)(2,1)S(1)} %get-tuple-element.42), channel_id=1, source_target_pairs={{0,8},{8,0},{16,24},{24,16},{1,9},{9,1},{17,25},{25,17},{2,10},{10... | collective-permute-start | bytes 589832 | tf_op jit(solution)/shard_map/ppermute | solution.py:165
  29.1 12.3 %copy-start.1 = (s32[128,1]{0,1:T(1,128)S(1)}, s32[128,1]{0,1:T(1,128)}, u32[]{:S(2)}) copy-start(s32[128,1]{0,1:T(1,128)} %param.7) | copy-start | bytes 1540
  31.1 10.3 %all-to-all-start = ((f32[8,8,128]{2,1,0:T(8,128)}), f32[8,8,128]{2,1,0:T(8,128)S(1)}, u32[]{:S(2)}, u32[]{:S(2)}) async-start(f32[8,8,128]{2,1,0:T(8,128)} %get-tuple-element.39), calls=%async_computation | async-start | bytes 65536 | tf_op jit(solution)/shard_map/all_to_all | solution.py:168

commit v9 on v8

--- a/solution.py
+++ b/solution.py
@@ -10,7 +10,7 @@
 LANES = 128
 F32 = jnp.float32
 BF16 = jnp.bfloat16
-ORDER = (7, 1, 2, 6, 5, 4, 3, 0)
+ORDER = (6, 2, 1, 7, 5, 4, 3, 0)
 
 
 def kernel_call(body, outs, operands, name, flops=0, scratch=(), stay=()):

time: 42.3 us -> 41.9 us (level)
  waiting for transfers between devices: 13.7 us -> 11.6 us
  starting transfers between devices: 19.2 us -> 20.9 us
    ppermute x13, waiting for transfers between devices: 11.7 us -> 9.48 us  [swap(): return lax.ppermute(array, axis, [(r, r ^ k) for r in range(size)])]
    ppermute x13, starting transfers between devices: 15.5 us -> 17.6 us  [swap(): return lax.ppermute(array, axis, [(r, r ^ k) for r in range(size)])]
  transfers between devices with their start and end apart: 14 -> 14, of which waited for: 6 -> 5; matrix products, arithmetic and copies ran while one was open for 0% -> 0% of each run, Pallas kernels for 15% -> 15%
where the time goes in v9:
time: 41.9 us; the launch traced here: 41.7 us
  starting transfers between devices  20.9 us (50%)
  waiting for transfers between devices  11.6 us (28%)
  Pallas kernels  8.38 us (20%)
  between operations  0.72 us (2%)
    ppermute x13, starting transfers between devices, swap(): return lax.ppermute(array, axis, [(r, r ^ k) for r in range(size)])  17.6 us
    ppermute x13, waiting for transfers between devices, swap(): return lax.ppermute(array, axis, [(r, r ^ k) for r in range(size)])  9.48 us
    pallas_call x6, Pallas kernels, kernel_call(): pl.pallas_call(body, out_shape=outs, in_specs=[hbm if i in stay else vmem...  8.38 us
    all_to_all x1, starting transfers between devices, exchange(): lax.all_to_all(array, 'expert', split_axis=0, concat_axis=0, tiled=True)  3.33 us
    all_to_all x1, waiting for transfers between devices, exchange(): lax.all_to_all(array, 'expert', split_axis=0, concat_axis=0, tiled=True)  2.14 us
  transfers between devices with their start and end apart: 14, of which 5 were waited for; matrix products, arithmetic and copies ran while one was open for 0% of the time, Pallas kernels for 15%

profile of v9, /device:TPU:0, one launch (start us, length us, event | category | flops | bytes accessed | tf_op | source)
XLA Modules:
  0.0 41.7 jit_solution(6920711290949653506)
XLA Ops:
  0.6 1.5 %place.1 = (bf16[24,2176]{1,0:T(8,128)(2,1)S(1)}, bf16[24,2176]{1,0:T(8,128)(2,1)S(1)}, bf16[24,2176]{1,0:T(8,128)(2,1)S(1)}, bf16[24,2176]{1,0:T(8,128)(2,1)S(1...) custom-call(s32[1,128]{1,0:T(1,128)} %bitcast.12, ...), custom_call_target="tpu_custom_call" | custom-call | flops 100663296 | bytes 1361152 | tf_op jit(solution)/shard_map/place/pallas_call | solution.py:23
  2.1 5.1 %collective-permute-start = (bf16[24,2176]{1,0:T(8,128)(2,1)S(1)}, bf16[24,2176]{1,0:T(8,128)(2,1)S(1)}, u32[]{:S(2)}, u32[]{:S(2)}) collective-permute-start(bf16[24,2176]{1,0:T(8,128)(2,1)S(1)} %get-tuple-element.25), channel_id=1, source_target_pairs={{0,6},{1,7},{2,4},{3,5},{4,2},{5,3},{6,0},{7,1},{8,14},{9,15},{10,... | collective-permute-start | bytes 313352 | tf_op jit(solution)/shard_map/ppermute | solution.py:165
  7.2 1.5 %collective-permute-start.10 = (bf16[192,768]{1,0:T(8,128)(2,1)}, bf16[192,768]{1,0:T(8,128)(2,1)S(1)}, u32[]{:S(2)}, u32[]{:S(2)}) collective-permute-start(bf16[192,768]{1,0:T(8,128)(2,1)} %bitcast.7), channel_id=1, source_target_pairs={{0,16},{8,24},{16,0},{24,8},{1,17},{9,25},{17,1},{25,9},{2,18},{10... | collective-permute-start | bytes 884744 | tf_op jit(solution)/shard_map/ppermute | solution.py:165
  8.7 0.0 collective-permute-start.1
  8.7 1.5 %collective-permute-start.2 = (bf16[24,2176]{1,0:T(8,128)(2,1)S(1)}, bf16[24,2176]{1,0:T(8,128)(2,1)S(1)}, u32[]{:S(2)}, u32[]{:S(2)}) collective-permute-start(bf16[24,2176]{1,0:T(8,128)(2,1)S(1)} %get-tuple-element.27), channel_id=1, source_target_pairs={{0,1},{1,0},{2,3},{3,2},{4,5},{5,4},{6,7},{7,6},{8,9},{9,8},{10,11... | collective-permute-start | bytes 313352 | tf_op jit(solution)/shard_map/ppermute | solution.py:165
  10.2 0.9 %collective-permute-start.3 = (bf16[24,2176]{1,0:T(8,128)(2,1)S(1)}, bf16[24,2176]{1,0:T(8,128)(2,1)S(1)}, u32[]{:S(2)}, u32[]{:S(2)}) collective-permute-start(bf16[24,2176]{1,0:T(8,128)(2,1)S(1)} %get-tuple-element.28), channel_id=1, source_target_pairs={{0,7},{1,6},{2,5},{3,4},{4,3},{5,2},{6,1},{7,0},{8,15},{9,14},{10,... | collective-permute-start | bytes 313352 | tf_op jit(solution)/shard_map/ppermute | solution.py:165
  11.1 0.0 collective-permute-done.refs_0_
  11.1 3.5 %collective-permute-start.4 = (bf16[24,2176]{1,0:T(8,128)(2,1)S(1)}, bf16[24,2176]{1,0:T(8,128)(2,1)S(1)}, u32[]{:S(2)}, u32[]{:S(2)}) collective-permute-start(bf16[24,2176]{1,0:T(8,128)(2,1)S(1)} %get-tuple-element.29), channel_id=1, source_target_pairs={{0,5},{1,4},{2,7},{3,6},{4,1},{5,0},{6,3},{7,2},{8,13},{9,12},{10,... | collective-permute-start | bytes 313352 | tf_op jit(solution)/shard_map/ppermute | solution.py:165
  14.6 0.0 collective-permute-done.1.refs_1_
  14.6 0.3 collective-permute-start.5
  15.0 0.0 collective-permute-done.2.refs_2_
  15.0 2.5 %collective-permute-start.6 = (bf16[24,2176]{1,0:T(8,128)(2,1)S(1)}, bf16[24,2176]{1,0:T(8,128)(2,1)S(1)}, u32[]{:S(2)}, u32[]{:S(2)}) collective-permute-start(bf16[24,2176]{1,0:T(8,128)(2,1)S(1)} %get-tuple-element.31), channel_id=1, source_target_pairs={{0,3},{1,2},{2,1},{3,0},{4,7},{5,6},{6,5},{7,4},{8,11},{9,10},{10,... | collective-permute-start | bytes 313352 | tf_op jit(solution)/shard_map/ppermute | solution.py:165
  17.5 1.9 %fetch.1.weight_ref = bf16[768,2048]{1,0:T(8,128)(2,1)S(1)} custom-call(bf16[768,2048]{1,0:T(8,128)(2,1)} %bitcast.14), custom_call_target="tpu_custom_call" | custom-call | flops 603979776 | bytes 6291456 | tf_op jit(solution)/shard_map/fetch/pallas_call | solution.py:23
  19.4 0.0 collective-permute-done.3.refs_3_
  19.4 0.1 collective-permute-start.11
  19.5 6.4 %collective-permute-done.4.refs_4_ = bf16[24,2176]{1,0:T(8,128)(2,1)S(1)} collective-permute-done((bf16[24,2176]{1,0:T(8,128)(2,1)S(1)}, bf16[24,2176]{1,0:T(8,128)(2,1)S(1)}, u32[]{:S(2)}, u32[]{:S(2)}) %collective-permute-start.4) | collective-permute-done | bytes 104480 | tf_op jit(solution)/shard_map/ppermute | solution.py:165
  25.9 0.0 collective-permute-start.12
  25.9 0.5 %collective-permute-done.5.refs_5_ = bf16[24,2176]{1,0:T(8,128)(2,1)S(1)} collective-permute-done((bf16[24,2176]{1,0:T(8,128)(2,1)S(1)}, bf16[24,2176]{1,0:T(8,128)(2,1)S(1)}, u32[]{:S(2)}, u32[]{:S(2)}) %collective-permute-start.5) | collective-permute-done | bytes 104480 | tf_op jit(solution)/shard_map/ppermute | solution.py:165
  26.4 0.5 %weigh.1 = (bf16[192,2048]{1,0:T(8,128)(2,1)S(1)}, f32[192,128]{1,0:T(8,128)S(1)}, bf16[192,512]{1,0:T(8,128)(2,1)S(1)}, bf16[192,512]{1,0:T(8,128)(2,1)S(1)}, b...) custom-call(bf16[24,2176]{1,0:T(8,128)(2,1)S(1)} %collective-permute-done.refs_0_, ...), custom_call_target="tpu_custom_call" | custom-call | flops 786432 | bytes 2506752 | tf_op jit(solution)/shard_map/weigh/pallas_call | solution.py:23
  26.9 0.6 %collective-permute-start.7 = (bf16[192,512]{1,0:T(8,128)(2,1)S(1)}, bf16[192,512]{1,0:T(8,128)(2,1)S(1)}, u32[]{:S(2)}, u32[]{:S(2)}) collective-permute-start(bf16[192,512]{1,0:T(8,128)(2,1)S(1)} %get-tuple-element.40), channel_id=1, source_target_pairs={{0,16},{8,24},{16,0},{24,8},{1,17},{9,25},{17,1},{25,9},{2,18},{10... | collective-permute-start | bytes 589832 | tf_op jit(solution)/shard_map/ppermute | solution.py:165
  27.5 0.8 %collective-permute-start.8 = (bf16[192,512]{1,0:T(8,128)(2,1)S(1)}, bf16[192,512]{1,0:T(8,128)(2,1)S(1)}, u32[]{:S(2)}, u32[]{:S(2)}) collective-permute-start(bf16[192,512]{1,0:T(8,128)(2,1)S(1)} %get-tuple-element.41), channel_id=1, source_target_pairs={{0,24},{8,16},{16,8},{24,0},{1,25},{9,17},{17,9},{25,1},{2,26},{10... | collective-permute-start | bytes 589832 | tf_op jit(solution)/shard_map/ppermute | solution.py:165
  28.3 0.0 collective-permute-done.10.refs_4_
  28.3 0.8 %collective-permute-start.9 = (bf16[192,512]{1,0:T(8,128)(2,1)S(1)}, bf16[192,512]{1,0:T(8,128)(2,1)S(1)}, u32[]{:S(2)}, u32[]{:S(2)}) collective-permute-start(bf16[192,512]{1,0:T(8,128)(2,1)S(1)} %get-tuple-element.42), channel_id=1, source_target_pairs={{0,8},{8,0},{16,24},{24,16},{1,9},{9,1},{17,25},{25,17},{2,10},{10... | collective-permute-start | bytes 589832 | tf_op jit(solution)/shard_map/ppermute | solution.py:165
  29.1 2.0 %act.1 = (bf16[192,768]{1,0:T(8,128)(2,1)}, f32[8,8,128]{2,1,0:T(8,128)}) custom-call(bf16[192,2048]{1,0:T(8,128)(2,1)S(1)} %get-tuple-element.33.rows_ref, f32[192,128]{1,0:T(8,128)S(1)} %get-tuple-element.34.prob_ref, bf16[768,2048]{1,0:T(8,128)(2,1)S(1)} %fetch.1.weight_ref, bf16[192,768]{1,0:T(8,128)(2,1)S(1)} %bitcast.10), custom_call_target="tpu_custom_call" | custom-call | flops 603979776 | bytes 4653056 | tf_op jit(solution)/shard_map/act/pallas_call | solution.py:23
  31.1 3.3 %all-to-all-start = ((f32[8,8,128]{2,1,0:T(8,128)}), f32[8,8,128]{2,1,0:T(8,128)S(1)}, u32[]{:S(2)}, u32[]{:S(2)}) async-start(f32[8,8,128]{2,1,0:T(8,128)} %get-tuple-element.39), calls=%async_computation | async-start | bytes 65536 | tf_op jit(solution)/shard_map/all_to_all | solution.py:168
  34.4 0.0 collective-permute-done.12.refs_6_
  34.4 0.3 collective-permute-done.7.refs_0_
  34.7 2.2 %collective-permute-done.8.refs_1_ = bf16[192,512]{1,0:T(8,128)(2,1)S(1)} collective-permute-done((bf16[192,512]{1,0:T(8,128)(2,1)S(1)}, bf16[192,512]{1,0:T(8,128)(2,1)S(1)}, u32[]{:S(2)}, u32[]{:S(2)}) %collective-permute-start.8) | collective-permute-done | bytes 196640 | tf_op jit(solution)/shard_map/ppermute | solution.py:165
  37.0 0.0 collective-permute-done.9.refs_2_
  37.0 2.0 %gradient.1 = f32[512,768]{1,0:T(8,128)} custom-call(bf16[192,512]{1,0:T(8,128)(2,1)S(1)} %collective-permute-done.7.refs_0_, bf16[192,512]{1,0:T(8,128)(2,1)S(1)} %collective-permute-done.8.refs_1_, bf16[192,512]{1,0:T(8,128)(2,1)S(1)} %collective-permute-done.9.refs_2_, bf16[192,512]{1,0:T(8,128)(2,1)S(1)} %get-tuple-element.43.refs_3_, ...), custom_call_target="tpu_custom_call" | custom-call | flops 603979776 | bytes 3538944 | tf_op jit(solution)/shard_map/gradient/pallas_call | solution.py:23
  38.9 2.1 %all-to-all-done.table_ref = f32[8,8,128]{2,1,0:T(8,128)S(1)} async-done(((f32[8,8,128]{2,1,0:T(8,128)}), f32[8,8,128]{2,1,0:T(8,128)S(1)}, u32[]{:S(2)}, u32[]{:S(2)}) %all-to-all-start) | async-done | bytes 32800 | tf_op jit(solution)/shard_map/all_to_all | solution.py:168
  41.1 0.6 %pick.1 = f32[1,128]{1,0:T(1,128)} custom-call(s32[1,128]{1,0:T(1,128)S(1)} %bitcast.13, s32[1,128]{1,0:T(1,128)S(1)} %get-tuple-element.35.within_ref, f32[8,8,128]{2,1,0:T(8,128)S(1)} %all-to-all-done.table_ref), custom_call_target="tpu_custom_call" | custom-call | bytes 34304 | tf_op jit(solution)/shard_map/pick/pallas_call | solution.py:23
  (6 shorter events, 0.0 us)
Async XLA Ops:
  2.1 9.0 %collective-permute-start = (bf16[24,2176]{1,0:T(8,128)(2,1)S(1)}, bf16[24,2176]{1,0:T(8,128)(2,1)S(1)}, u32[]{:S(2)}, u32[]{:S(2)}) collective-permute-start(bf16[24,2176]{1,0:T(8,128)(2,1)S(1)} %get-tuple-element.25), channel_id=1, source_target_pairs={{0,6},{1,7},{2,4},{3,5},{4,2},{5,3},{6,0},{7,1},{8,14},{9,15},{10,... | collective-permute-start | bytes 313352 | tf_op jit(solution)/shard_map/ppermute | solution.py:165
  7.2 21.1 %collective-permute-start.10 = (bf16[192,768]{1,0:T(8,128)(2,1)}, bf16[192,768]{1,0:T(8,128)(2,1)S(1)}, u32[]{:S(2)}, u32[]{:S(2)}) collective-permute-start(bf16[192,768]{1,0:T(8,128)(2,1)} %bitcast.7), channel_id=1, source_target_pairs={{0,16},{8,24},{16,0},{24,8},{1,17},{9,25},{17,1},{25,9},{2,18},{10... | collective-permute-start | bytes 884744 | tf_op jit(solution)/shard_map/ppermute | solution.py:165
  8.7 5.9 %collective-permute-start.1 = (bf16[24,2176]{1,0:T(8,128)(2,1)S(1)}, bf16[24,2176]{1,0:T(8,128)(2,1)S(1)}, u32[]{:S(2)}, u32[]{:S(2)}) collective-permute-start(bf16[24,2176]{1,0:T(8,128)(2,1)S(1)} %get-tuple-element.26), channel_id=1, source_target_pairs={{0,2},{1,3},{2,0},{3,1},{4,6},{5,7},{6,4},{7,5},{8,10},{9,11},{10,... | collective-permute-start | bytes 313352 | tf_op jit(solution)/shard_map/ppermute | solution.py:165
  8.7 6.2 %collective-permute-start.2 = (bf16[24,2176]{1,0:T(8,128)(2,1)S(1)}, bf16[24,2176]{1,0:T(8,128)(2,1)S(1)}, u32[]{:S(2)}, u32[]{:S(2)}) collective-permute-start(bf16[24,2176]{1,0:T(8,128)(2,1)S(1)} %get-tuple-element.27), channel_id=1, source_target_pairs={{0,1},{1,0},{2,3},{3,2},{4,5},{5,4},{6,7},{7,6},{8,9},{9,8},{10,11... | collective-permute-start | bytes 313352 | tf_op jit(solution)/shard_map/ppermute | solution.py:165
  10.2 9.1 %collective-permute-start.3 = (bf16[24,2176]{1,0:T(8,128)(2,1)S(1)}, bf16[24,2176]{1,0:T(8,128)(2,1)S(1)}, u32[]{:S(2)}, u32[]{:S(2)}) collective-permute-start(bf16[24,2176]{1,0:T(8,128)(2,1)S(1)} %get-tuple-element.28), channel_id=1, source_target_pairs={{0,7},{1,6},{2,5},{3,4},{4,3},{5,2},{6,1},{7,0},{8,15},{9,14},{10,... | collective-permute-start | bytes 313352 | tf_op jit(solution)/shard_map/ppermute | solution.py:165
  11.1 14.8 %collective-permute-start.4 = (bf16[24,2176]{1,0:T(8,128)(2,1)S(1)}, bf16[24,2176]{1,0:T(8,128)(2,1)S(1)}, u32[]{:S(2)}, u32[]{:S(2)}) collective-permute-start(bf16[24,2176]{1,0:T(8,128)(2,1)S(1)} %get-tuple-element.29), channel_id=1, source_target_pairs={{0,5},{1,4},{2,7},{3,6},{4,1},{5,0},{6,3},{7,2},{8,13},{9,12},{10,... | collective-permute-start | bytes 313352 | tf_op jit(solution)/shard_map/ppermute | solution.py:165
  14.6 11.8 %collective-permute-start.5 = (bf16[24,2176]{1,0:T(8,128)(2,1)S(1)}, bf16[24,2176]{1,0:T(8,128)(2,1)S(1)}, u32[]{:S(2)}, u32[]{:S(2)}) collective-permute-start(bf16[24,2176]{1,0:T(8,128)(2,1)S(1)} %get-tuple-element.30), channel_id=1, source_target_pairs={{0,4},{1,5},{2,6},{3,7},{4,0},{5,1},{6,2},{7,3},{8,12},{9,13},{10,... | collective-permute-start | bytes 313352 | tf_op jit(solution)/shard_map/ppermute | solution.py:165
  15.0 4.4 %copy-start = (bf16[1,1,192,768]{3,2,1,0:T(8,128)(2,1)S(1)}, bf16[1,1,192,768]{3,2,1,0:T(8,128)(2,1)}, u32[]{:S(2)}) copy-start(bf16[1,1,192,768]{3,2,1,0:T(8,128)(2,1)} %param.8) | copy-start | bytes 884740
  15.0 11.4 %collective-permute-start.6 = (bf16[24,2176]{1,0:T(8,128)(2,1)S(1)}, bf16[24,2176]{1,0:T(8,128)(2,1)S(1)}, u32[]{:S(2)}, u32[]{:S(2)}) collective-permute-start(bf16[24,2176]{1,0:T(8,128)(2,1)S(1)} %get-tuple-element.31), channel_id=1, source_target_pairs={{0,3},{1,2},{2,1},{3,0},{4,7},{5,6},{6,5},{7,4},{8,11},{9,10},{10,... | collective-permute-start | bytes 313352 | tf_op jit(solution)/shard_map/ppermute | solution.py:165
  19.4 15.0 %collective-permute-start.11 = (bf16[192,768]{1,0:T(8,128)(2,1)S(1)}, bf16[192,768]{1,0:T(8,128)(2,1)S(1)}, u32[]{:S(2)}, u32[]{:S(2)}) collective-permute-start(bf16[192,768]{1,0:T(8,128)(2,1)S(1)} %bitcast.8), channel_id=1, source_target_pairs={{0,24},{8,16},{16,8},{24,0},{1,25},{9,17},{17,9},{25,1},{2,26},{10... | collective-permute-start | bytes 884744 | tf_op jit(solution)/shard_map/ppermute | solution.py:165
  25.9 8.6 %collective-permute-start.12 = (bf16[192,768]{1,0:T(8,128)(2,1)S(1)}, bf16[192,768]{1,0:T(8,128)(2,1)S(1)}, u32[]{:S(2)}, u32[]{:S(2)}) collective-permute-start(bf16[192,768]{1,0:T(8,128)(2,1)S(1)} %bitcast.9), channel_id=1, source_target_pairs={{0,8},{8,0},{16,24},{24,16},{1,9},{9,1},{17,25},{25,17},{2,10},{10... | collective-permute-start | bytes 884744 | tf_op jit(solution)/shard_map/ppermute | solution.py:165
  26.9 7.8 %collective-permute-start.7 = (bf16[192,512]{1,0:T(8,128)(2,1)S(1)}, bf16[192,512]{1,0:T(8,128)(2,1)S(1)}, u32[]{:S(2)}, u32[]{:S(2)}) collective-permute-start(bf16[192,512]{1,0:T(8,128)(2,1)S(1)} %get-tuple-element.40), channel_id=1, source_target_pairs={{0,16},{8,24},{16,0},{24,8},{1,17},{9,25},{17,1},{25,9},{2,18},{10... | collective-permute-start | bytes 589832 | tf_op jit(solution)/shard_map/ppermute | solution.py:165
  27.5 9.5 %collective-permute-start.8 = (bf16[192,512]{1,0:T(8,128)(2,1)S(1)}, bf16[192,512]{1,0:T(8,128)(2,1)S(1)}, u32[]{:S(2)}, u32[]{:S(2)}) collective-permute-start(bf16[192,512]{1,0:T(8,128)(2,1)S(1)} %get-tuple-element.41), channel_id=1, source_target_pairs={{0,24},{8,16},{16,8},{24,0},{1,25},{9,17},{17,9},{25,1},{2,26},{10... | collective-permute-start | bytes 589832 | tf_op jit(solution)/shard_map/ppermute | solution.py:165
  28.3 8.7 %collective-permute-start.9 = (bf16[192,512]{1,0:T(8,128)(2,1)S(1)}, bf16[192,512]{1,0:T(8,128)(2,1)S(1)}, u32[]{:S(2)}, u32[]{:S(2)}) collective-permute-start(bf16[192,512]{1,0:T(8,128)(2,1)S(1)} %get-tuple-element.42), channel_id=1, source_target_pairs={{0,8},{8,0},{16,24},{24,16},{1,9},{9,1},{17,25},{25,17},{2,10},{10... | collective-permute-start | bytes 589832 | tf_op jit(solution)/shard_map/ppermute | solution.py:165
  29.1 12.0 %copy-start.1 = (s32[128,1]{0,1:T(1,128)S(1)}, s32[128,1]{0,1:T(1,128)}, u32[]{:S(2)}) copy-start(s32[128,1]{0,1:T(1,128)} %param.7) | copy-start | bytes 1540
  31.1 10.0 %all-to-all-start = ((f32[8,8,128]{2,1,0:T(8,128)}), f32[8,8,128]{2,1,0:T(8,128)S(1)}, u32[]{:S(2)}, u32[]{:S(2)}) async-start(f32[8,8,128]{2,1,0:T(8,128)} %get-tuple-element.39), calls=%async_computation | async-start | bytes 65536 | tf_op jit(solution)/shard_map/all_to_all | solution.py:168
